TPU v7x, 256 devices: a whole 4x4x8 slice. The times are simulated.
256 devices in a mesh: dp: 16 (over y, x), seq: 8 (over z), tensor: 2 (over core).
Axes of the slice: x: 4, y: 4, z: 8, core: 2. Of those that a mesh axis runs over, the one named last changes fastest.
Arguments:
- queries: bfloat16 [24576, 2048], P(('dp', 'seq'), 'tensor'), may hold values from -150 to 150
- keys: bfloat16 [24576, 2048], P(('dp', 'seq'), 'tensor'), may hold values from -6 to 6
- values: bfloat16 [24576, 2048], P(('dp', 'seq'), 'tensor'), may hold values from -6 to 6
- out_grad: bfloat16 [24576, 3072], P(('dp', 'seq'), 'tensor'), may hold values from -24 to 24
- gate: float32 [16, 3072], P('dp'), may hold values from -4 to 4
- proj_weight: bfloat16 [3072, 2048], P(('dp', 'seq'), 'tensor'), may hold values from -0.125 to 0.125
- lengths: int32 [16], P('dp'), may hold values from 128 to 1536, as said below
Outputs:
- query_grad: bfloat16 [24576, 2048], P(('dp', 'seq'), 'tensor')
- key_grad: bfloat16 [24576, 2048], P(('dp', 'seq'), 'tensor')
- value_grad: bfloat16 [24576, 2048], P(('dp', 'seq'), 'tensor')
- proj_grad: float32 [3072, 2048], P(('dp', 'seq'), 'tensor')
Inputs may be any that keep to these rules, and one draw needn't show every extreme that they name: `lengths`: each a multiple of 128; some sample has exactly 1536 tokens.
All inputs are finite; a program needn't handle non-finite values.
Results may differ from a plain program's by a relative error of at most 0.022.
Values may be sent and summed in bfloat16 or wider, within the bound.
No kernel may reach another device: no remote copies, remote signals or barrier semaphores. Data moves between devices by JAX's collectives and lax.ppermute only.
A program may use at most 64 MiB of HBM per device.

v0:
```python
import math

import jax
import jax.numpy as jnp
from jax import lax
from jax.sharding import PartitionSpec as P

HD = 128


def attend_head(query, key_rows, value_rows, grad_out, key_live):
    length_all = query.shape[0]
    block = math.gcd(512, length_all)
    factor = query.shape[1] ** (-0.5)

    def visit(carry, number):
        key_acc, value_acc = carry
        start = number * block
        query_block = lax.dynamic_slice_in_dim(query, start, block, 0)
        grad_block = lax.dynamic_slice_in_dim(grad_out, start, block, 0)
        scores = jnp.dot(query_block, key_rows.T, preferred_element_type=jnp.float32) * factor
        scores = jnp.where(key_live[None, :], scores, -jnp.inf)
        top = jnp.max(scores, axis=1, keepdims=True)
        weights = jnp.exp(scores - top)
        probs = weights / jnp.sum(weights, axis=1, keepdims=True)
        probs_low = probs.astype(jnp.bfloat16)
        output = jnp.dot(probs_low, value_rows, preferred_element_type=jnp.float32)
        delta = jnp.sum(grad_block.astype(jnp.float32) * output, axis=1, keepdims=True)
        prob_grad = jnp.dot(grad_block, value_rows.T, preferred_element_type=jnp.float32)
        score_grad = (probs * (prob_grad - delta)).astype(jnp.bfloat16)
        query_part = jnp.dot(score_grad, key_rows, preferred_element_type=jnp.float32) * factor
        key_acc = (
            key_acc
            + jnp.dot(score_grad.T, query_block, preferred_element_type=jnp.float32) * factor
        )
        value_acc = value_acc + jnp.dot(probs_low.T, grad_block, preferred_element_type=jnp.float32)
        return (
            (key_acc, value_acc),
            (output.astype(jnp.bfloat16), query_part.astype(jnp.bfloat16)),
        )

    zeros = jnp.zeros(query.shape, jnp.float32)
    (key_acc, value_acc), (outputs, query_parts) = lax.scan(
        visit, (zeros, zeros), jnp.arange(length_all // block, dtype=jnp.int32)
    )
    width = query.shape[1]
    return (
        outputs.reshape(length_all, width),
        query_parts.reshape(length_all, width),
        key_acc.astype(jnp.bfloat16),
        value_acc.astype(jnp.bfloat16),
    )


def per_device(queries, keys, values, out_grad, gate, proj_weight, lengths):
    token_rows = queries.shape[0]
    whole_grad = lax.all_gather(out_grad, "tensor", axis=1, tiled=True)
    position = lax.axis_index("seq") * token_rows + jnp.arange(token_rows, dtype=jnp.int32)
    live = position < lengths[0]
    scaled_grad = jnp.where(live[:, None], whole_grad.astype(jnp.float32) * gate, 0.0).astype(
        jnp.bfloat16
    )
    columns = scaled_grad
    attn_grad = jnp.dot(
        columns,
        lax.all_gather(proj_weight, ("dp", "seq"), axis=0, tiled=True),
        preferred_element_type=jnp.float32,
    ).astype(jnp.bfloat16)
    head_query, head_key, head_value, head_grad = (
        lax.all_to_all(queries, "seq", split_axis=1, concat_axis=0, tiled=True),
        lax.all_to_all(keys, "seq", split_axis=1, concat_axis=0, tiled=True),
        lax.all_to_all(values, "seq", split_axis=1, concat_axis=0, tiled=True),
        lax.all_to_all(attn_grad, "seq", split_axis=1, concat_axis=0, tiled=True),
    )
    length_all = head_query.shape[0]
    heads_here = head_query.shape[1] // HD
    key_live = jnp.arange(length_all, dtype=jnp.int32) < lengths[0]

    def split(array):
        return array.reshape(length_all, heads_here, HD).transpose(1, 0, 2)

    def head_grads(member):
        return attend_head(member[0], member[1], member[2], member[3], key_live)

    results = lax.map(
        head_grads, (split(head_query), split(head_key), split(head_value), split(head_grad))
    )

    def merge(array):
        return array.transpose(1, 0, 2).reshape(length_all, heads_here * HD)

    attn_out, query_grad, key_grad, value_grad = [merge(array) for array in results]
    token_out, query_back, key_back, value_back = (
        lax.all_to_all(attn_out, "seq", split_axis=0, concat_axis=1, tiled=True),
        lax.all_to_all(query_grad, "seq", split_axis=0, concat_axis=1, tiled=True),
        lax.all_to_all(key_grad, "seq", split_axis=0, concat_axis=1, tiled=True),
        lax.all_to_all(value_grad, "seq", split_axis=0, concat_axis=1, tiled=True),
    )
    columns = scaled_grad
    proj_grad = lax.psum_scatter(
        lax.dot_general(
            columns, token_out, (((0,), (0,)), ((), ())), preferred_element_type=jnp.float32
        ),
        ("dp", "seq"),
        scatter_dimension=0,
        tiled=True,
    )
    return (query_back, key_back, value_back, proj_grad)


def solution(mesh):
    return jax.shard_map(
        per_device,
        mesh=mesh,
        in_specs=(
            P(("dp", "seq"), "tensor"),
            P(("dp", "seq"), "tensor"),
            P(("dp", "seq"), "tensor"),
            P(("dp", "seq"), "tensor"),
            P("dp", None),
            P(("dp", "seq"), "tensor"),
            P("dp"),
        ),
        out_specs=(
            P(("dp", "seq"), "tensor"),
            P(("dp", "seq"), "tensor"),
            P(("dp", "seq"), "tensor"),
            P(("dp", "seq"), "tensor"),
        ),
        check_vma=False,
    )
```

profile of v0, /device:TPU:2, one launch (start us, length us, event | category | flops | bytes accessed | tf_op | source)
XLA Modules:
  0.0 1086.9 jit_solution(15669354248196226452)
XLA Ops:
  8.7 0.8 copy_bitcast_fusion.6
  9.5 8.5 all-to-all-start
  18.0 1.8 copy_bitcast_fusion.5
  19.8 12.9 %all-to-all-done = bf16[192,8,128]{2,0,1:T(8,128)(2,1)S(1)} async-done(((bf16[192,8,128]{2,0,1:T(8,128)(2,1)}), bf16[192,8,128]{2,0,1:T(8,128)(2,1)S(1)}, u32[]{:S(2)}, u32[]{:S(2)}) %all-to-all-start) | async-done | bytes 393248 | tf_op jit(solution)/shard_map/all_to_all | solution.py:70
  32.7 3.5 all-to-all-start.1
  36.1 0.8 copy_bitcast_fusion.3
  37.0 13.3 %all-to-all-done.1 = bf16[192,8,128]{2,0,1:T(8,128)(2,1)S(1)} async-done(((bf16[192,8,128]{2,0,1:T(8,128)(2,1)}), bf16[192,8,128]{2,0,1:T(8,128)(2,1)S(1)}, u32[]{:S(2)}, u32[]{:S(2)}) %all-to-all-start.1) | async-done | bytes 393248 | tf_op jit(solution)/shard_map/all_to_all | solution.py:71
  50.3 3.5 all-to-all-start.3
  54.4 98.2 %all-gather.5.cloned.1.call-done = bf16[3072,1024]{1,0:T(8,128)(2,1)} async-done(((bf16[24,1024]{1,0:T(8,128)(2,1)}), bf16[3072,1024]{1,0:T(8,128)(2,1)}) %all-gather.5.cloned.1.call-update) | async-done | bytes 6291472 | tf_op jit(solution)/shard_map/all_gather | solution.py:66
  152.6 4.6 fusion.18
  157.2 0.8 copy.71
  158.0 4.5 all-to-all-start.2
  162.6 12.0 %all-to-all-done.2 = bf16[192,8,128]{2,0,1:T(8,128)(2,1)S(1)} async-done(((bf16[192,8,128]{2,0,1:T(8,128)(2,1)}), bf16[192,8,128]{2,0,1:T(8,128)(2,1)S(1)}, u32[]{:S(2)}, u32[]{:S(2)}) %all-to-all-start.2) | async-done | bytes 393248 | tf_op jit(solution)/shard_map/all_to_all | solution.py:73
  174.6 60.3 %while.30 = (s32[]{:T(128)}, f32[1536,128]{1,0:T(8,128)}, f32[1536,128]{1,0:T(8,128)}, bf16[3,512,128]{2,1,0:T(8,128)(2,1)}, bf16[3,512,128]{2,1,0:T(8,128)(2,1)...) while((s32[]{:T(128)}, f32[1536,128]{1,0:T(8,128)}, ...), condition=%wide.region_4.5_spmd.clone, body=%wide.region_0.4_spmd.clone.sunk | while | flops 1218772992 | bytes 53889268 | solution.py:43
  179.7 2.3 convert_bitcast_fusion.2
  182.0 1.7 copy.75
  183.7 1.6 constant_dynamic-update-slice_fusion.2
  185.3 2.4 convolution_add_fusion.2
  187.7 1.7 fusion.74
  189.4 2.3 fusion.76
  191.7 1.8 fusion.75
  193.6 0.9 copy-done.7
  199.6 2.3 convert_bitcast_fusion.2
  201.9 1.7 copy.75
  203.6 1.6 constant_dynamic-update-slice_fusion.2
  205.2 2.7 convolution_add_fusion.2
  207.9 1.7 fusion.74
  209.6 2.3 fusion.76
  211.9 1.8 fusion.75
  213.8 0.9 copy-done.7
  219.8 2.3 convert_bitcast_fusion.2
  222.1 1.7 copy.75
  223.8 1.6 constant_dynamic-update-slice_fusion.2
  225.4 2.7 convolution_add_fusion.2
  228.1 1.7 fusion.74
  229.8 2.3 fusion.76
  232.1 1.8 fusion.75
  234.0 0.9 copy-done.7
  234.9 15.2 %all_to_all.140 = bf16[8,192,128]{2,1,0:T(8,128)(2,1)S(1)} all-to-all(bf16[8,192,128]{2,1,0:T(8,128)(2,1)} %bitcast.107), channel_id=1, replica_groups=mesh['dp'=16,'seq'=8,'tensor'=2] {'seq'}, dimensions={0} | all-to-all | bytes 786432 | tf_op jit(solution)/shard_map/all_to_all | solution.py:94
  250.2 7.7 fusion.19
  257.9 3.6 all-to-all-start.4
  262.3 11.4 %all-to-all-done.4 = bf16[8,192,128]{2,1,0:T(8,128)(2,1)S(1)} async-done(((bf16[8,192,128]{2,1,0:T(8,128)(2,1)}), bf16[8,192,128]{2,1,0:T(8,128)(2,1)S(1)}, u32[]{:S(2)}, u32[]{:S(2)}) %all-to-all-start.4) | async-done | bytes 393248 | tf_op jit(solution)/shard_map/all_to_all | solution.py:95
  273.7 3.5 all-to-all-start.5
  277.2 0.8 convert_element_type.36
  278.0 11.3 %all-to-all-done.5 = bf16[8,192,128]{2,1,0:T(8,128)(2,1)S(1)} async-done(((bf16[8,192,128]{2,1,0:T(8,128)(2,1)}), bf16[8,192,128]{2,1,0:T(8,128)(2,1)S(1)}, u32[]{:S(2)}, u32[]{:S(2)}) %all-to-all-start.5) | async-done | bytes 393248 | tf_op jit(solution)/shard_map/all_to_all | solution.py:96
  289.3 3.5 all-to-all-start.6
  294.3 10.6 all-to-all-done.6
  305.7 774.7 %reduce-scatter.2.cloned.1.call-done = f32[24,1024]{1,0:T(8,128)} async-done(((f32[3072,1024]{1,0:T(8,128)}), f32[24,1024]{1,0:T(8,128)}) %reduce-scatter.2.cloned.1.call-update) | async-done | bytes 98320 | tf_op jit(solution)/shard_map/reduce_scatter | solution.py:100
  (138 shorter events, 17.8 us)
Async XLA Ops:
  7.2 1.5 copy-start
  7.2 28.9 %copy-start.16 = (bf16[192,1024]{1,0:T(8,128)(2,1)S(1)}, bf16[192,1024]{1,0:T(8,128)(2,1)}, u32[]{:S(2)}) copy-start(bf16[192,1024]{1,0:T(8,128)(2,1)} %param.11) | copy-start | bytes 1179652
  7.2 145.4 %copy-start.17 = (f32[1,3072]{1,0:T(1,128)S(1)}, f32[1,3072]{1,0:T(1,128)}, u32[]{:S(2)}) copy-start(f32[1,3072]{1,0:T(1,128)} %param.13) | copy-start | bytes 36868
  7.2 47.2 %all-gather.3.cloned.1.call-start = ((), (), s32[]{:S(2)}) async-start(), calls=%async_computation.9 | async-start | bytes 1769472 | tf_op jit(solution)/shard_map/all_gather | solution.py:57
  7.9 144.6 %all-gather.5.cloned.1.call-start = ((), (), s32[]{:S(2)}) async-start(), calls=%async_computation.10 | async-start | bytes 6340608 | tf_op jit(solution)/shard_map/all_gather | solution.py:66
  9.5 23.2 %all-to-all-start = ((bf16[192,8,128]{2,0,1:T(8,128)(2,1)}), bf16[192,8,128]{2,0,1:T(8,128)(2,1)S(1)}, u32[]{:S(2)}, u32[]{:S(2)}) async-start(bf16[192,8,128]{2,0,1:T(8,128)(2,1)} %copy_bitcast_fusion.6), calls=%async_computation | async-start | bytes 786432 | tf_op jit(solution)/shard_map/all_to_all | solution.py:70
  32.7 17.6 %all-to-all-start.1 = ((bf16[192,8,128]{2,0,1:T(8,128)(2,1)}), bf16[192,8,128]{2,0,1:T(8,128)(2,1)S(1)}, u32[]{:S(2)}, u32[]{:S(2)}) async-start(bf16[192,8,128]{2,0,1:T(8,128)(2,1)} %copy_bitcast_fusion.5), calls=%async_computation.1 | async-start | bytes 786432 | tf_op jit(solution)/shard_map/all_to_all | solution.py:71
  50.3 107.8 %all-to-all-start.3 = ((bf16[192,8,128]{2,0,1:T(8,128)(2,1)}), bf16[192,8,128]{2,0,1:T(8,128)(2,1)S(1)}, u32[]{:S(2)}, u32[]{:S(2)}) async-start(bf16[192,8,128]{2,0,1:T(8,128)(2,1)} %copy_bitcast_fusion.3), calls=%async_computation.3 | async-start | bytes 786432 | tf_op jit(solution)/shard_map/all_to_all | solution.py:72
  54.4 102.8 %copy-start.18 = (pred[192]{0:T(512)(128)(4,1)}, pred[192]{0:T(512)(128)(4,1)S(1)}, u32[]{:S(2)}) copy-start(pred[192]{0:T(512)(128)(4,1)S(1)} %add_compare_fusion) | copy-start | bytes 580
  158.0 16.6 %all-to-all-start.2 = ((bf16[192,8,128]{2,0,1:T(8,128)(2,1)}), bf16[192,8,128]{2,0,1:T(8,128)(2,1)S(1)}, u32[]{:S(2)}, u32[]{:S(2)}) async-start(bf16[192,8,128]{2,0,1:T(8,128)(2,1)} %bitcast.79), calls=%async_computation.2 | async-start | bytes 786432 | tf_op jit(solution)/shard_map/all_to_all | solution.py:73
  162.5 917.9 %reduce-scatter.2.cloned.1.call-start = ((), (), s32[]{:S(2)}) async-start(), calls=%async_computation.11 | async-start | bytes 12681216 | tf_op jit(solution)/shard_map/reduce_scatter | solution.py:100
  174.6 3.6 copy-start.9
  174.6 3.6 copy-start.12
  174.7 3.6 copy-start.14
  176.8 1.5 copy-start.1
  183.7 4.0 copy-start.2
  187.7 4.1 copy-start.6
  189.3 5.1 copy-start.4
  189.4 5.1 copy-start.10
  189.4 5.1 copy-start.13
  189.4 5.1 copy-start.15
  189.4 5.1 copy-start.20
  194.5 3.6 copy-start.9
  194.6 3.6 copy-start.12
  194.6 3.6 copy-start.14
  196.6 1.5 copy-start.1
  203.6 4.3 copy-start.2
  207.9 4.1 copy-start.6
  209.5 5.1 copy-start.4
  209.5 5.1 copy-start.10
  209.6 5.1 copy-start.13
  209.6 5.1 copy-start.15
  209.6 5.1 copy-start.20
  214.7 3.6 copy-start.9
  214.7 3.6 copy-start.12
  214.8 3.6 copy-start.14
  223.8 4.3 copy-start.2
  228.1 4.1 copy-start.6
  229.7 5.1 copy-start.4
  229.7 5.1 copy-start.10
  229.8 5.1 copy-start.13
  229.8 5.1 copy-start.15
  229.8 5.1 copy-start.20
  257.9 3.6 copy-start.8
  257.9 19.2 %copy-start.5 = (f32[1536,128]{1,0:T(8,128)S(1)}, f32[1536,128]{1,0:T(8,128)}, u32[]{:S(2)}) copy-start(f32[1536,128]{1,0:T(8,128)} %get-tuple-element.96) | copy-start | bytes 2359300
  257.9 15.8 %all-to-all-start.4 = ((bf16[8,192,128]{2,1,0:T(8,128)(2,1)}), bf16[8,192,128]{2,1,0:T(8,128)(2,1)S(1)}, u32[]{:S(2)}, u32[]{:S(2)}) async-start(bf16[8,192,128]{2,1,0:T(8,128)(2,1)} %bitcast.10), calls=%async_computation.4 | async-start | bytes 786432 | tf_op jit(solution)/shard_map/all_to_all | solution.py:95
  273.7 15.6 %all-to-all-start.5 = ((bf16[8,192,128]{2,1,0:T(8,128)(2,1)}), bf16[8,192,128]{2,1,0:T(8,128)(2,1)S(1)}, u32[]{:S(2)}, u32[]{:S(2)}) async-start(bf16[8,192,128]{2,1,0:T(8,128)(2,1)} %bitcast.12), calls=%async_computation.5 | async-start | bytes 786432 | tf_op jit(solution)/shard_map/all_to_all | solution.py:96
  289.3 15.7 %all-to-all-start.6 = ((bf16[8,192,128]{2,1,0:T(8,128)(2,1)}), bf16[8,192,128]{2,1,0:T(8,128)(2,1)S(1)}, u32[]{:S(2)}, u32[]{:S(2)}) async-start(bf16[8,192,128]{2,1,0:T(8,128)(2,1)} %bitcast.14), calls=%async_computation.6 | async-start | bytes 786432 | tf_op jit(solution)/shard_map/all_to_all | solution.py:97
  (13 other events, 15.4 us)
Sparse Core Ops, SparseCore 0:
  9.8 17.4 all-gather.2
  31.0 121.4 all-gather.4
  258.0 822.3 reduce-scatter.1
where the time goes:
time: 1090 us
  waiting for transfers between devices  946 us (87%)
  matrix products  46.6 us (4%)
  starting transfers between devices  30.5 us (3%)
  local copies, waits for them, and re-layouts  24.5 us (2%)
  blocking collectives  15.2 us (1%)
  between operations  14.6 us (1%)
    reduce_scatter x1, waiting for transfers between devices, per_device(): lax.psum_scatter(lax.dot_general(columns, token_out, (((0,), (0,)), ((),...  775 us
    all_gather x1, waiting for transfers between devices, per_device(): lax.all_gather(proj_weight, ('dp', 'seq'), axis=0, tiled=True)  98.2 us
  transfers between devices with their start and end apart: 10, of which 8 were waited for; matrix products, arithmetic and copies ran while one was open for 1% of the time, Pallas kernels for 0%

commit v1 on v0

v1 whole, which is shorter than its diff:
```python
import functools
import math

import jax
import jax.numpy as jnp
from jax import lax
from jax.experimental import pallas as pl
from jax.experimental.pallas import tpu as pltpu
from jax.sharding import PartitionSpec as P

HD = 128
BLOCK = 256
VMEM_LIMIT = 48 * 1024 * 1024
BF16 = jnp.bfloat16
F32 = jnp.float32
FACTOR = HD**-0.5
FACTOR_LOG2 = HD**-0.5 * math.log2(math.e)
NT = (((1,), (1,)), ((), ()))


def cost(flops, read, exps=0):
    return pl.CostEstimate(flops=int(flops), bytes_accessed=int(read), transcendentals=int(exps))


def params():
    return pltpu.CompilerParams(vmem_limit_bytes=VMEM_LIMIT)


def pack_kernel(query_ref, key_ref, value_ref, weight_ref, out_ref):
    rows = query_ref.shape[0]
    out_ref[0, 0:rows, :] = query_ref[...]
    out_ref[0, rows : 2 * rows, :] = key_ref[...]
    out_ref[0, 2 * rows : 3 * rows, :] = value_ref[...]
    weight = weight_ref[...].astype(F32)
    spare = out_ref.shape[1] - 3 * rows - weight.shape[0]
    weight = jnp.concatenate([weight, jnp.zeros((spare, HD), F32)], axis=0)
    out_ref[0, 3 * rows :, :] = weight.astype(BF16)


def pack(queries, keys, values, weight, slots):
    rows = queries.shape[0]
    wrows = weight.shape[0]
    height = 3 * rows + -(-wrows // 16) * 16
    column = pl.BlockSpec((rows, HD), lambda z: (0, z))
    return pl.pallas_call(
        pack_kernel,
        grid=(slots,),
        out_shape=jax.ShapeDtypeStruct((slots, height, HD), BF16),
        in_specs=[column, column, column, pl.BlockSpec((wrows, HD), lambda z: (0, z))],
        out_specs=pl.BlockSpec((1, height, HD), lambda z: (z, 0, 0)),
        compiler_params=params(),
        cost_estimate=cost(0, 2 * 2 * slots * height * HD),
    )(queries, keys, values, weight)


def unpack_kernel(packed_ref, query_ref, key_ref, value_ref, weight_ref):
    rows = query_ref.shape[0]
    query_ref[...] = packed_ref[0, 0:rows, :]
    key_ref[...] = packed_ref[0, rows : 2 * rows, :]
    value_ref[...] = packed_ref[0, 2 * rows : 3 * rows, :]
    weight_ref[...] = packed_ref[0, 3 * rows :, :].astype(F32)[: weight_ref.shape[0]]


def unpack(packed, rows, wrows):
    slots, height, _ = packed.shape
    column = pl.BlockSpec((rows, HD), lambda z: (0, z))
    token = jax.ShapeDtypeStruct((rows, slots * HD), BF16)
    return pl.pallas_call(
        unpack_kernel,
        grid=(slots,),
        out_shape=[token, token, token, jax.ShapeDtypeStruct((wrows, slots * HD), F32)],
        in_specs=[pl.BlockSpec((1, height, HD), lambda z: (z, 0, 0))],
        out_specs=[column, column, column, pl.BlockSpec((wrows, HD), lambda z: (0, z))],
        compiler_params=params(),
        cost_estimate=cost(0, 2 * 2 * slots * height * HD),
    )(packed)


def forward_kernel(rows, length_ref, packed_ref, probs_ref, out_ref, low_ref, value_t):
    slots = packed_ref.shape[0]
    total = slots * rows
    step = pl.program_id(0)

    @pl.when(step == 0)
    def _():
        value_t[...] = packed_ref[:, 2 * rows : 3 * rows, :].reshape(total, HD).T

    keys = packed_ref[:, rows : 2 * rows, :].reshape(total, HD)
    queries = packed_ref[:, 0:rows, :].reshape(total, HD)
    for number in range(total // BLOCK):

        @pl.when(step == number)
        def _():
            block = queries[number * BLOCK : (number + 1) * BLOCK]
            scores = lax.dot_general(keys, block, NT, preferred_element_type=F32)
            live = lax.broadcasted_iota(jnp.int32, (total, BLOCK), 0) < length_ref[0]
            scores = jnp.where(live, scores, -jnp.inf)
            top = jnp.max(scores, axis=0, keepdims=True)
            weights = jnp.exp2((scores - top) * FACTOR_LOG2)
            probs = weights * (1.0 / jnp.sum(weights, axis=0, keepdims=True))
            low = probs.astype(BF16)
            probs_ref[...] = low
            output = jnp.dot(value_t[...], low, preferred_element_type=F32)
            out_ref[...] = output
            low_ref[...] = output.astype(BF16)


def attend_forward(packed, lengths, rows):
    slots = packed.shape[0]
    total = slots * rows
    return pl.pallas_call(
        functools.partial(forward_kernel, rows),
        grid=(total // BLOCK,),
        out_shape=[
            jax.ShapeDtypeStruct((total, total), BF16),
            jax.ShapeDtypeStruct((HD, total), F32),
            jax.ShapeDtypeStruct((HD, total), BF16),
        ],
        in_specs=[
            pl.BlockSpec(memory_space=pltpu.SMEM),
            pl.BlockSpec(packed.shape, lambda i: (0, 0, 0)),
        ],
        out_specs=[
            pl.BlockSpec((total, BLOCK), lambda i: (0, i)),
            pl.BlockSpec((HD, BLOCK), lambda i: (0, i)),
            pl.BlockSpec((HD, BLOCK), lambda i: (0, i)),
        ],
        scratch_shapes=[pltpu.VMEM((HD, total), BF16)],
        compiler_params=params(),
        cost_estimate=cost(8 * total * total * HD, 2 * total * total, total * total),
    )(lengths, packed)


def project_kernel(grad_ref, weight_ref, own_ref, other_ref):
    product = jnp.dot(grad_ref[...], weight_ref[...], preferred_element_type=F32)
    own_ref[...] = product[:, :HD]
    other_ref[...] = product[:, HD:].astype(BF16)


def project(grad, weight):
    total, features = grad.shape
    return pl.pallas_call(
        project_kernel,
        grid=(total // BLOCK,),
        out_shape=[
            jax.ShapeDtypeStruct((total, HD), F32),
            jax.ShapeDtypeStruct((total, HD), BF16),
        ],
        in_specs=[
            pl.BlockSpec((BLOCK, features), lambda i: (i, 0)),
            pl.BlockSpec((features, 2 * HD), lambda i: (0, 0)),
        ],
        out_specs=[pl.BlockSpec((BLOCK, HD), lambda i: (i, 0))] * 2,
        compiler_params=params(),
        cost_estimate=cost(4 * total * features * HD, 2 * total * features),
    )(grad, weight)


def weight_grad_kernel(own_t_ref, other_t_ref, grad_ref, own_ref, other_ref):
    for source, target in ((own_t_ref, own_ref), (other_t_ref, other_ref)):
        product = jnp.dot(source[...], grad_ref[...], preferred_element_type=F32)
        target[...] = product.T.astype(BF16)


def weight_grad(own_t, other_t, grad):
    total, features = grad.shape
    return pl.pallas_call(
        weight_grad_kernel,
        grid=(features // BLOCK,),
        out_shape=[jax.ShapeDtypeStruct((features, HD), BF16)] * 2,
        in_specs=[
            pl.BlockSpec((HD, total), lambda i: (0, 0)),
            pl.BlockSpec((HD, total), lambda i: (0, 0)),
            pl.BlockSpec((total, BLOCK), lambda i: (0, i)),
        ],
        out_specs=[pl.BlockSpec((BLOCK, HD), lambda i: (i, 0))] * 2,
        compiler_params=params(),
        cost_estimate=cost(4 * total * features * HD, 2 * total * features),
    )(own_t, other_t, grad)


def backward_kernel(
    rows, packed_ref, probs_ref, out_ref, own_ref, got_ref, result_ref, key_t, query_acc, key_acc, value_acc
):
    slots = packed_ref.shape[0]
    total = slots * rows
    step = pl.program_id(0)
    keys = packed_ref[:, rows : 2 * rows, :].reshape(total, HD)

    @pl.when(step == 0)
    def _():
        key_t[...] = keys.T
        key_acc[...] = jnp.zeros_like(key_acc)
        value_acc[...] = jnp.zeros_like(value_acc)

    values = packed_ref[:, 2 * rows : 3 * rows, :].reshape(total, HD)
    queries = packed_ref[:, 0:rows, :].reshape(total, HD)
    grad = (own_ref[...] + got_ref[...].astype(F32)).astype(BF16)
    delta = jnp.sum(grad.astype(F32).T * out_ref[...], axis=0, keepdims=True)
    prob_grad = lax.dot_general(values, grad, NT, preferred_element_type=F32)
    low = probs_ref[...]
    score_grad = (low.astype(F32) * (prob_grad - delta)).astype(BF16)
    value_acc[...] += jnp.dot(low, grad, preferred_element_type=F32)
    query_t = jnp.dot(key_t[...], score_grad, preferred_element_type=F32) * FACTOR
    for number in range(total // BLOCK):

        @pl.when(step == number)
        def _():
            block = queries[number * BLOCK : (number + 1) * BLOCK]
            key_acc[...] += jnp.dot(score_grad, block, preferred_element_type=F32)
            query_acc[number * BLOCK : (number + 1) * BLOCK, :] = query_t.T.astype(BF16)

    @pl.when(step == total // BLOCK - 1)
    def _():
        result_ref[:, 0:rows, :] = query_acc[...].reshape(slots, rows, HD)
        result_ref[:, rows : 2 * rows, :] = (
            (key_acc[...] * FACTOR).astype(BF16).reshape(slots, rows, HD)
        )
        result_ref[:, 2 * rows : 3 * rows, :] = value_acc[...].astype(BF16).reshape(slots, rows, HD)


def attend_backward(packed, probs, out, own, got, rows):
    slots = packed.shape[0]
    total = slots * rows
    return pl.pallas_call(
        functools.partial(backward_kernel, rows),
        grid=(total // BLOCK,),
        out_shape=jax.ShapeDtypeStruct((slots, 3 * rows, HD), BF16),
        in_specs=[
            pl.BlockSpec(packed.shape, lambda i: (0, 0, 0)),
            pl.BlockSpec((total, BLOCK), lambda i: (0, i)),
            pl.BlockSpec((HD, BLOCK), lambda i: (0, i)),
            pl.BlockSpec((BLOCK, HD), lambda i: (i, 0)),
            pl.BlockSpec((BLOCK, HD), lambda i: (i, 0)),
        ],
        out_specs=pl.BlockSpec((slots, 3 * rows, HD), lambda i: (0, 0, 0)),
        scratch_shapes=[
            pltpu.VMEM((HD, total), BF16),
            pltpu.VMEM((total, HD), BF16),
            pltpu.VMEM((total, HD), F32),
            pltpu.VMEM((total, HD), F32),
        ],
        compiler_params=params(),
        cost_estimate=cost(8 * total * total * HD, 2 * total * total),
    )(packed, probs, out, own, got)


def per_device(queries, keys, values, out_grad, gate, proj_weight, lengths):
    seq = lax.axis_size("seq")
    rows = queries.shape[0]
    half = out_grad.shape[1]
    wrows = proj_weight.shape[0]
    core = lax.axis_index("tensor")
    swap = [(0, 1), (1, 0)]

    position = lax.axis_index("seq") * rows + jnp.arange(rows, dtype=jnp.int32)
    live = position < lengths[0]
    gate_here = lax.dynamic_slice_in_dim(gate, core * half, half, 1)
    scaled = jnp.where(live[:, None], out_grad.astype(F32) * gate_here, 0.0).astype(BF16)
    grad = lax.all_gather(scaled, "seq", axis=0, tiled=True)

    packed = lax.all_to_all(
        pack(queries, keys, values, proj_weight, seq), "seq", split_axis=0, concat_axis=0, tiled=True
    )
    weight_rows = packed[:, 3 * rows : 3 * rows + wrows].reshape(seq * wrows, HD)
    weight_head = lax.all_gather(weight_rows, "dp", axis=0, tiled=True)
    weight_own = lax.dynamic_slice_in_dim(weight_head, core * half, half, 0)
    weight_send = lax.dynamic_slice_in_dim(weight_head, (1 - core) * half, half, 0)
    weight_other = lax.ppermute(weight_send, "tensor", swap)
    weight = jnp.concatenate([weight_own, weight_other], axis=1)

    probs, out, low = attend_forward(packed, lengths, rows)
    low_other = lax.ppermute(low, "tensor", swap)

    own, other = project(grad, weight)
    got = lax.ppermute(other, "tensor", swap)

    proj_own, proj_send = weight_grad(low, low_other, grad)
    proj_got = lax.ppermute(proj_send, "tensor", swap)
    first = jnp.where(core == 0, proj_own, proj_got)
    second = jnp.where(core == 0, proj_got, proj_own)
    parts = jnp.concatenate([first, second], axis=0).reshape(-1, seq * wrows, HD)
    parts = lax.all_to_all(parts, "dp", split_axis=0, concat_axis=0, tiled=True)

    grads = attend_backward(packed, probs, out, own, got, rows)
    proj = jnp.sum(parts.astype(F32), axis=0).astype(BF16).reshape(seq, wrows, HD)
    spare = packed.shape[1] - 3 * rows - wrows
    result = jnp.concatenate([grads, proj, jnp.zeros((seq, spare, HD), BF16)], axis=1)
    result = lax.all_to_all(result, "seq", split_axis=0, concat_axis=0, tiled=True)
    return tuple(unpack(result, rows, wrows))


def solution(mesh):
    token = P(("dp", "seq"), "tensor")
    return jax.shard_map(
        per_device,
        mesh=mesh,
        in_specs=(token, token, token, token, P("dp", None), token, P("dp")),
        out_specs=(token, token, token, token),
        check_vma=False,
    )
```

time: 1090 us -> 196 us (0.18)
  waiting for transfers between devices: 946 us -> 22.6 us
  blocking collectives: 15.2 us -> 115 us
  matrix products: 46.6 us -> 0 us
  Pallas kernels: 0 us -> 32 us
  starting transfers between devices: 30.5 us -> 6.17 us
  local copies, waits for them, and re-layouts: 24.5 us -> 0.2 us
    reduce_scatter x1 -> x0, waiting for transfers between devices: 775 us -> none  [per_device(): lax.psum_scatter(lax.dot_general(columns, token_out, (((0,), (0,)), ((),...]
    all_gather x2 -> x1, waiting for transfers between devices: 98.2 us -> 19.2 us  [per_device(): grad = lax.all_gather(scaled, 'seq', axis=0, tiled=True)]
    all_to_all x1 -> x2, blocking collectives: 15.2 us -> 90.3 us  [the longest x1 52.8 us: per_device(): lax.all_to_all(pack(queries, keys, values, proj_weight, seq), 'seq', spli...]
    all_to_all x7 -> x1, waiting for transfers between devices: 71.4 us -> 0.01 us  [per_device(): parts = lax.all_to_all(parts, 'dp', split_axis=0, concat_axis=0, tiled=True)]
    dot_general x20 -> x0, matrix products: 46.6 us -> none  [the longest x3 7.8 us: visit(): jnp.dot(probs_low.T, grad_block, preferred_element_type=jnp.float32)]
    pallas_call x0 -> x6, Pallas kernels: none -> 32 us  [the longest x1 9.64 us: attend_forward(): pl.pallas_call(functools.partial(forward_kernel, rows), grid=(total // BL...]
    all_to_all x7 -> x1, starting transfers between devices: 30.4 us -> 5.66 us  [per_device(): parts = lax.all_to_all(parts, 'dp', split_axis=0, concat_axis=0, tiled=True)]
    all_gather x0 -> x1, blocking collectives: none -> 24.4 us  [per_device(): weight_head = lax.all_gather(weight_rows, 'dp', axis=0, tiled=True)]
  transfers between devices with their start and end apart: 10 -> 6, of which waited for: 8 -> 3; matrix products, arithmetic and copies ran while one was open for 1% -> 1% of each run, Pallas kernels for 0% -> 12%
where the time goes in v1:
time: 196 us; the launch traced here: 195 us
  blocking collectives  115 us (59%)
  Pallas kernels  32 us (16%)
  waiting for transfers between devices  22.6 us (12%)
  between operations  15 us (8%)
  starting transfers between devices  6.17 us (3%)
  other arithmetic  4.62 us (2%)
    all_to_all x1, blocking collectives, per_device(): lax.all_to_all(pack(queries, keys, values, proj_weight, seq), 'seq', spli...  52.8 us
    all_to_all x1, blocking collectives, per_device(): lax.all_to_all(result, 'seq', split_axis=0, concat_axis=0, tiled=True)  37.6 us
    all_gather x1, blocking collectives, per_device(): weight_head = lax.all_gather(weight_rows, 'dp', axis=0, tiled=True)  24.4 us
    all_gather x1, waiting for transfers between devices, per_device(): grad = lax.all_gather(scaled, 'seq', axis=0, tiled=True)  19.2 us
    pallas_call x1, Pallas kernels, attend_forward(): pl.pallas_call(functools.partial(forward_kernel, rows), grid=(total // BL...  9.64 us
    pallas_call x1, Pallas kernels, attend_backward(): pl.pallas_call(functools.partial(backward_kernel, rows), grid=(total // B...  8.53 us
    all_to_all x1, starting transfers between devices, per_device(): parts = lax.all_to_all(parts, 'dp', split_axis=0, concat_axis=0, tiled=True)  5.66 us
    pallas_call x1, Pallas kernels, weight_grad(): pl.pallas_call(weight_grad_kernel, grid=(features // BLOCK,), out_shape=[...  5.38 us
  transfers between devices with their start and end apart: 6, of which 3 were waited for; matrix products, arithmetic and copies ran while one was open for 1% of the time, Pallas kernels for 12%

profile of v1, /device:TPU:2, one launch (start us, length us, event | category | flops | bytes accessed | tf_op | source)
XLA Modules:
  0.0 195.4 jit_solution(3139294421580654487)
XLA Ops:
  7.2 0.0 copy-start
  7.2 0.0 copy-start.3
  7.2 0.0 copy-start.4
  7.2 0.0 copy-start.5
  7.2 0.0 copy-start.6
  7.2 0.0 all-gather.2.cloned.1.call-start
  8.0 0.0 copy-done
  8.1 2.1 %select_convert_fusion = bf16[192,1536]{1,0:T(8,128)(2,1)} fusion(bf16[192,1536]{1,0:T(8,128)(2,1)} %param.10, f32[1536]{0:T(1024)S(1)} %dynamic-slice_reduce_fusion, pred[192]{0:T(512)(128)(4,1)S(1)} %add_compare_fusion), kind=kLoop, calls=%fused_computation.1 | loop fusion | flops 1179648 | bytes 1185984 | tf_op jit(solution)/shard_map/convert_element_type | solution.py:259
  10.1 0.0 all-gather.2.cloned.1.call-update
  10.2 0.0 copy-done.3
  10.2 0.0 copy-done.4
  10.2 0.0 copy-done.5
  10.2 0.0 copy-done.6
  10.2 0.6 shard_map.102
  10.8 52.8 %all_to_all.15.packed_ref = bf16[8,608,128]{2,1,0:T(8,128)(2,1)S(1)} all-to-all(bf16[8,608,128]{2,1,0:T(8,128)(2,1)S(1)} %shard_map.102), channel_id=1, replica_groups=mesh['dp'=16,'seq'=8,'tensor'=2] {'seq'}, dimensions={0} | all-to-all | bytes 2490368 | tf_op jit(solution)/shard_map/all_to_all | solution.py:262
  63.6 0.0 copy-start.1
  63.6 9.6 %shard_map.103 = (bf16[1536,1536]{1,0:T(8,128)(2,1)}, f32[128,1536]{1,0:T(8,128)S(1)}, bf16[128,1536]{1,0:T(8,128)(2,1)S(1)}) custom-call(s32[1]{0:T(128)} %copy.11.length_ref, bf16[8,608,128]{2,1,0:T(8,128)(2,1)S(1)} %all_to_all.15.packed_ref), custom_call_target="tpu_custom_call" | custom-call | flops 2415919104 | bytes 4718592 | tf_op jit(solution)/shard_map/pallas_call | solution.py:111
  73.3 0.0 collective-permute-start.2
  73.3 0.0 copy-done.1
  73.3 0.0 slice-start
  73.3 1.7 collective-permute-done.2.other_t_ref
  75.0 19.2 %all-gather.2.cloned.1.call-done.grad_ref = bf16[1536,1536]{1,0:T(8,128)(2,1)} async-done(((bf16[192,1536]{1,0:T(8,128)(2,1)}), bf16[1536,1536]{1,0:T(8,128)(2,1)}) %all-gather.2.cloned.1.call-update) | async-done | bytes 4718608 | tf_op jit(solution)/shard_map/all_gather | solution.py:260
  94.2 5.4 %shard_map.106 = (bf16[1536,128]{1,0:T(8,128)(2,1)S(1)}, bf16[1536,128]{1,0:T(8,128)(2,1)S(1)}) custom-call(bf16[128,1536]{1,0:T(8,128)(2,1)S(1)} %get-tuple-element.15.own_t_ref, bf16[128,1536]{1,0:T(8,128)(2,1)S(1)} %collective-permute-done.2.other_t_ref, bf16[1536,1536]{1,0:T(8,128)(2,1)} %all-gather.2.cloned.1.call-done.grad_ref), custom_call_target="tpu_custom_call" | custom-call | flops 1207959552 | bytes 4718592 | tf_op jit(solution)/shard_map/pallas_call | solution.py:167
  99.6 0.1 collective-permute-start.3
  99.7 0.0 slice-done
  99.7 24.4 %all_gather.7 = bf16[3072,128]{1,0:T(8,128)(2,1)S(1)} all-gather(bf16[192,128]{1,0:T(8,128)(2,1)S(1)} %bitcast.5), channel_id=1, replica_groups=mesh['dp'=16,'seq'=8,'tensor'=2] {'dp'}, dimensions={0}, use_global_device_ids=true | all-gather | bytes 835584 | tf_op jit(solution)/shard_map/all_gather | solution.py:266
  124.1 0.1 constant_dynamic-slice_fusion.1
  124.2 0.1 collective-permute-start
  124.3 0.0 collective-permute-done.3
  124.3 0.1 broadcast_select_fusion.1
  124.4 0.9 pad_maximum_fusion.1
  125.3 5.7 %all-to-all-start.1 = ((bf16[16,192,128]{2,1,0:T(8,128)(2,1)}), bf16[16,192,128]{2,1,0:T(8,128)(2,1)S(1)}, u32[]{:S(2)}, u32[]{:S(2)}) async-start(bf16[16,192,128]{2,1,0:T(8,128)(2,1)} %bitcast.2), calls=%async_computation.1 | async-start | bytes 1572864 | tf_op jit(solution)/shard_map/all_to_all | solution.py:283
  131.0 0.0 collective-permute-done
  131.0 1.1 pad_maximum_fusion.weight_ref
  132.1 0.0 copy-start.2
  132.1 5.2 %shard_map.104 = (f32[1536,128]{1,0:T(8,128)S(1)}, bf16[1536,128]{1,0:T(8,128)(2,1)S(1)}) custom-call(bf16[1536,1536]{1,0:T(8,128)(2,1)} %all-gather.2.cloned.1.call-done.grad_ref, bf16[1536,256]{1,0:T(8,128)(2,1)S(1)} %pad_maximum_fusion.weight_ref), custom_call_target="tpu_custom_call" | custom-call | flops 1207959552 | bytes 4718592 | tf_op jit(solution)/shard_map/pallas_call | solution.py:142
  137.3 0.3 collective-permute-start.1
  137.6 0.1 pad.2.clone
  137.6 1.6 collective-permute-done.1.got_ref
  139.3 0.0 copy-done.2
  139.3 8.5 %shard_map.105 = bf16[8,576,128]{2,1,0:T(8,128)(2,1)S(1)} custom-call(bf16[8,608,128]{2,1,0:T(8,128)(2,1)S(1)} %copy-done.2, bf16[1536,1536]{1,0:T(8,128)(2,1)} %get-tuple-element.11.probs_ref, f32[128,1536]{1,0:T(8,128)S(1)} %get-tuple-element.12.out_ref, f32[1536,128]{1,0:T(8,128)S(1)} %get-tuple-element.13.own_ref, ...), custom_call_target="tpu_custom_call" | custom-call | flops 2415919104 | bytes 4718592 | tf_op jit(solution)/shard_map/pallas_call | solution.py:225
  147.8 0.0 all-to-all-done.1
  147.8 0.1 reduce_sum.12
  147.9 0.3 maximum_maximum_fusion
  148.2 37.6 %all_to_all.16.packed_ref = bf16[8,608,128]{2,1,0:T(8,128)(2,1)S(1)} all-to-all(bf16[8,608,128]{2,1,0:T(8,128)(2,1)S(1)} %maximum_maximum_fusion), channel_id=1, replica_groups=mesh['dp'=16,'seq'=8,'tensor'=2] {'seq'}, dimensions={0} | all-to-all | bytes 2490368 | tf_op jit(solution)/shard_map/all_to_all | solution.py:289
  185.8 2.7 %shard_map.107 = (bf16[192,1024]{1,0:T(8,128)(2,1)}, bf16[192,1024]{1,0:T(8,128)(2,1)}, bf16[192,1024]{1,0:T(8,128)(2,1)}, f32[24,1024]{1,0:T(8,128)}) custom-call(bf16[8,608,128]{2,1,0:T(8,128)(2,1)S(1)} %all_to_all.16.packed_ref), custom_call_target="tpu_custom_call" | custom-call | bytes 2490368 | tf_op jit(solution)/shard_map/pallas_call | solution.py:68
  (3 shorter events, 0.0 us)
Async XLA Ops:
  7.2 0.8 copy-start
  7.2 3.0 %copy-start.3 = (bf16[192,1024]{1,0:T(8,128)(2,1)S(1)}, bf16[192,1024]{1,0:T(8,128)(2,1)}, u32[]{:S(2)}) copy-start(bf16[192,1024]{1,0:T(8,128)(2,1)} %query_ref.1) | copy-start | bytes 1179652
  7.2 3.0 %copy-start.4 = (bf16[192,1024]{1,0:T(8,128)(2,1)S(1)}, bf16[192,1024]{1,0:T(8,128)(2,1)}, u32[]{:S(2)}) copy-start(bf16[192,1024]{1,0:T(8,128)(2,1)} %key_ref.1) | copy-start | bytes 1179652
  7.2 3.0 %copy-start.5 = (bf16[192,1024]{1,0:T(8,128)(2,1)S(1)}, bf16[192,1024]{1,0:T(8,128)(2,1)}, u32[]{:S(2)}) copy-start(bf16[192,1024]{1,0:T(8,128)(2,1)} %value_ref.1) | copy-start | bytes 1179652
  7.2 3.0 %copy-start.6 = (bf16[24,1024]{1,0:T(8,128)(2,1)S(1)}, bf16[24,1024]{1,0:T(8,128)(2,1)}, u32[]{:S(2)}) copy-start(bf16[24,1024]{1,0:T(8,128)(2,1)} %weight_ref.1) | copy-start | bytes 147460
  7.2 87.0 %all-gather.2.cloned.1.call-start = ((), (), s32[]{:S(2)}) async-start(), calls=%async_computation.3 | async-start | bytes 5308416 | tf_op jit(solution)/shard_map/all_gather | solution.py:260
  63.6 9.6 %copy-start.1 = (bf16[8,608,128]{2,1,0:T(8,128)(2,1)}, bf16[8,608,128]{2,1,0:T(8,128)(2,1)S(1)}, u32[]{:S(2)}) copy-start(bf16[8,608,128]{2,1,0:T(8,128)(2,1)S(1)} %all_to_all.15.packed_ref) | copy-start | bytes 3735556
  73.3 1.7 collective-permute-start.2
  73.3 26.5 %slice-start = ((bf16[8,608,128]{2,1,0:T(8,128)(2,1)}), bf16[8,24,128]{2,1,0:T(8,128)(2,1)S(1)}, s32[]{:S(2)}) async-start(bf16[8,608,128]{2,1,0:T(8,128)(2,1)} %copy-done.1), calls=%async_computation.4 | async-start | bytes 98304 | tf_op jit(solution)/shard_map/slice | solution.py:265
  99.6 24.7 %collective-permute-start.3 = (bf16[1536,128]{1,0:T(8,128)(2,1)S(1)}, bf16[1536,128]{1,0:T(8,128)(2,1)S(1)}, u32[]{:S(2)}, u32[]{:S(2)}) collective-permute-start(bf16[1536,128]{1,0:T(8,128)(2,1)S(1)} %get-tuple-element.17), channel_id=1, source_target_pairs={{0,1},{1,0},{2,3},{3,2},{4,5},{5,4},{6,7},{7,6},{8,9},{9,8},{10,11... | collective-permute-start | bytes 1179656 | tf_op jit(solution)/shard_map/ppermute | solution.py:279
  124.2 6.8 %collective-permute-start = (bf16[1536,128]{1,0:T(8,128)(2,1)S(1)}, bf16[1536,128]{1,0:T(8,128)(2,1)}, u32[]{:S(2)}, u32[]{:S(2)}) collective-permute-start(bf16[1536,128]{1,0:T(8,128)(2,1)S(1)} %get-tuple-element.19), channel_id=1, source_target_pairs={{0,1},{1,0},{2,3},{3,2},{4,5},{5,4},{6,7},{7,6},{8,9},{9,8},{10,11... | collective-permute-start | bytes 1179656 | tf_op jit(solution)/shard_map/ppermute | solution.py:269
  125.3 22.5 %all-to-all-start.1 = ((bf16[16,192,128]{2,1,0:T(8,128)(2,1)}), bf16[16,192,128]{2,1,0:T(8,128)(2,1)S(1)}, u32[]{:S(2)}, u32[]{:S(2)}) async-start(bf16[16,192,128]{2,1,0:T(8,128)(2,1)} %bitcast.2), calls=%async_computation.1 | async-start | bytes 1572864 | tf_op jit(solution)/shard_map/all_to_all | solution.py:283
  132.1 7.2 %copy-start.2 = (bf16[8,608,128]{2,1,0:T(8,128)(2,1)S(1)}, bf16[8,608,128]{2,1,0:T(8,128)(2,1)}, u32[]{:S(2)}) copy-start(bf16[8,608,128]{2,1,0:T(8,128)(2,1)} %copy-done.1) | copy-start | bytes 3735556
  137.3 2.0 %collective-permute-start.1 = (bf16[1536,128]{1,0:T(8,128)(2,1)S(1)}, bf16[1536,128]{1,0:T(8,128)(2,1)S(1)}, u32[]{:S(2)}, u32[]{:S(2)}) collective-permute-start(bf16[1536,128]{1,0:T(8,128)(2,1)S(1)} %get-tuple-element.14), channel_id=1, source_target_pairs={{0,1},{1,0},{2,3},{3,2},{4,5},{5,4},{6,7},{7,6},{8,9},{9,8},{10,11... | collective-permute-start | bytes 1179656 | tf_op jit(solution)/shard_map/ppermute | solution.py:276
Sparse Core Ops, SparseCore 0:
  10.3 83.8 all-gather.1

commit v2 on v1

v2 whole, which is shorter than its diff:
```python
import functools
import math

import jax
import jax.numpy as jnp
from jax import lax
from jax.experimental import pallas as pl
from jax.experimental.pallas import tpu as pltpu
from jax.sharding import PartitionSpec as P

HD = 128
PAIR = 2
FBLOCK = 256
VMEM_LIMIT = 48 * 1024 * 1024
BF16 = jnp.bfloat16
F32 = jnp.float32
FACTOR = HD**-0.5
FACTOR_LOG2 = HD**-0.5 * math.log2(math.e)
NT = (((1,), (1,)), ((), ()))
OFFSETS = (-1, 1, -2, 2, -3, 3, 0, 4)
GROUPS = ((0, 4), (4, 6), (6, 8))


def cost(flops, read, exps=0):
    return pl.CostEstimate(flops=int(flops), bytes_accessed=int(read), transcendentals=int(exps))


def params():
    return pltpu.CompilerParams(vmem_limit_bytes=VMEM_LIMIT)


def whole(array):
    zeros = (0,) * array.ndim
    return pl.BlockSpec(array.shape, lambda *_: zeros)


def smem():
    return pl.BlockSpec(memory_space=pltpu.SMEM)


def scale_kernel(length_ref, grad_ref, gate_ref, out_ref):
    rows, half = grad_ref.shape
    start = pl.multiple_of(lax.axis_index("tensor") * half, HD)
    gate = gate_ref[:, pl.ds(start, half)]
    left = length_ref[0] - lax.axis_index("seq") * rows
    live = lax.broadcasted_iota(jnp.int32, (rows, 1), 0) < left
    out_ref[...] = jnp.where(live, grad_ref[...].astype(F32) * gate, 0.0).astype(BF16)


def scale(out_grad, gate, lengths):
    return pl.pallas_call(
        scale_kernel,
        out_shape=jax.ShapeDtypeStruct(out_grad.shape, BF16),
        in_specs=[smem(), whole(out_grad), whole(gate)],
        out_specs=whole(out_grad),
        compiler_params=params(),
        cost_estimate=cost(0, 4 * out_grad.size),
    )(lengths, out_grad, gate)


def pack_kernel(query_ref, key_ref, value_ref, weight_ref, out_ref):
    rows = query_ref.shape[0]
    out_ref[0, 0:rows, :] = query_ref[...]
    out_ref[0, rows : 2 * rows, :] = key_ref[...]
    out_ref[0, 2 * rows : 3 * rows, :] = value_ref[...]
    weight = weight_ref[...].astype(F32)
    spare = out_ref.shape[1] - 3 * rows - weight.shape[0]
    weight = jnp.concatenate([weight, jnp.zeros((spare, HD), F32)], axis=0)
    out_ref[0, 3 * rows :, :] = weight.astype(BF16)


def pack(queries, keys, values, weight, slots):
    rows = queries.shape[0]
    wrows = weight.shape[0]
    height = 3 * rows + -(-wrows // 16) * 16
    column = pl.BlockSpec((rows, HD), lambda z: (0, z))
    return pl.pallas_call(
        pack_kernel,
        grid=(slots,),
        out_shape=jax.ShapeDtypeStruct((slots, height, HD), BF16),
        in_specs=[column, column, column, pl.BlockSpec((wrows, HD), lambda z: (0, z))],
        out_specs=pl.BlockSpec((1, height, HD), lambda z: (z, 0, 0)),
        compiler_params=params(),
        cost_estimate=cost(0, 2 * 2 * slots * height * HD),
    )(queries, keys, values, weight)


def unpack_kernel(packed_ref, query_ref, key_ref, value_ref, weight_ref):
    rows = query_ref.shape[0]
    query_ref[...] = packed_ref[0, 0:rows, :]
    key_ref[...] = packed_ref[0, rows : 2 * rows, :]
    value_ref[...] = packed_ref[0, 2 * rows : 3 * rows, :]
    weight_ref[...] = packed_ref[0, 3 * rows :, :].astype(F32)[: weight_ref.shape[0]]


def unpack(packed, rows, wrows):
    slots, height, _ = packed.shape
    column = pl.BlockSpec((rows, HD), lambda z: (0, z))
    token = jax.ShapeDtypeStruct((rows, slots * HD), BF16)
    return pl.pallas_call(
        unpack_kernel,
        grid=(slots,),
        out_shape=[token, token, token, jax.ShapeDtypeStruct((wrows, slots * HD), F32)],
        in_specs=[pl.BlockSpec((1, height, HD), lambda z: (z, 0, 0))],
        out_specs=[column, column, column, pl.BlockSpec((wrows, HD), lambda z: (0, z))],
        compiler_params=params(),
        cost_estimate=cost(0, 2 * 2 * slots * height * HD),
    )(packed)


def slot_of(number, slots):
    even = number % 2 == 0
    distance = number // 2 + 1
    offset = jnp.where(even, slots - distance, distance)
    offset = jnp.where(number == 6, 0, jnp.where(number == 7, 4, offset))
    return lax.rem(lax.axis_index("seq") + offset, slots)


def forward_kernel(rows, length_ref, packed_ref, weights_ref, inverse_ref, out_ref, low_ref, value_t):
    slots = packed_ref.shape[0]
    total = slots * rows
    step = pl.program_id(0)

    @pl.when(step == 0)
    def _():
        value_t[...] = packed_ref[:, 2 * rows : 3 * rows, :].reshape(total, HD).T

    keys = packed_ref[:, rows : 2 * rows, :].reshape(total, HD)
    block = jnp.concatenate(
        [packed_ref[slot_of(PAIR * step + i, slots), 0:rows, :] for i in range(PAIR)], axis=0
    )
    scores = lax.dot_general(keys, block, NT, preferred_element_type=F32)
    live = lax.broadcasted_iota(jnp.int32, (total, 1), 0) < length_ref[0]
    scores = jnp.where(live, scores, -jnp.inf)
    top = jnp.max(scores, axis=0, keepdims=True)
    weights = jnp.exp2((scores - top) * FACTOR_LOG2)
    inverse = 1.0 / jnp.sum(weights, axis=0, keepdims=True)
    inverse_ref[...] = inverse
    weights = weights.astype(BF16)
    weights_ref[...] = weights
    output = jnp.dot(value_t[...], weights, preferred_element_type=F32) * inverse
    out_ref[...] = output
    low_ref[...] = output.astype(BF16)


def attend_forward(packed, lengths, rows):
    slots = packed.shape[0]
    total = slots * rows
    width = PAIR * rows
    return pl.pallas_call(
        functools.partial(forward_kernel, rows),
        grid=(slots // PAIR,),
        out_shape=[
            jax.ShapeDtypeStruct((total, total), BF16),
            jax.ShapeDtypeStruct((1, total), F32),
            jax.ShapeDtypeStruct((HD, total), F32),
            jax.ShapeDtypeStruct((HD, total), BF16),
        ],
        in_specs=[smem(), whole(packed)],
        out_specs=[
            pl.BlockSpec((total, width), lambda i: (0, i)),
            pl.BlockSpec((1, width), lambda i: (0, i)),
            pl.BlockSpec((HD, width), lambda i: (0, i)),
            pl.BlockSpec((HD, width), lambda i: (0, i)),
        ],
        scratch_shapes=[pltpu.VMEM((HD, total), BF16)],
        compiler_params=params(),
        cost_estimate=cost(4 * total * total * HD, 2 * total * total, total * total),
    )(lengths, packed)


def project_kernel(*refs):
    *grads, weight_ref, own_ref, other_ref = refs
    start = 0
    for grad in grads:
        product = jnp.dot(grad[...], weight_ref[...], preferred_element_type=F32)
        stop = start + grad.shape[0]
        own_ref[start:stop, :] = product[:, :HD]
        other_ref[start:stop, :] = product[:, HD:].astype(BF16)
        start = stop


def project(grads, weight):
    total = sum(grad.shape[0] for grad in grads)
    features = weight.shape[0]
    shapes = [jax.ShapeDtypeStruct((total, HD), F32), jax.ShapeDtypeStruct((total, HD), BF16)]
    return pl.pallas_call(
        project_kernel,
        out_shape=shapes,
        in_specs=[whole(array) for array in (*grads, weight)],
        out_specs=[whole(shape) for shape in shapes],
        compiler_params=params(),
        cost_estimate=cost(4 * total * features * HD, 2 * total * features),
    )(*grads, weight)


def weight_grad_kernel(own_t_ref, other_t_ref, *refs):
    *grads, own_ref, other_ref = refs
    outputs = jnp.concatenate([own_t_ref[...], other_t_ref[...]], axis=0)
    grad = jnp.concatenate([grad[...] for grad in grads], axis=0)
    product = jnp.dot(outputs, grad, preferred_element_type=F32)
    own_ref[...] = product[:HD].T.astype(BF16)
    other_ref[...] = product[HD:].T.astype(BF16)


def weight_grad(own_t, other_t, grads):
    total = own_t.shape[1]
    features = grads[0].shape[1]
    return pl.pallas_call(
        weight_grad_kernel,
        grid=(features // FBLOCK,),
        out_shape=[jax.ShapeDtypeStruct((features, HD), BF16)] * 2,
        in_specs=[whole(own_t), whole(other_t)]
        + [pl.BlockSpec((grad.shape[0], FBLOCK), lambda i: (0, i)) for grad in grads],
        out_specs=[pl.BlockSpec((FBLOCK, HD), lambda i: (i, 0))] * 2,
        compiler_params=params(),
        cost_estimate=cost(4 * total * features * HD, 2 * total * features),
    )(own_t, other_t, *grads)


def backward_kernel(rows, group, first, last, *refs):
    packed_ref, weights_ref, inverse_ref, out_ref, own_ref, got_ref, *refs = refs
    slots = packed_ref.shape[0]
    total = slots * rows
    width = PAIR * rows
    start, stop = group
    steps = (stop - start) // PAIR
    step = pl.program_id(0)
    sums, refs = ((), refs) if first else (refs[:2], refs[2:])
    if last:
        *before, result_ref, key_t, query_acc, key_acc, value_acc = refs
    else:
        query_acc, key_acc, value_acc, key_t = refs
    keys = packed_ref[:, rows : 2 * rows, :].reshape(total, HD)

    @pl.when(step == 0)
    def _():
        key_t[...] = keys.T
        key_acc[...] = jnp.zeros_like(key_acc) if first else sums[0][...]
        value_acc[...] = jnp.zeros_like(value_acc) if first else sums[1][...]

    values = packed_ref[:, 2 * rows : 3 * rows, :].reshape(total, HD)
    block = jnp.concatenate(
        [packed_ref[slot_of(start + PAIR * step + i, slots), 0:rows, :] for i in range(PAIR)], axis=0
    )
    grad = (own_ref[...] + got_ref[...].astype(F32)).astype(BF16)
    delta = jnp.sum(grad.astype(F32).T * out_ref[...], axis=0, keepdims=True)
    inverse = inverse_ref[...]
    prob_grad = lax.dot_general(values, grad, NT, preferred_element_type=F32)
    weights = weights_ref[...]
    score_grad = (weights.astype(F32) * ((prob_grad - delta) * inverse)).astype(BF16)
    scaled = (grad.astype(F32).T * inverse).T.astype(BF16)
    value_acc[...] += jnp.dot(weights, scaled, preferred_element_type=F32)
    key_acc[...] += jnp.dot(score_grad, block, preferred_element_type=F32)
    query_t = jnp.dot(key_t[...], score_grad, preferred_element_type=F32) * FACTOR
    query_acc[pl.ds(pl.multiple_of(step * width, width), width), :] = query_t.T.astype(BF16)

    if last:

        @pl.when(step == steps - 1)
        def _():
            number = 0
            for source in (*before, query_acc):
                for place in range(0, source.shape[0], rows):
                    result_ref[slot_of(number, slots), 0:rows, :] = source[place : place + rows, :]
                    number += 1
            result_ref[:, rows : 2 * rows, :] = (
                (key_acc[...] * FACTOR).astype(BF16).reshape(slots, rows, HD)
            )
            result_ref[:, 2 * rows : 3 * rows, :] = (
                value_acc[...].astype(BF16).reshape(slots, rows, HD)
            )


def attend_backward(packed, state, own, got, rows, group, done, sums):
    weights, inverse, out = state
    slots = packed.shape[0]
    total = slots * rows
    width = PAIR * rows
    start, stop = group
    size = (stop - start) * rows
    first, last = not sums, stop == slots
    shift = start // PAIR
    sum_shapes = [jax.ShapeDtypeStruct((total, HD), F32)] * 2
    if last:
        shapes = [jax.ShapeDtypeStruct((slots, 3 * rows, HD), BF16)]
        scratch = [pltpu.VMEM((size, HD), BF16)] + [pltpu.VMEM((total, HD), F32)] * 2
    else:
        shapes = [jax.ShapeDtypeStruct((size, HD), BF16), *sum_shapes]
        scratch = []
    extra = [*sums, *done] if last else list(sums)
    return pl.pallas_call(
        functools.partial(backward_kernel, rows, group, first, last),
        grid=((stop - start) // PAIR,),
        out_shape=shapes,
        in_specs=[
            whole(packed),
            pl.BlockSpec((total, width), lambda i: (0, i + shift)),
            pl.BlockSpec((1, width), lambda i: (0, i + shift)),
            pl.BlockSpec((HD, width), lambda i: (0, i + shift)),
            pl.BlockSpec((width, HD), lambda i: (i, 0)),
            pl.BlockSpec((width, HD), lambda i: (i, 0)),
            *[whole(array) for array in extra],
        ],
        out_specs=[whole(shape) for shape in shapes],
        scratch_shapes=[pltpu.VMEM((HD, total), BF16), *scratch],
        compiler_params=params(),
        cost_estimate=cost(8 * total * size * HD, 2 * total * size),
    )(packed, weights, inverse, out, own, got, *extra)


def per_device(queries, keys, values, out_grad, gate, proj_weight, lengths):
    seq = lax.axis_size("seq")
    rows = queries.shape[0]
    half = out_grad.shape[1]
    wrows = proj_weight.shape[0]
    core = lax.axis_index("tensor")
    swap = [(0, 1), (1, 0)]
    right = [(i, (i + 1) % seq) for i in range(seq)]
    left = [(i, (i - 1) % seq) for i in range(seq)]

    own_rows = scale(out_grad, gate, lengths)
    from_left, from_right = [own_rows], [own_rows]
    for _ in range(3):
        from_left.append(lax.ppermute(from_left[-1], "seq", right))
        from_right.append(lax.ppermute(from_right[-1], "seq", left))
    far = [
        lax.ppermute(from_left[3][: rows // 2], "seq", right),
        lax.ppermute(from_right[3][rows // 2 :], "seq", left),
    ]
    blocks = [[array] for i in range(1, 4) for array in (from_left[i], from_right[i])] + [[own_rows], far]

    packed = lax.all_to_all(
        pack(queries, keys, values, proj_weight, seq), "seq", split_axis=0, concat_axis=0, tiled=True
    )
    weight_rows = packed[:, 3 * rows : 3 * rows + wrows].reshape(1, seq * wrows, HD)
    copies = jnp.broadcast_to(weight_rows, (lax.axis_size("dp"), seq * wrows, HD))
    weight_head = lax.all_to_all(copies, "dp", split_axis=0, concat_axis=0, tiled=True).reshape(-1, HD)
    weight_own = lax.dynamic_slice_in_dim(weight_head, core * half, half, 0)
    weight_send = lax.dynamic_slice_in_dim(weight_head, (1 - core) * half, half, 0)
    weight_other = lax.ppermute(weight_send, "tensor", swap)
    weight = jnp.concatenate([weight_own, weight_other], axis=1)

    *state, low = attend_forward(packed, lengths, rows)
    low_other = lax.ppermute(low, "tensor", swap)

    done, sums = [], []
    for start, stop in GROUPS:
        own, other = project(sum(blocks[start:stop], []), weight)
        got = lax.ppermute(other, "tensor", swap)
        query_rows, *sums = attend_backward(packed, state, own, got, rows, (start, stop), done, sums)
        done.append(query_rows)
    grads = done[-1]

    proj_own, proj_send = weight_grad(low, low_other, sum(blocks, []))
    proj_got = lax.ppermute(proj_send, "tensor", swap)
    first = jnp.where(core == 0, proj_own, proj_got)
    second = jnp.where(core == 0, proj_got, proj_own)
    parts = jnp.concatenate([first, second], axis=0).reshape(-1, seq * wrows, HD)
    parts = lax.all_to_all(parts, "dp", split_axis=0, concat_axis=0, tiled=True)

    proj = jnp.sum(parts.astype(F32), axis=0).astype(BF16).reshape(seq, wrows, HD)
    spare = packed.shape[1] - 3 * rows - wrows
    result = jnp.concatenate([grads, proj, jnp.zeros((seq, spare, HD), BF16)], axis=1)
    result = lax.all_to_all(result, "seq", split_axis=0, concat_axis=0, tiled=True)
    return tuple(unpack(result, rows, wrows))


def solution(mesh):
    token = P(("dp", "seq"), "tensor")
    return jax.shard_map(
        per_device,
        mesh=mesh,
        in_specs=(token, token, token, token, P("dp", None), token, P("dp")),
        out_specs=(token, token, token, token),
        check_vma=False,
    )
```

time: 196 us -> 184 us (0.939)
  blocking collectives: 115 us -> 38.9 us
  waiting for transfers between devices: 22.6 us -> 56.9 us
  starting transfers between devices: 6.17 us -> 38 us
  between operations: 15 us -> 1.67 us
  local copies, waits for them, and re-layouts: 0.2 us -> 8.88 us
    ppermute x0 -> x8, waiting for transfers between devices: none -> 56.9 us  [the longest x3 50.2 us: per_device(): from_left.append(lax.ppermute(from_left[-1], 'seq', right))]
    all_to_all x1 -> x0, blocking collectives: 52.8 us -> none  [per_device(): lax.all_to_all(pack(queries, keys, values, proj_weight, seq), 'seq', spli...]
    all_gather x1 -> x0, blocking collectives: 24.4 us -> none  [per_device(): weight_head = lax.all_gather(weight_rows, 'dp', axis=0, tiled=True)]
    all_gather x1 -> x0, waiting for transfers between devices: 19.2 us -> none  [per_device(): grad = lax.all_gather(scaled, 'seq', axis=0, tiled=True)]
    all_to_all x0 -> x2, starting transfers between devices: none -> 16.1 us  [the longest x1 8.6 us: per_device(): lax.all_to_all(pack(queries, keys, values, proj_weight, seq), 'seq', spli...]
    ppermute x0 -> x8, starting transfers between devices: none -> 13.2 us  [the longest x3 7.77 us: per_device(): from_right.append(lax.ppermute(from_right[-1], 'seq', left))]
    unnamed x14 -> x32, local copies, waits for them, and re-layouts: 0.03 us -> 4.62 us
    pallas_call x1, Pallas kernels: 0.64 us -> 2.98 us  [pack(): pl.pallas_call(pack_kernel, grid=(slots,), out_shape=jax.ShapeDtypeStruct...]
  transfers between devices with their start and end apart: 6 -> 17, of which waited for: 3 -> 4; matrix products, arithmetic and copies ran while one was open for 1% -> 4% of each run, Pallas kernels for 12% -> 15%
where the time goes in v2:
time: 184 us; the launch traced here: 182 us
  waiting for transfers between devices  56.9 us (31%)
  blocking collectives  38.9 us (21%)
  starting transfers between devices  38 us (21%)
  Pallas kernels  32.9 us (18%)
  local copies, waits for them, and re-layouts  8.88 us (5%)
  other arithmetic  4.82 us (3%)
    ppermute x3, waiting for transfers between devices, per_device(): from_left.append(lax.ppermute(from_left[-1], 'seq', right))  50.2 us
    all_to_all x1, blocking collectives, per_device(): lax.all_to_all(result, 'seq', split_axis=0, concat_axis=0, tiled=True)  38.9 us
    pallas_call x3, Pallas kernels, attend_backward(): pl.pallas_call(functools.partial(backward_kernel, rows, group, first, las...  10 us
    all_to_all x1, starting transfers between devices, per_device(): lax.all_to_all(pack(queries, keys, values, proj_weight, seq), 'seq', spli...  8.6 us
    ppermute x3, starting transfers between devices, per_device(): from_right.append(lax.ppermute(from_right[-1], 'seq', left))  7.77 us
    all_to_all x1, starting transfers between devices, per_device(): lax.all_to_all(copies, 'dp', split_axis=0, concat_axis=0, tiled=True)  7.48 us
    all_to_all x1, starting transfers between devices, per_device(): parts = lax.all_to_all(parts, 'dp', split_axis=0, concat_axis=0, tiled=True)  7.36 us
    pallas_call x1, Pallas kernels, attend_forward(): pl.pallas_call(functools.partial(forward_kernel, rows), grid=(slots // PA...  6.9 us
  transfers between devices with their start and end apart: 17, of which 4 were waited for; matrix products, arithmetic and copies ran while one was open for 4% of the time, Pallas kernels for 15%

profile of v2, /device:TPU:2, one launch (start us, length us, event | category | flops | bytes accessed | tf_op | source)
XLA Modules:
  0.0 182.1 jit_solution(11410986975580745257)
XLA Ops:
  0.6 1.0 copy-done.11
  1.6 1.0 copy-done.12
  2.6 1.0 copy-done.13
  3.6 0.8 copy-done.14
  4.4 3.0 %shard_map.102 = bf16[8,608,128]{2,1,0:T(8,128)(2,1)} custom-call(bf16[192,1024]{1,0:T(8,128)(2,1)S(1)} %copy-done.11, bf16[192,1024]{1,0:T(8,128)(2,1)S(1)} %copy-done.12, bf16[192,1024]{1,0:T(8,128)(2,1)S(1)} %copy-done.13, bf16[24,1024]{1,0:T(8,128)(2,1)S(1)} %copy-done.14), custom_call_target="tpu_custom_call" | custom-call | bytes 2490368 | tf_op jit(solution)/shard_map/pallas_call | solution.py:77
  7.4 8.6 %all-to-all-start = ((bf16[8,608,128]{2,1,0:T(8,128)(2,1)}), bf16[8,608,128]{2,1,0:T(8,128)(2,1)S(1)}, u32[]{:S(2)}, u32[]{:S(2)}) async-start(bf16[8,608,128]{2,1,0:T(8,128)(2,1)} %shard_map.102), calls=%async_computation | async-start | bytes 2490368 | tf_op jit(solution)/shard_map/all_to_all | solution.py:333
  16.7 0.1 shard_map.104.refs_0_.refs_6_
  16.8 2.1 %collective-permute-start = (bf16[192,1536]{1,0:T(8,128)(2,1)S(1)}, bf16[192,1536]{1,0:T(8,128)(2,1)S(1)}, u32[]{:S(2)}, u32[]{:S(2)}) collective-permute-start(bf16[192,1536]{1,0:T(8,128)(2,1)S(1)} %shard_map.104.refs_0_.refs_6_), channel_id=1, source_target_pairs={{0,2},{2,4},{4,6},{6,8},{8,10},{10,12},{12,14},{14,0},{1,3},{3,5},... | collective-permute-start | bytes 1769480 | tf_op jit(solution)/shard_map/ppermute | solution.py:325
  18.9 1.3 collective-permute-start.4
  20.2 38.6 %collective-permute-done.refs_0_ = bf16[192,1536]{1,0:T(8,128)(2,1)S(1)} collective-permute-done((bf16[192,1536]{1,0:T(8,128)(2,1)S(1)}, bf16[192,1536]{1,0:T(8,128)(2,1)S(1)}, u32[]{:S(2)}, u32[]{:S(2)}) %collective-permute-start) | collective-permute-done | bytes 589856 | tf_op jit(solution)/shard_map/ppermute | solution.py:325
  58.9 3.2 %collective-permute-start.5 = (bf16[192,1536]{1,0:T(8,128)(2,1)S(1)}, bf16[192,1536]{1,0:T(8,128)(2,1)}, u32[]{:S(2)}, u32[]{:S(2)}) collective-permute-start(bf16[192,1536]{1,0:T(8,128)(2,1)S(1)} %collective-permute-done.4.refs_1_), channel_id=1, source_target_pairs={{0,14},{2,0},{4,2},{6,4},{8,6},{10,8},{12,10},{14,12},{1,15},{3,1}... | collective-permute-start | bytes 1769480 | tf_op jit(solution)/shard_map/ppermute | solution.py:326
  62.1 0.8 copy-done.5
  62.9 11.6 %collective-permute-done.1.refs_2_ = bf16[192,1536]{1,0:T(8,128)(2,1)} collective-permute-done((bf16[192,1536]{1,0:T(8,128)(2,1)S(1)}, bf16[192,1536]{1,0:T(8,128)(2,1)}, u32[]{:S(2)}, u32[]{:S(2)}) %collective-permute-start.1) | collective-permute-done | bytes 589856 | tf_op jit(solution)/shard_map/ppermute | solution.py:325
  74.5 0.0 collective-permute-done.5.refs_3_
  74.5 3.2 %collective-permute-start.6 = (bf16[192,1536]{1,0:T(8,128)(2,1)}, bf16[192,1536]{1,0:T(8,128)(2,1)}, u32[]{:S(2)}, u32[]{:S(2)}) collective-permute-start(bf16[192,1536]{1,0:T(8,128)(2,1)} %collective-permute-done.5.refs_3_), channel_id=1, source_target_pairs={{0,14},{2,0},{4,2},{6,4},{8,6},{10,8},{12,10},{14,12},{1,15},{3,1}... | collective-permute-start | bytes 1769480 | tf_op jit(solution)/shard_map/ppermute | solution.py:326
  77.7 0.0 all-to-all-done.packed_ref.refs_0_
  77.8 1.0 broadcast_in_dim.11
  78.8 7.5 %all-to-all-start.1 = ((bf16[16,192,128]{2,1,0:T(8,128)(2,1)}), bf16[16,192,128]{2,1,0:T(8,128)(2,1)}, u32[]{:S(2)}, u32[]{:S(2)}) async-start(bf16[16,192,128]{2,1,0:T(8,128)(2,1)} %broadcast_in_dim.11), calls=%async_computation.1 | async-start | bytes 1572864 | tf_op jit(solution)/shard_map/all_to_all | solution.py:338
  86.3 6.9 %shard_map.103 = (bf16[1536,1536]{1,0:T(8,128)(2,1)}, f32[1,1536]{1,0:T(1,128)S(1)}, f32[128,1536]{1,0:T(8,128)S(1)}, bf16[128,1536]{1,0:T(8,128)(2,1)S(1)}) custom-call(s32[1]{0:T(128)S(6)} %copy.11.length_ref, bf16[8,608,128]{2,1,0:T(8,128)(2,1)S(1)} %all-to-all-done.packed_ref.refs_0_), custom_call_target="tpu_custom_call" | custom-call | flops 1207959552 | bytes 4718592 | tf_op jit(solution)/shard_map/pallas_call | solution.py:150
  93.2 0.0 collective-permute-start.12
  93.2 0.1 collective-permute-start.3
  93.3 0.0 collective-permute-done.6.refs_1_.refs_5_
  93.4 1.1 slice.13
  94.4 3.2 %collective-permute-start.7 = (bf16[96,1536]{1,0:T(8,128)(2,1)S(1)}, bf16[96,1536]{1,0:T(8,128)(2,1)S(1)}, u32[]{:S(2)}, u32[]{:S(2)}) collective-permute-start(bf16[96,1536]{1,0:T(8,128)(2,1)S(1)} %slice.13), channel_id=1, source_target_pairs={{0,14},{2,0},{4,2},{6,4},{8,6},{10,8},{12,10},{14,12},{1,15},{3,1}... | collective-permute-start | bytes 884744 | tf_op jit(solution)/shard_map/ppermute | solution.py:329
  97.6 6.3 %collective-permute-done.3.refs_1_.refs_7_ = bf16[96,1536]{1,0:T(8,128)(2,1)S(1)} collective-permute-done((bf16[96,1536]{1,0:T(8,128)(2,1)S(1)}, bf16[96,1536]{1,0:T(8,128)(2,1)S(1)}, u32[]{:S(2)}, u32[]{:S(2)}) %collective-permute-start.3) | collective-permute-done | bytes 294944 | tf_op jit(solution)/shard_map/ppermute | solution.py:328
  103.9 0.3 collective-permute-done.7.refs_2_.refs_8_
  104.3 5.9 %shard_map.111 = (bf16[1536,128]{1,0:T(8,128)(2,1)S(1)}, bf16[1536,128]{1,0:T(8,128)(2,1)}) custom-call(bf16[128,1536]{1,0:T(8,128)(2,1)S(1)} %get-tuple-element.37.own_t_ref, bf16[128,1536]{1,0:T(8,128)(2,1)S(1)} %collective-permute-done.12.other_t_ref, bf16[192,1536]{1,0:T(8,128)(2,1)S(1)} %copy-done.3, bf16[192,1536]{1,0:T(8,128)(2,1)S(1)} %copy-done.6, ...), custom_call_target="tpu_custom_call" | custom-call | flops 1207959552 | bytes 4718592 | tf_op jit(solution)/shard_map/pallas_call | solution.py:209
  110.2 2.0 %constant_dynamic-slice_fusion.1 = (bf16[1536,128]{1,0:T(8,128)(2,1)}, bf16[1536,128]{1,0:T(8,128)(2,1)}) fusion(bf16[3072,128]{1,0:T(8,128)(2,1)} %bitcast.1, s32[]{:T(128)S(6)} %select_n.18, s32[]{:T(128)S(6)} %select_n.19), kind=kLoop, calls=%fused_computation.6 | loop fusion | bytes 1572872 | tf_op jit(solution)/shard_map/dynamic_slice | solution.py:339
  112.3 0.5 collective-permute-start.8
  112.8 1.1 broadcast_select_fusion.1
  113.8 0.9 pad_maximum_fusion.1
  114.8 7.4 %all-to-all-start.2 = ((bf16[16,192,128]{2,1,0:T(8,128)(2,1)}), bf16[16,192,128]{2,1,0:T(8,128)(2,1)}, u32[]{:S(2)}, u32[]{:S(2)}) async-start(bf16[16,192,128]{2,1,0:T(8,128)(2,1)} %bitcast.4), calls=%async_computation.2 | async-start | bytes 1572864 | tf_op jit(solution)/shard_map/all_to_all | solution.py:360
  122.1 1.3 pad_maximum_fusion.refs_3_.refs_2_.refs_4_
  123.4 0.0 copy-done.7
  123.4 2.1 %shard_map.107 = (f32[768,128]{1,0:T(8,128)S(1)}, bf16[768,128]{1,0:T(8,128)(2,1)S(1)}) custom-call(bf16[192,1536]{1,0:T(8,128)(2,1)S(1)} %copy-done.4, bf16[192,1536]{1,0:T(8,128)(2,1)S(1)} %copy-done.7, bf16[192,1536]{1,0:T(8,128)(2,1)} %collective-permute-done.1.refs_2_, bf16[192,1536]{1,0:T(8,128)(2,1)} %collective-permute-done.5.refs_3_, ...), custom_call_target="tpu_custom_call" | custom-call | flops 603979776 | bytes 2359296 | tf_op jit(solution)/shard_map/pallas_call | solution.py:187
  125.5 0.3 collective-permute-start.11
  125.8 0.1 pad.2.clone
  125.9 0.5 shard_map.105
  126.5 0.6 collective-permute-start.9
  127.0 1.5 shard_map.106
  128.6 0.1 collective-permute-start.10
  128.7 4.5 %shard_map.108 = (bf16[768,128]{1,0:T(8,128)(2,1)S(1)}, f32[1536,128]{1,0:T(8,128)S(1)}, f32[1536,128]{1,0:T(8,128)S(1)}) custom-call(bf16[8,608,128]{2,1,0:T(8,128)(2,1)S(1)} %all-to-all-done.packed_ref.refs_0_, bf16[1536,1536]{1,0:T(8,128)(2,1)} %get-tuple-element.22.refs_1_, f32[1,1536]{1,0:T(1,128)S(1)} %get-tuple-element.23.refs_2_, ...), custom_call_target="tpu_custom_call" | custom-call | flops 1207959552 | bytes 2359296 | tf_op jit(solution)/shard_map/pallas_call | solution.py:292
  133.3 2.7 %shard_map.109 = (bf16[384,128]{1,0:T(8,128)(2,1)S(1)}, f32[1536,128]{1,0:T(8,128)S(1)}, f32[1536,128]{1,0:T(8,128)S(1)}) custom-call(bf16[8,608,128]{2,1,0:T(8,128)(2,1)S(1)} %all-to-all-done.packed_ref.refs_0_, bf16[1536,1536]{1,0:T(8,128)(2,1)} %get-tuple-element.22.refs_1_, f32[1,1536]{1,0:T(1,128)S(1)} %get-tuple-element.23.refs_2_, ...), custom_call_target="tpu_custom_call" | custom-call | flops 603979776 | bytes 1179648 | tf_op jit(solution)/shard_map/pallas_call | solution.py:292
  136.0 2.8 %shard_map.110 = bf16[8,576,128]{2,1,0:T(8,128)(2,1)S(1)} custom-call(bf16[8,608,128]{2,1,0:T(8,128)(2,1)S(1)} %all-to-all-done.packed_ref.refs_0_, bf16[1536,1536]{1,0:T(8,128)(2,1)} %get-tuple-element.22.refs_1_, f32[1,1536]{1,0:T(1,128)S(1)} %get-tuple-element.23.refs_2_, f32[128,1536]{1,0:T(8,128)S(1)} %get-tuple-element.24.refs_3_, ...), custom_call_target="tpu_custom_call" | custom-call | flops 603979776 | bytes 1179648 | tf_op jit(solution)/shard_map/pallas_call | solution.py:292
  138.8 1.2 reduce_sum.12
  140.0 0.3 maximum_maximum_fusion
  140.4 38.9 %all_to_all.20.packed_ref = bf16[8,608,128]{2,1,0:T(8,128)(2,1)S(1)} all-to-all(bf16[8,608,128]{2,1,0:T(8,128)(2,1)S(1)} %maximum_maximum_fusion), channel_id=1, replica_groups=mesh['dp'=16,'seq'=8,'tensor'=2] {'seq'}, dimensions={0} | all-to-all | bytes 2490368 | tf_op jit(solution)/shard_map/all_to_all | solution.py:365
  179.3 2.7 %shard_map.112 = (bf16[192,1024]{1,0:T(8,128)(2,1)}, bf16[192,1024]{1,0:T(8,128)(2,1)}, bf16[192,1024]{1,0:T(8,128)(2,1)}, f32[24,1024]{1,0:T(8,128)}) custom-call(bf16[8,608,128]{2,1,0:T(8,128)(2,1)S(1)} %all_to_all.20.packed_ref), custom_call_target="tpu_custom_call" | custom-call | bytes 2490368 | tf_op jit(solution)/shard_map/pallas_call | solution.py:100
  (42 shorter events, 0.1 us)
Async XLA Ops:
  0.6 1.0 copy-start.11
  1.6 1.0 copy-start.12
  2.6 1.0 copy-start.13
  3.6 0.8 copy-start.14
  7.4 9.3 %copy-start.10 = (bf16[192,1536]{1,0:T(8,128)(2,1)S(1)}, bf16[192,1536]{1,0:T(8,128)(2,1)}, u32[]{:S(2)}) copy-start(bf16[192,1536]{1,0:T(8,128)(2,1)} %grad_ref.1) | copy-start | bytes 1769476
  7.4 9.3 %copy-start.15 = (f32[1,3072]{1,0:T(1,128)S(1)}, f32[1,3072]{1,0:T(1,128)}, u32[]{:S(2)}) copy-start(f32[1,3072]{1,0:T(1,128)} %gate_ref.1) | copy-start | bytes 36868
  7.4 70.3 %all-to-all-start = ((bf16[8,608,128]{2,1,0:T(8,128)(2,1)}), bf16[8,608,128]{2,1,0:T(8,128)(2,1)S(1)}, u32[]{:S(2)}, u32[]{:S(2)}) async-start(bf16[8,608,128]{2,1,0:T(8,128)(2,1)} %shard_map.102), calls=%async_computation | async-start | bytes 2490368 | tf_op jit(solution)/shard_map/all_to_all | solution.py:333
  16.8 76.4 %copy-start = (bf16[192,1536]{1,0:T(8,128)(2,1)}, bf16[192,1536]{1,0:T(8,128)(2,1)S(1)}, u32[]{:S(2)}) copy-start(bf16[192,1536]{1,0:T(8,128)(2,1)S(1)} %shard_map.104.refs_0_.refs_6_) | copy-start | bytes 1769476
  16.8 42.0 %collective-permute-start = (bf16[192,1536]{1,0:T(8,128)(2,1)S(1)}, bf16[192,1536]{1,0:T(8,128)(2,1)S(1)}, u32[]{:S(2)}, u32[]{:S(2)}) collective-permute-start(bf16[192,1536]{1,0:T(8,128)(2,1)S(1)} %shard_map.104.refs_0_.refs_6_), channel_id=1, source_target_pairs={{0,2},{2,4},{4,6},{6,8},{8,10},{10,12},{12,14},{14,0},{1,3},{3,5},... | collective-permute-start | bytes 1769480 | tf_op jit(solution)/shard_map/ppermute | solution.py:325
  18.9 40.0 %collective-permute-start.4 = (bf16[192,1536]{1,0:T(8,128)(2,1)S(1)}, bf16[192,1536]{1,0:T(8,128)(2,1)S(1)}, u32[]{:S(2)}, u32[]{:S(2)}) collective-permute-start(bf16[192,1536]{1,0:T(8,128)(2,1)S(1)} %shard_map.104.refs_0_.refs_6_), channel_id=1, source_target_pairs={{0,14},{2,0},{4,2},{6,4},{8,6},{10,8},{12,10},{14,12},{1,15},{3,1}... | collective-permute-start | bytes 1769480 | tf_op jit(solution)/shard_map/ppermute | solution.py:326
  58.9 19.9 %copy-start.2 = (bf16[192,1536]{1,0:T(8,128)(2,1)}, bf16[192,1536]{1,0:T(8,128)(2,1)S(1)}, u32[]{:S(2)}) copy-start(bf16[192,1536]{1,0:T(8,128)(2,1)S(1)} %collective-permute-done.refs_0_) | copy-start | bytes 1769476
  58.9 15.6 %collective-permute-start.1 = (bf16[192,1536]{1,0:T(8,128)(2,1)S(1)}, bf16[192,1536]{1,0:T(8,128)(2,1)}, u32[]{:S(2)}, u32[]{:S(2)}) collective-permute-start(bf16[192,1536]{1,0:T(8,128)(2,1)S(1)} %collective-permute-done.refs_0_), channel_id=1, source_target_pairs={{0,2},{2,4},{4,6},{6,8},{8,10},{10,12},{12,14},{14,0},{1,3},{3,5},... | collective-permute-start | bytes 1769480 | tf_op jit(solution)/shard_map/ppermute | solution.py:325
  58.9 15.6 %collective-permute-start.5 = (bf16[192,1536]{1,0:T(8,128)(2,1)S(1)}, bf16[192,1536]{1,0:T(8,128)(2,1)}, u32[]{:S(2)}, u32[]{:S(2)}) collective-permute-start(bf16[192,1536]{1,0:T(8,128)(2,1)S(1)} %collective-permute-done.4.refs_1_), channel_id=1, source_target_pairs={{0,14},{2,0},{4,2},{6,4},{8,6},{10,8},{12,10},{14,12},{1,15},{3,1}... | collective-permute-start | bytes 1769480 | tf_op jit(solution)/shard_map/ppermute | solution.py:326
  62.1 0.8 copy-start.5
  74.5 18.7 %collective-permute-start.2 = (bf16[192,1536]{1,0:T(8,128)(2,1)}, bf16[192,1536]{1,0:T(8,128)(2,1)S(1)}, u32[]{:S(2)}, u32[]{:S(2)}) collective-permute-start(bf16[192,1536]{1,0:T(8,128)(2,1)} %collective-permute-done.1.refs_2_), channel_id=1, source_target_pairs={{0,2},{2,4},{4,6},{6,8},{8,10},{10,12},{12,14},{14,0},{1,3},{3,5},... | collective-permute-start | bytes 1769480 | tf_op jit(solution)/shard_map/ppermute | solution.py:325
  74.5 18.8 %collective-permute-start.6 = (bf16[192,1536]{1,0:T(8,128)(2,1)}, bf16[192,1536]{1,0:T(8,128)(2,1)}, u32[]{:S(2)}, u32[]{:S(2)}) collective-permute-start(bf16[192,1536]{1,0:T(8,128)(2,1)} %collective-permute-done.5.refs_3_), channel_id=1, source_target_pairs={{0,14},{2,0},{4,2},{6,4},{8,6},{10,8},{12,10},{14,12},{1,15},{3,1}... | collective-permute-start | bytes 1769480 | tf_op jit(solution)/shard_map/ppermute | solution.py:326
  78.8 31.4 %all-to-all-start.1 = ((bf16[16,192,128]{2,1,0:T(8,128)(2,1)}), bf16[16,192,128]{2,1,0:T(8,128)(2,1)}, u32[]{:S(2)}, u32[]{:S(2)}) async-start(bf16[16,192,128]{2,1,0:T(8,128)(2,1)} %broadcast_in_dim.11), calls=%async_computation.1 | async-start | bytes 1572864 | tf_op jit(solution)/shard_map/all_to_all | solution.py:338
  93.2 11.1 %copy-start.3 = (bf16[192,1536]{1,0:T(8,128)(2,1)S(1)}, bf16[192,1536]{1,0:T(8,128)(2,1)}, u32[]{:S(2)}) copy-start(bf16[192,1536]{1,0:T(8,128)(2,1)} %copy-done.2) | copy-start | bytes 1769476
  93.2 11.1 %copy-start.6 = (bf16[192,1536]{1,0:T(8,128)(2,1)S(1)}, bf16[192,1536]{1,0:T(8,128)(2,1)}, u32[]{:S(2)}) copy-start(bf16[192,1536]{1,0:T(8,128)(2,1)} %copy-done.5) | copy-start | bytes 1769476
  93.2 11.1 %collective-permute-start.12 = (bf16[128,1536]{1,0:T(8,128)(2,1)S(1)}, bf16[128,1536]{1,0:T(8,128)(2,1)S(1)}, u32[]{:S(2)}, u32[]{:S(2)}) collective-permute-start(bf16[128,1536]{1,0:T(8,128)(2,1)S(1)} %get-tuple-element.37.own_t_ref), channel_id=1, source_target_pairs={{0,1},{1,0},{2,3},{3,2},{4,5},{5,4},{6,7},{7,6},{8,9},{9,8},{10,11... | collective-permute-start | bytes 1179656 | tf_op jit(solution)/shard_map/ppermute | solution.py:345
  93.2 10.7 %collective-permute-start.3 = (bf16[96,1536]{1,0:T(8,128)(2,1)S(1)}, bf16[96,1536]{1,0:T(8,128)(2,1)S(1)}, u32[]{:S(2)}, u32[]{:S(2)}) collective-permute-start(bf16[96,1536]{1,0:T(8,128)(2,1)S(1)} %slice.12), channel_id=1, source_target_pairs={{0,2},{2,4},{4,6},{6,8},{8,10},{10,12},{12,14},{14,0},{1,3},{3,5},... | collective-permute-start | bytes 884744 | tf_op jit(solution)/shard_map/ppermute | solution.py:328
  94.4 9.9 %collective-permute-start.7 = (bf16[96,1536]{1,0:T(8,128)(2,1)S(1)}, bf16[96,1536]{1,0:T(8,128)(2,1)S(1)}, u32[]{:S(2)}, u32[]{:S(2)}) collective-permute-start(bf16[96,1536]{1,0:T(8,128)(2,1)S(1)} %slice.13), channel_id=1, source_target_pairs={{0,14},{2,0},{4,2},{6,4},{8,6},{10,8},{12,10},{14,12},{1,15},{3,1}... | collective-permute-start | bytes 884744 | tf_op jit(solution)/shard_map/ppermute | solution.py:329
  104.3 5.9 %copy-start.8 = (bf16[96,1536]{1,0:T(8,128)(2,1)}, bf16[96,1536]{1,0:T(8,128)(2,1)S(1)}, u32[]{:S(2)}) copy-start(bf16[96,1536]{1,0:T(8,128)(2,1)S(1)} %collective-permute-done.7.refs_2_.refs_8_) | copy-start | bytes 884740
  110.2 2.6 %collective-permute-start.13 = (bf16[1536,128]{1,0:T(8,128)(2,1)}, bf16[1536,128]{1,0:T(8,128)(2,1)}, u32[]{:S(2)}, u32[]{:S(2)}) collective-permute-start(bf16[1536,128]{1,0:T(8,128)(2,1)} %get-tuple-element.39), channel_id=1, source_target_pairs={{0,1},{1,0},{2,3},{3,2},{4,5},{5,4},{6,7},{7,6},{8,9},{9,8},{10,11... | collective-permute-start | bytes 1179656 | tf_op jit(solution)/shard_map/ppermute | solution.py:356
  112.3 9.9 %collective-permute-start.8 = (bf16[1536,128]{1,0:T(8,128)(2,1)}, bf16[1536,128]{1,0:T(8,128)(2,1)}, u32[]{:S(2)}, u32[]{:S(2)}) collective-permute-start(bf16[1536,128]{1,0:T(8,128)(2,1)} %get-tuple-element.41), channel_id=1, source_target_pairs={{0,1},{1,0},{2,3},{3,2},{4,5},{5,4},{6,7},{7,6},{8,9},{9,8},{10,11... | collective-permute-start | bytes 1179656 | tf_op jit(solution)/shard_map/ppermute | solution.py:341
  114.8 8.6 %copy-start.4 = (bf16[192,1536]{1,0:T(8,128)(2,1)S(1)}, bf16[192,1536]{1,0:T(8,128)(2,1)}, u32[]{:S(2)}) copy-start(bf16[192,1536]{1,0:T(8,128)(2,1)} %copy-done.2) | copy-start | bytes 1769476
  114.8 24.0 %all-to-all-start.2 = ((bf16[16,192,128]{2,1,0:T(8,128)(2,1)}), bf16[16,192,128]{2,1,0:T(8,128)(2,1)}, u32[]{:S(2)}, u32[]{:S(2)}) async-start(bf16[16,192,128]{2,1,0:T(8,128)(2,1)} %bitcast.4), calls=%async_computation.2 | async-start | bytes 1572864 | tf_op jit(solution)/shard_map/all_to_all | solution.py:360
  122.1 1.3 copy-start.7
  123.4 2.5 %copy-start.1 = (bf16[192,1536]{1,0:T(8,128)(2,1)S(1)}, bf16[192,1536]{1,0:T(8,128)(2,1)}, u32[]{:S(2)}) copy-start(bf16[192,1536]{1,0:T(8,128)(2,1)} %copy-done) | copy-start | bytes 1769476
  123.4 2.5 %copy-start.9 = (bf16[96,1536]{1,0:T(8,128)(2,1)S(1)}, bf16[96,1536]{1,0:T(8,128)(2,1)}, u32[]{:S(2)}) copy-start(bf16[96,1536]{1,0:T(8,128)(2,1)} %copy-done.8) | copy-start | bytes 884740
  125.5 3.1 %collective-permute-start.11 = (bf16[768,128]{1,0:T(8,128)(2,1)S(1)}, bf16[768,128]{1,0:T(8,128)(2,1)S(1)}, u32[]{:S(2)}, u32[]{:S(2)}) collective-permute-start(bf16[768,128]{1,0:T(8,128)(2,1)S(1)} %get-tuple-element.30), channel_id=1, source_target_pairs={{0,1},{1,0},{2,3},{3,2},{4,5},{5,4},{6,7},{7,6},{8,9},{9,8},{10,11... | collective-permute-start | bytes 589832 | tf_op jit(solution)/shard_map/ppermute | solution.py:350
  126.5 9.5 %collective-permute-start.9 = (bf16[384,128]{1,0:T(8,128)(2,1)S(1)}, bf16[384,128]{1,0:T(8,128)(2,1)S(1)}, u32[]{:S(2)}, u32[]{:S(2)}) collective-permute-start(bf16[384,128]{1,0:T(8,128)(2,1)S(1)} %get-tuple-element.26), channel_id=1, source_target_pairs={{0,1},{1,0},{2,3},{3,2},{4,5},{5,4},{6,7},{7,6},{8,9},{9,8},{10,11... | collective-permute-start | bytes 294920 | tf_op jit(solution)/shard_map/ppermute | solution.py:350
  128.6 4.7 %collective-permute-start.10 = (bf16[384,128]{1,0:T(8,128)(2,1)S(1)}, bf16[384,128]{1,0:T(8,128)(2,1)S(1)}, u32[]{:S(2)}, u32[]{:S(2)}) collective-permute-start(bf16[384,128]{1,0:T(8,128)(2,1)S(1)} %get-tuple-element.28), channel_id=1, source_target_pairs={{0,1},{1,0},{2,3},{3,2},{4,5},{5,4},{6,7},{7,6},{8,9},{9,8},{10,11... | collective-permute-start | bytes 294920 | tf_op jit(solution)/shard_map/ppermute | solution.py:350

commit v3 on v2

v3 whole, which is shorter than its diff:
```python
import functools
import math

import jax
import jax.numpy as jnp
from jax import lax
from jax.experimental import pallas as pl
from jax.experimental.pallas import tpu as pltpu
from jax.sharding import PartitionSpec as P

HD = 128
PAIR = 2
FBLOCK = 256
MIB = 1024 * 1024
BF16 = jnp.bfloat16
F32 = jnp.float32
FACTOR = HD**-0.5
FACTOR_LOG2 = HD**-0.5 * math.log2(math.e)
NT = (((1,), (1,)), ((), ()))


def cost(flops, read, exps=0):
    return pl.CostEstimate(flops=int(flops), bytes_accessed=int(read), transcendentals=int(exps))


def params(limit=48):
    return pltpu.CompilerParams(vmem_limit_bytes=limit * MIB)


def whole(array):
    zeros = (0,) * array.ndim
    return pl.BlockSpec(array.shape, lambda *_: zeros)


def smem():
    return pl.BlockSpec(memory_space=pltpu.SMEM)


def scale_kernel(length_ref, grad_ref, gate_ref, out_ref):
    rows, half = grad_ref.shape
    start = pl.multiple_of(lax.axis_index("tensor") * half, HD)
    gate = gate_ref[:, pl.ds(start, half)]
    left = length_ref[0] - lax.axis_index("seq") * rows
    live = lax.broadcasted_iota(jnp.int32, (rows, 1), 0) < left
    out_ref[...] = jnp.where(live, grad_ref[...].astype(F32) * gate, 0.0).astype(BF16)


def scale(out_grad, gate, lengths):
    return pl.pallas_call(
        scale_kernel,
        out_shape=jax.ShapeDtypeStruct(out_grad.shape, BF16),
        in_specs=[smem(), whole(out_grad), whole(gate)],
        out_specs=whole(out_grad),
        compiler_params=params(),
        cost_estimate=cost(0, 4 * out_grad.size),
    )(lengths, out_grad, gate)


def anywhere():
    return pl.BlockSpec(memory_space=pl.ANY)


def corner(array):
    zeros = (0,) * array.ndim
    return pl.BlockSpec((1,) * (array.ndim - 2) + (16, HD), lambda *_: zeros)


def pack_kernel(query_ref, key_ref, value_ref, weight_ref, out_ref, sems):
    rows = query_ref.shape[0]
    slots, height, _ = out_ref.shape
    copies = []
    for slot in range(slots):
        for i, ref in enumerate((query_ref, key_ref, value_ref)):
            source = ref.at[:, slot * HD : (slot + 1) * HD]
            target = out_ref.at[slot, i * rows : (i + 1) * rows, :]
            copies.append(pltpu.make_async_copy(source, target, sems.at[len(copies)]))
    for copy in copies:
        copy.start()
    weight = weight_ref[...].astype(F32)
    spare = height - 3 * rows - weight.shape[0]
    weight = jnp.concatenate([weight, jnp.zeros((spare, weight.shape[1]), F32)], axis=0).astype(BF16)
    for slot in range(slots):
        out_ref[slot, 3 * rows : height, :] = weight[:, slot * HD : (slot + 1) * HD]
    for copy in copies:
        copy.wait()


def pack(queries, keys, values, weight, slots):
    rows = queries.shape[0]
    wrows = weight.shape[0]
    shape = jax.ShapeDtypeStruct((slots, 3 * rows + -(-wrows // 16) * 16, HD), BF16)
    return pl.pallas_call(
        pack_kernel,
        out_shape=shape,
        in_specs=[anywhere(), anywhere(), anywhere(), whole(weight)],
        out_specs=whole(shape),
        scratch_shapes=[pltpu.SemaphoreType.DMA((3 * slots,))],
        compiler_params=params(60),
        cost_estimate=cost(0, 4 * shape.size),
    )(queries, keys, values, weight)


def unpack_kernel(packed_ref, query_ref, key_ref, value_ref, weight_ref, padded, sems):
    rows = query_ref.shape[0]
    slots, height, _ = packed_ref.shape
    wrows = weight_ref.shape[0]
    first = pltpu.make_async_copy(packed_ref.at[:, 3 * rows : height, :], padded, sems.at[0])
    first.start()
    copies = []
    for slot in range(slots):
        for i, ref in enumerate((query_ref, key_ref, value_ref)):
            source = packed_ref.at[slot, i * rows : (i + 1) * rows, :]
            target = ref.at[:, slot * HD : (slot + 1) * HD]
            copies.append(pltpu.make_async_copy(source, target, sems.at[len(copies) + 1]))
    for copy in copies:
        copy.start()
    first.wait()
    for slot in range(slots):
        weight_ref[:, slot * HD : (slot + 1) * HD] = padded[slot].astype(F32)[:wrows]
    for copy in copies:
        copy.wait()


def unpack(packed, rows, wrows):
    slots, height, _ = packed.shape
    token = jax.ShapeDtypeStruct((rows, slots * HD), BF16)
    weight = jax.ShapeDtypeStruct((wrows, slots * HD), F32)
    return pl.pallas_call(
        unpack_kernel,
        out_shape=[token, token, token, weight],
        in_specs=[anywhere()],
        out_specs=[anywhere(), anywhere(), anywhere(), whole(weight)],
        scratch_shapes=[
            pltpu.VMEM((slots, height - 3 * rows, HD), BF16),
            pltpu.SemaphoreType.DMA((3 * slots + 1,)),
        ],
        compiler_params=params(),
        cost_estimate=cost(0, 2 * 2 * slots * height * HD),
    )(packed)


def finish_kernel(grads_ref, parts_ref, out_ref, padded, sem):
    _, wrows, _ = parts_ref.shape
    slots, height, _ = out_ref.shape
    spare = padded.shape[1]
    total = parts_ref[0].astype(F32)
    for i in range(1, parts_ref.shape[0]):
        total += parts_ref[i].astype(F32)
    total = total.reshape(slots, wrows // slots, HD)
    zeros = jnp.zeros((spare - wrows // slots, HD), F32)
    for slot in range(slots):
        padded[slot] = jnp.concatenate([total[slot], zeros], axis=0).astype(BF16)
    copy = pltpu.make_async_copy(padded, out_ref.at[:, height - spare : height, :], sem)
    copy.start()
    copy.wait()


def finish(grads, parts, spare):
    return pl.pallas_call(
        finish_kernel,
        out_shape=jax.ShapeDtypeStruct(grads.shape, grads.dtype),
        in_specs=[anywhere(), whole(parts)],
        out_specs=anywhere(),
        scratch_shapes=[pltpu.VMEM((grads.shape[0], spare, HD), BF16), pltpu.SemaphoreType.DMA(())],
        input_output_aliases={0: 0},
        compiler_params=params(),
        cost_estimate=cost(0, 2 * parts.size),
    )(grads, parts)


def slot_of(number, slots):
    even = number % 2 == 0
    distance = number // 2 + 1
    offset = jnp.where(even, slots - distance, distance)
    offset = jnp.where(number == 6, 0, jnp.where(number == 7, 4, offset))
    return lax.rem(lax.axis_index("seq") + offset, slots)


def forward_kernel(rows, length_ref, packed_ref, _, weights_ref, inverse_ref, out_ref, low_ref, value_t):
    slots = packed_ref.shape[0]
    total = slots * rows
    step = pl.program_id(0)

    @pl.when(step == 0)
    def _():
        value_t[...] = packed_ref[:, 2 * rows : 3 * rows, :].reshape(total, HD).T

    keys = packed_ref[:, rows : 2 * rows, :].reshape(total, HD)
    block = jnp.concatenate(
        [packed_ref[slot_of(PAIR * step + i, slots), 0:rows, :] for i in range(PAIR)], axis=0
    )
    scores = lax.dot_general(keys, block, NT, preferred_element_type=F32)
    live = lax.broadcasted_iota(jnp.int32, (total, 1), 0) < length_ref[0]
    scores = jnp.where(live, scores, -jnp.inf)
    top = jnp.max(scores, axis=0, keepdims=True)
    weights = jnp.exp2((scores - top) * FACTOR_LOG2)
    inverse = 1.0 / jnp.sum(weights, axis=0, keepdims=True)
    inverse_ref[...] = inverse
    weights = weights.astype(BF16)
    weights_ref[...] = weights
    output = jnp.dot(value_t[...], weights, preferred_element_type=F32) * inverse
    out_ref[...] = output
    low_ref[...] = output.astype(BF16)


def attend_forward(packed, lengths, rows, after):
    slots = packed.shape[0]
    total = slots * rows
    width = PAIR * rows
    return pl.pallas_call(
        functools.partial(forward_kernel, rows),
        grid=(slots // PAIR,),
        out_shape=[
            jax.ShapeDtypeStruct((total, total), BF16),
            jax.ShapeDtypeStruct((1, total), F32),
            jax.ShapeDtypeStruct((HD, total), F32),
            jax.ShapeDtypeStruct((HD, total), BF16),
        ],
        in_specs=[smem(), whole(packed), corner(after)],
        out_specs=[
            pl.BlockSpec((total, width), lambda i: (0, i)),
            pl.BlockSpec((1, width), lambda i: (0, i)),
            pl.BlockSpec((HD, width), lambda i: (0, i)),
            pl.BlockSpec((HD, width), lambda i: (0, i)),
        ],
        scratch_shapes=[pltpu.VMEM((HD, total), BF16)],
        compiler_params=params(),
        cost_estimate=cost(4 * total * total * HD, 2 * total * total, total * total),
    )(lengths, packed, after)


def project_kernel(*refs):
    *grads, own_weight_ref, other_weight_ref, _, own_ref, other_ref = refs
    half = grads[0].shape[1]
    core = lax.axis_index("tensor")
    mine = pl.ds(pl.multiple_of(core * half, half), half)
    weight = jnp.concatenate([own_weight_ref[mine, :], other_weight_ref[mine, :]], axis=1)
    start = 0
    for grad in grads:
        product = jnp.dot(grad[...], weight, preferred_element_type=F32)
        stop = start + grad.shape[0]
        own_ref[start:stop, :] = product[:, :HD]
        other_ref[start:stop, :] = product[:, HD:].astype(BF16)
        start = stop


def project(grads, own_weight, other_weight, after):
    total = sum(grad.shape[0] for grad in grads)
    features = grads[0].shape[1]
    shapes = [jax.ShapeDtypeStruct((total, HD), F32), jax.ShapeDtypeStruct((total, HD), BF16)]
    return pl.pallas_call(
        project_kernel,
        grid=(1,),
        out_shape=shapes,
        in_specs=[whole(array) for array in (*grads, own_weight, other_weight)] + [corner(after)],
        out_specs=[whole(shape) for shape in shapes],
        compiler_params=params(),
        cost_estimate=cost(4 * total * features * HD, 2 * total * features),
    )(*grads, own_weight, other_weight, after)


def weight_grad_kernel(group, final, *refs):
    start, stop = group
    own_t_ref, other_t_ref, *refs = refs
    if final:
        *grads, sum_ref, own_ref, other_ref = refs
    else:
        *grads, sum_ref = refs
    outputs = jnp.concatenate([own_t_ref[:, start:stop], other_t_ref[:, start:stop]], axis=0)
    features = grads[0].shape[1]
    for begin in range(0, features, FBLOCK):
        columns = slice(begin, begin + FBLOCK)
        grad = jnp.concatenate([grad[:, columns] for grad in grads], axis=0)
        product = jnp.dot(outputs, grad, preferred_element_type=F32)
        if final:
            product = (product + sum_ref[:, columns]).T.astype(BF16)
            own_ref[columns, :] = product[:, :HD]
            other_ref[columns, :] = product[:, HD:]
        else:
            sum_ref[:, columns] = product


def weight_grad(own_t, other_t, grads, group, before):
    features = grads[0].shape[1]
    final = before is not None
    if final:
        shapes = [jax.ShapeDtypeStruct((features, HD), BF16)] * 2
    else:
        shapes = [jax.ShapeDtypeStruct((2 * HD, features), F32)]
    inputs = [own_t, other_t, *grads] + ([before] if final else [])
    return pl.pallas_call(
        functools.partial(weight_grad_kernel, group, final),
        out_shape=shapes,
        in_specs=[whole(array) for array in inputs],
        out_specs=[whole(shape) for shape in shapes],
        compiler_params=params(),
        cost_estimate=cost(4 * (group[1] - group[0]) * features * HD, 2 * (group[1] - group[0]) * features),
    )(*inputs)


def hold_kernel(*_):
    pass


def hold(arrays, micros):
    return pl.pallas_call(
        hold_kernel,
        out_shape=[jax.ShapeDtypeStruct(array.shape, array.dtype) for array in arrays],
        in_specs=[anywhere()] * len(arrays),
        out_specs=[anywhere()] * len(arrays),
        input_output_aliases={i: i for i in range(len(arrays))},
        cost_estimate=pl.CostEstimate(flops=int(micros * 1e9), bytes_accessed=int(micros * 3e6), transcendentals=0),
    )(*arrays)


def halves_kernel(left_ref, right_ref, first_ref, second_ref):
    half = first_ref.shape[0]
    first_ref[...] = left_ref[:half]
    second_ref[...] = right_ref[half:]


def halves(left, right):
    half, features = left.shape[0] // 2, left.shape[1]
    shape = jax.ShapeDtypeStruct((half, features), BF16)
    return pl.pallas_call(
        halves_kernel,
        out_shape=[shape, shape],
        in_specs=[whole(left), whole(right)],
        out_specs=[whole(shape), whole(shape)],
        compiler_params=params(),
        cost_estimate=cost(0, 4 * left.size),
    )(left, right)


def join_kernel(own_ref, got_ref, _, out_ref):
    core = lax.axis_index("tensor")
    count = out_ref.shape[0] // 2
    out_ref[pl.ds(core * count, count)] = own_ref[...].reshape(count, *out_ref.shape[1:])
    out_ref[pl.ds((1 - core) * count, count)] = got_ref[...].reshape(count, *out_ref.shape[1:])


def join(own, got, slots, after):
    shape = jax.ShapeDtypeStruct((slots, 2 * own.shape[0] // slots, HD), BF16)
    return pl.pallas_call(
        join_kernel,
        grid=(1,),
        out_shape=shape,
        in_specs=[whole(own), whole(got), corner(after)],
        out_specs=whole(shape),
        compiler_params=params(),
        cost_estimate=cost(0, 8 * own.size),
    )(own, got, after)


def backward_kernel(rows, start, first, last, *refs):
    packed_ref, weights_ref, inverse_ref, out_ref, own_ref, got_ref, _, *refs = refs
    slots = packed_ref.shape[0]
    total = slots * rows
    width = PAIR * rows
    step = pl.program_id(0)
    if last:
        *sums, done_ref, result_ref, key_t, query_acc, key_acc, value_acc = refs
    else:
        query_acc, key_acc, value_acc, key_t = refs
    keys = packed_ref[:, rows : 2 * rows, :].reshape(total, HD)

    @pl.when(step == 0)
    def _():
        key_t[...] = keys.T
        key_acc[...] = jnp.zeros_like(key_acc) if first else sums[0][...]
        value_acc[...] = jnp.zeros_like(value_acc) if first else sums[1][...]

    here = pl.ds(pl.multiple_of(step * width, width), width)
    values = packed_ref[:, 2 * rows : 3 * rows, :].reshape(total, HD)
    block = jnp.concatenate(
        [packed_ref[slot_of(start + PAIR * step + i, slots), 0:rows, :] for i in range(PAIR)], axis=0
    )
    grad = (own_ref[...] + got_ref[...].astype(F32)).astype(BF16)
    grad_t = grad.astype(F32).T
    inverse = inverse_ref[...]
    delta = jnp.sum(grad_t * out_ref[...], axis=0, keepdims=True)
    prob_grad = lax.dot_general(values, grad, NT, preferred_element_type=F32)
    weights = weights_ref[...]
    score_grad = (weights.astype(F32) * ((prob_grad - delta) * inverse)).astype(BF16)
    scaled = (grad_t * inverse).T.astype(BF16)
    value_acc[...] += jnp.dot(weights, scaled, preferred_element_type=F32)
    key_acc[...] += jnp.dot(score_grad, block, preferred_element_type=F32)
    query_t = jnp.dot(key_t[...], score_grad, preferred_element_type=F32) * FACTOR
    query_acc[here, :] = query_t.T.astype(BF16)

    if last:

        @pl.when(step == pl.num_programs(0) - 1)
        def _():
            number = 0
            for source in (done_ref, query_acc):
                for place in range(0, source.shape[0], rows):
                    result_ref[slot_of(number, slots), 0:rows, :] = source[place : place + rows, :]
                    number += 1
            result_ref[:, rows : 2 * rows, :] = (
                (key_acc[...] * FACTOR).astype(BF16).reshape(slots, rows, HD)
            )
            result_ref[:, 2 * rows : 3 * rows, :] = (
                value_acc[...].astype(BF16).reshape(slots, rows, HD)
            )


def attend_backward(packed, state, own, got, rows, start, before, after):
    weights, inverse, out = state
    slots = packed.shape[0]
    total = slots * rows
    width = PAIR * rows
    size = own.shape[0]
    first, last = start == 0, start * rows + size == total
    shift = start // PAIR
    sums = [jax.ShapeDtypeStruct((total, HD), F32)] * 2
    if last:
        shapes = [jax.ShapeDtypeStruct(packed.shape, BF16)]
        scratch = [pltpu.VMEM((size, HD), BF16)] + [pltpu.VMEM((total, HD), F32)] * 2
    else:
        shapes = [jax.ShapeDtypeStruct((size, HD), BF16), *sums]
        scratch = []
    return pl.pallas_call(
        functools.partial(backward_kernel, rows, start, first, last),
        grid=(size // width,),
        out_shape=shapes,
        in_specs=[
            whole(packed),
            pl.BlockSpec((total, width), lambda i: (0, i + shift)),
            pl.BlockSpec((1, width), lambda i: (0, i + shift)),
            pl.BlockSpec((HD, width), lambda i: (0, i + shift)),
            pl.BlockSpec((width, HD), lambda i: (i, 0)),
            pl.BlockSpec((width, HD), lambda i: (i, 0)),
            corner(after),
            *[whole(array) for array in before],
        ],
        out_specs=[whole(shape) for shape in shapes],
        scratch_shapes=[pltpu.VMEM((HD, total), BF16), *scratch],
        compiler_params=params(),
        cost_estimate=cost(8 * total * size * HD, 2 * total * size),
    )(packed, weights, inverse, out, own, got, after, *before)


def per_device(queries, keys, values, out_grad, gate, proj_weight, lengths):
    seq, dp = lax.axis_size("seq"), lax.axis_size("dp")
    rows = queries.shape[0]
    wrows = proj_weight.shape[0]
    swap = [(0, 1), (1, 0)]
    right = [(i, (i + 1) % seq) for i in range(seq)]
    left = [(i, (i - 1) % seq) for i in range(seq)]

    own_rows = scale(out_grad, gate, lengths)
    from_left, from_right = [own_rows], [own_rows]
    for i in range(2):
        from_left.append(lax.ppermute(from_left[-1], "seq", right))
        from_right.append(lax.ppermute(from_right[-1], "seq", left))
        if i == 0:
            from_left[1], from_right[1] = hold((from_left[1], from_right[1]), 40)

    packed = lax.all_to_all(
        pack(queries, keys, values, proj_weight, seq), "seq", split_axis=0, concat_axis=0, tiled=True
    )
    weight_rows = packed[:, 3 * rows : 3 * rows + wrows].reshape(1, seq * wrows, HD)
    copies = jnp.broadcast_to(weight_rows, (dp, seq * wrows, HD))
    own_weight = lax.all_to_all(copies, "dp", split_axis=0, concat_axis=0, tiled=True).reshape(-1, HD)
    other_weight = lax.ppermute(own_weight, "tensor", swap)

    *state, low = attend_forward(packed, lengths, rows, copies)
    low_other = lax.ppermute(low, "tensor", swap)

    from_left.append(lax.ppermute(from_left[-1], "seq", right))
    from_right.append(lax.ppermute(from_right[-1], "seq", left))
    far_left, far_right, low = lax.optimization_barrier((from_left[3], from_right[3], low))
    far_left, far_right = halves(far_left, far_right)
    far = [lax.ppermute(far_left, "seq", right), lax.ppermute(far_right, "seq", left)]
    near = [array for i in range(1, 4) for array in (from_left[i], from_right[i])]
    last = [own_rows, *far]
    cut, total = 6 * rows, seq * rows

    own, other = project(near, own_weight, other_weight, far_left)
    got = lax.ppermute(other, "tensor", swap)
    proj_sum = weight_grad(low, low_other, near, (0, cut), None)[0]
    query_rows, *sums = attend_backward(packed, state, own, got, rows, 0, [], proj_sum)

    proj_own, proj_send = weight_grad(low, low_other, last, (cut, total), proj_sum)
    proj_got = lax.ppermute(proj_send, "tensor", swap)
    own, other = project(last, own_weight, other_weight, proj_own)
    got = lax.ppermute(other, "tensor", swap)
    joined = join(proj_own, proj_got, dp, own)
    parts = lax.all_to_all(joined, "dp", split_axis=0, concat_axis=0, tiled=True)

    grads = attend_backward(packed, state, own, got, rows, 6, [*sums, query_rows], joined)[0]
    result = finish(grads, parts, packed.shape[1] - 3 * rows)
    result = lax.all_to_all(result, "seq", split_axis=0, concat_axis=0, tiled=True)
    return tuple(unpack(result, rows, wrows))


def solution(mesh):
    token = P(("dp", "seq"), "tensor")
    return jax.shard_map(
        per_device,
        mesh=mesh,
        in_specs=(token, token, token, token, P("dp", None), token, P("dp")),
        out_specs=(token, token, token, token),
        check_vma=False,
    )
```

time: 184 us -> 161 us (0.88)
  waiting for transfers between devices: 56.9 us -> 40.8 us
  other arithmetic: 4.82 us -> 0 us
  blocking collectives: 38.9 us -> 36.3 us
  local copies, waits for them, and re-layouts: 8.88 us -> 11 us
    ppermute x3, waiting for transfers between devices: 50.2 us -> 9.75 us  [per_device(): from_left.append(lax.ppermute(from_left[-1], 'seq', right))]
    all_to_all x1, waiting for transfers between devices: 0.01 us -> 20.3 us  [per_device(): lax.all_to_all(pack(queries, keys, values, proj_weight, seq), 'seq', spli...]
    ppermute x3, waiting for transfers between devices: 0.01 us -> 7.32 us  [per_device(): from_right.append(lax.ppermute(from_right[-1], 'seq', left))]
    unnamed x32 -> x50, local copies, waits for them, and re-layouts: 4.62 us -> 9.74 us
    ppermute x3, starting transfers between devices: 7.77 us -> 12.4 us  [per_device(): from_right.append(lax.ppermute(from_right[-1], 'seq', left))]
    ppermute x3, waiting for transfers between devices: 6.64 us -> 2.31 us  [the longest x1 2.31 us: per_device(): lax.ppermute(far_left, 'seq', right)]
    all_to_all x1, starting transfers between devices: 8.6 us -> 4.65 us  [per_device(): lax.all_to_all(pack(queries, keys, values, proj_weight, seq), 'seq', spli...]
    all_to_all x1, blocking collectives: 38.9 us -> 36.3 us  [per_device(): lax.all_to_all(result, 'seq', split_axis=0, concat_axis=0, tiled=True)]
  transfers between devices with their start and end apart: 17 -> 16, of which waited for: 4 -> 7; matrix products, arithmetic and copies ran while one was open for 4% -> 1% of each run, Pallas kernels for 15% -> 18%
where the time goes in v3:
time: 161 us; the launch traced here: 160 us
  waiting for transfers between devices  40.8 us (25%)
  starting transfers between devices  36.6 us (23%)
  blocking collectives  36.3 us (23%)
  Pallas kernels  33.2 us (21%)
  local copies, waits for them, and re-layouts  11 us (7%)
  between operations  1.76 us (1%)
    all_to_all x1, blocking collectives, per_device(): lax.all_to_all(result, 'seq', split_axis=0, concat_axis=0, tiled=True)  36.3 us
    all_to_all x1, waiting for transfers between devices, per_device(): lax.all_to_all(pack(queries, keys, values, proj_weight, seq), 'seq', spli...  20.3 us
    ppermute x3, starting transfers between devices, per_device(): from_right.append(lax.ppermute(from_right[-1], 'seq', left))  12.4 us
    ppermute x3, waiting for transfers between devices, per_device(): from_left.append(lax.ppermute(from_left[-1], 'seq', right))  9.75 us
    unnamed x50, local copies, waits for them, and re-layouts  9.74 us
    pallas_call x2, Pallas kernels, attend_backward(): pl.pallas_call(functools.partial(backward_kernel, rows, start, first, las...  9.25 us
    pallas_call x1, Pallas kernels, attend_forward(): pl.pallas_call(functools.partial(forward_kernel, rows), grid=(slots // PA...  7.54 us
    all_to_all x1, starting transfers between devices, per_device(): lax.all_to_all(copies, 'dp', split_axis=0, concat_axis=0, tiled=True)  7.48 us
  transfers between devices with their start and end apart: 16, of which 7 were waited for; matrix products, arithmetic and copies ran while one was open for 1% of the time, Pallas kernels for 18%

profile of v3, /device:TPU:2, one launch (start us, length us, event | category | flops | bytes accessed | tf_op | source)
XLA Modules:
  0.0 159.6 jit_solution(3129236328444259666)
XLA Ops:
  1.3 1.1 copy-done.21
  2.3 0.7 copy-done.24
  3.1 0.1 shard_map.104.refs_2_.refs_0_
  3.2 5.9 %collective-permute-start.1 = (bf16[192,1536]{1,0:T(8,128)(2,1)S(1)}, bf16[192,1536]{1,0:T(8,128)(2,1)S(1)}, u32[]{:S(2)}, u32[]{:S(2)}) collective-permute-start(bf16[192,1536]{1,0:T(8,128)(2,1)S(1)} %shard_map.104.refs_2_.refs_0_), channel_id=1, source_target_pairs={{0,14},{2,0},{4,2},{6,4},{8,6},{10,8},{12,10},{14,12},{1,15},{3,1}... | collective-permute-start | bytes 1769480 | tf_op jit(solution)/shard_map/ppermute | solution.py:456
  9.1 0.0 collective-permute-start
  9.1 3.4 %shard_map.102 = bf16[8,608,128]{2,1,0:T(8,128)(2,1)} custom-call(bf16[192,1024]{1,0:T(8,128)(2,1)} %query_ref.1, bf16[192,1024]{1,0:T(8,128)(2,1)} %key_ref.1, bf16[192,1024]{1,0:T(8,128)(2,1)} %value_ref.1, bf16[24,1024]{1,0:T(8,128)(2,1)} %weight_ref.1), custom_call_target="tpu_custom_call" | custom-call | bytes 2490368 | tf_op jit(solution)/shard_map/pallas_call | solution.py:92
  12.6 4.6 %all-to-all-start = ((bf16[8,608,128]{2,1,0:T(8,128)(2,1)}), bf16[8,608,128]{2,1,0:T(8,128)(2,1)S(1)}, u32[]{:S(2)}, u32[]{:S(2)}) async-start(bf16[8,608,128]{2,1,0:T(8,128)(2,1)} %shard_map.102), calls=%async_computation | async-start | bytes 2490368 | tf_op jit(solution)/shard_map/all_to_all | solution.py:460
  17.2 7.3 %collective-permute-done.1.__1_ = bf16[192,1536]{1,0:T(8,128)(2,1)S(1)} collective-permute-done((bf16[192,1536]{1,0:T(8,128)(2,1)S(1)}, bf16[192,1536]{1,0:T(8,128)(2,1)S(1)}, u32[]{:S(2)}, u32[]{:S(2)}) %collective-permute-start.1) | collective-permute-done | bytes 589856 | tf_op jit(solution)/shard_map/ppermute | solution.py:456
  24.5 4.6 %collective-permute-done.__0_ = bf16[192,1536]{1,0:T(8,128)(2,1)S(1)} collective-permute-done((bf16[192,1536]{1,0:T(8,128)(2,1)S(1)}, bf16[192,1536]{1,0:T(8,128)(2,1)S(1)}, u32[]{:S(2)}, u32[]{:S(2)}) %collective-permute-start) | collective-permute-done | bytes 589856 | tf_op jit(solution)/shard_map/ppermute | solution.py:455
  29.1 0.8 copy-done.16
  29.9 3.2 %collective-permute-start.4 = (bf16[192,1536]{1,0:T(8,128)(2,1)}, bf16[192,1536]{1,0:T(8,128)(2,1)}, u32[]{:S(2)}, u32[]{:S(2)}) collective-permute-start(bf16[192,1536]{1,0:T(8,128)(2,1)} %get-tuple-element.28.refs_3_.refs_1_), channel_id=1, source_target_pairs={{0,14},{2,0},{4,2},{6,4},{8,6},{10,8},{12,10},{14,12},{1,15},{3,1}... | collective-permute-start | bytes 1769480 | tf_op jit(solution)/shard_map/ppermute | solution.py:456
  33.1 20.3 %all-to-all-done.packed_ref.refs_0_ = bf16[8,608,128]{2,1,0:T(8,128)(2,1)S(1)} async-done(((bf16[8,608,128]{2,1,0:T(8,128)(2,1)}), bf16[8,608,128]{2,1,0:T(8,128)(2,1)S(1)}, u32[]{:S(2)}, u32[]{:S(2)}) %all-to-all-start) | async-done | bytes 1245216 | tf_op jit(solution)/shard_map/all_to_all | solution.py:460
  53.5 1.2 broadcast_in_dim.8._
  54.7 7.5 %all-to-all-start.1 = ((bf16[16,192,128]{2,1,0:T(8,128)(2,1)}), bf16[16,192,128]{2,1,0:T(8,128)(2,1)}, u32[]{:S(2)}, u32[]{:S(2)}) async-start(bf16[16,192,128]{2,1,0:T(8,128)(2,1)} %broadcast_in_dim.8._), calls=%async_computation.1 | async-start | bytes 1572864 | tf_op jit(solution)/shard_map/all_to_all | solution.py:465
  62.2 2.3 %collective-permute-done.2.refs_4_.refs_2_ = bf16[192,1536]{1,0:T(8,128)(2,1)S(1)} collective-permute-done((bf16[192,1536]{1,0:T(8,128)(2,1)}, bf16[192,1536]{1,0:T(8,128)(2,1)S(1)}, u32[]{:S(2)}, u32[]{:S(2)}) %collective-permute-start.2) | collective-permute-done | bytes 589856 | tf_op jit(solution)/shard_map/ppermute | solution.py:455
  64.5 0.0 collective-permute-start.3
  64.5 0.0 collective-permute-done.4.refs_5_.refs_3_
  64.5 3.2 %collective-permute-start.5 = (bf16[192,1536]{1,0:T(8,128)(2,1)}, bf16[192,1536]{1,0:T(8,128)(2,1)S(1)}, u32[]{:S(2)}, u32[]{:S(2)}) collective-permute-start(bf16[192,1536]{1,0:T(8,128)(2,1)} %collective-permute-done.4.refs_5_.refs_3_), channel_id=1, source_target_pairs={{0,14},{2,0},{4,2},{6,4},{8,6},{10,8},{12,10},{14,12},{1,15},{3,1}... | collective-permute-start | bytes 1769480 | tf_op jit(solution)/shard_map/ppermute | solution.py:472
  67.7 7.5 %shard_map.103 = (bf16[1536,1536]{1,0:T(8,128)(2,1)}, f32[1,1536]{1,0:T(1,128)S(1)}, f32[128,1536]{1,0:T(8,128)S(1)}, bf16[128,1536]{1,0:T(8,128)(2,1)S(1)}) custom-call(s32[1]{0:T(128)S(6)} %copy.17.length_ref, bf16[8,608,128]{2,1,0:T(8,128)(2,1)S(1)} %all-to-all-done.packed_ref.refs_0_, bf16[16,192,128]{2,1,0:T(8,128)(2,1)} %broadcast_in_dim.8._), custom_call_target="tpu_custom_call" | custom-call | flops 1207959552 | bytes 4718592 | tf_op jit(solution)/shard_map/pallas_call | solution.py:210
  75.3 0.9 copy-done.8
  76.2 0.5 collective-permute-start.8
  76.7 2.9 %collective-permute-done.3.left_ref.refs_6_.refs_4_ = bf16[192,1536]{1,0:T(8,128)(2,1)S(1)} collective-permute-done((bf16[192,1536]{1,0:T(8,128)(2,1)S(1)}, bf16[192,1536]{1,0:T(8,128)(2,1)S(1)}, u32[]{:S(2)}, u32[]{:S(2)}) %collective-permute-start.3) | collective-permute-done | bytes 589856 | tf_op jit(solution)/shard_map/ppermute | solution.py:471
  79.6 0.0 copy-start.22
  79.6 3.2 %collective-permute-start.7 = (bf16[96,1536]{1,0:T(8,128)(2,1)S(1)}, bf16[96,1536]{1,0:T(8,128)(2,1)S(1)}, u32[]{:S(2)}, u32[]{:S(2)}) collective-permute-start(bf16[96,1536]{1,0:T(8,128)(2,1)S(1)} %get-tuple-element.33), channel_id=1, source_target_pairs={{0,14},{2,0},{4,2},{6,4},{8,6},{10,8},{12,10},{14,12},{1,15},{3,1}... | collective-permute-start | bytes 884744 | tf_op jit(solution)/shard_map/ppermute | solution.py:475
  82.9 0.0 collective-permute-done.9.refs_1_
  82.9 1.1 copy-done.3
  84.0 1.1 copy-done.17
  85.0 1.0 copy-done.20
  86.0 2.4 %shard_map.107.refs_5_.refs_6_ = f32[256,1536]{1,0:T(8,128)S(1)} custom-call(bf16[128,1536]{1,0:T(8,128)(2,1)S(1)} %copy-done.20, bf16[128,1536]{1,0:T(8,128)(2,1)} %collective-permute-done.9.refs_1_, bf16[192,1536]{1,0:T(8,128)(2,1)S(1)} %copy-done.17, bf16[192,1536]{1,0:T(8,128)(2,1)S(1)} %copy-done.14, bf16[192,1536]{1,0:T(8,128)(2,1)S(1)} %copy-done.11, ...), custom_call_target="tpu_custom_call" | custom-call | flops 905969664 | bytes 3538944 | tf_op jit(solution)/shard_map/pallas_call | solution.py:291
  88.5 0.0 collective-permute-done.7.refs_4_.refs_2_
  88.5 2.3 %collective-permute-done.6.refs_3_.refs_1_ = bf16[96,1536]{1,0:T(8,128)(2,1)S(1)} collective-permute-done((bf16[96,1536]{1,0:T(8,128)(2,1)S(1)}, bf16[96,1536]{1,0:T(8,128)(2,1)S(1)}, u32[]{:S(2)}, u32[]{:S(2)}) %collective-permute-start.6) | collective-permute-done | bytes 294944 | tf_op jit(solution)/shard_map/ppermute | solution.py:475
  90.8 1.7 %shard_map.108 = (bf16[1536,128]{1,0:T(8,128)(2,1)S(1)}, bf16[1536,128]{1,0:T(8,128)(2,1)S(1)}) custom-call(bf16[128,1536]{1,0:T(8,128)(2,1)S(1)} %copy-done.20, bf16[128,1536]{1,0:T(8,128)(2,1)} %collective-permute-done.9.refs_1_, bf16[192,1536]{1,0:T(8,128)(2,1)S(1)} %copy-done.6, bf16[96,1536]{1,0:T(8,128)(2,1)S(1)} %collective-permute-done.6.refs_3_.refs_1_, ...), custom_call_target="tpu_custom_call" | custom-call | flops 301989888 | bytes 1179648 | tf_op jit(solution)/shard_map/pallas_call | solution.py:291
  92.5 0.3 collective-permute-start.11
  92.8 1.9 %shard_map.109 = (f32[384,128]{1,0:T(8,128)S(1)}, bf16[384,128]{1,0:T(8,128)(2,1)S(1)}) custom-call(bf16[192,1536]{1,0:T(8,128)(2,1)S(1)} %copy-done.6, bf16[96,1536]{1,0:T(8,128)(2,1)S(1)} %collective-permute-done.6.refs_3_.refs_1_, bf16[96,1536]{1,0:T(8,128)(2,1)S(1)} %collective-permute-done.7.refs_4_.refs_2_, bf16[3072,128]{1,0:T(8,128)(2,1)} %bitcast.1.refs_3_.refs_6_, ...), custom_call_target="tpu_custom_call" | custom-call | flops 301989888 | bytes 1179648 | tf_op jit(solution)/shard_map/pallas_call | solution.py:251
  94.8 1.0 shard_map.110.refs_6_
  95.7 7.5 %all-to-all-start.2 = ((bf16[16,192,128]{2,1,0:T(8,128)(2,1)}), bf16[16,192,128]{2,1,0:T(8,128)(2,1)}, u32[]{:S(2)}, u32[]{:S(2)}) async-start(bf16[16,192,128]{2,1,0:T(8,128)(2,1)} %shard_map.110.refs_6_), calls=%async_computation.2 | async-start | bytes 1572864 | tf_op jit(solution)/shard_map/all_to_all | solution.py:490
  103.2 1.1 copy-done.15
  104.3 1.1 copy-done.18
  105.3 1.0 copy-done.23
  106.3 2.7 %shard_map.111 = (f32[1152,128]{1,0:T(8,128)S(1)}, bf16[1152,128]{1,0:T(8,128)(2,1)S(1)}) custom-call(bf16[192,1536]{1,0:T(8,128)(2,1)S(1)} %copy-done.18, bf16[192,1536]{1,0:T(8,128)(2,1)S(1)} %copy-done.15, bf16[192,1536]{1,0:T(8,128)(2,1)S(1)} %copy-done.12, bf16[192,1536]{1,0:T(8,128)(2,1)} %collective-permute-done.4.refs_5_.refs_3_, ...), custom_call_target="tpu_custom_call" | custom-call | flops 905969664 | bytes 3538944 | tf_op jit(solution)/shard_map/pallas_call | solution.py:251
  109.0 0.1 collective-permute-start.12
  109.1 0.5 collective-permute-start.10
  109.6 1.1 collective-permute-done.12.refs_5_
  110.7 6.0 %shard_map.112 = (bf16[1152,128]{1,0:T(8,128)(2,1)S(1)}, f32[1536,128]{1,0:T(8,128)S(1)}, f32[1536,128]{1,0:T(8,128)S(1)}) custom-call(bf16[8,608,128]{2,1,0:T(8,128)(2,1)S(1)} %all-to-all-done.packed_ref.refs_0_, bf16[1536,1536]{1,0:T(8,128)(2,1)} %get-tuple-element.24.refs_1_, f32[1,1536]{1,0:T(1,128)S(1)} %get-tuple-element.25.refs_2_, ...), custom_call_target="tpu_custom_call" | custom-call | flops 1811939328 | bytes 3538944 | tf_op jit(solution)/shard_map/pallas_call | solution.py:423
  116.8 3.2 %shard_map.113.grads_ref = bf16[8,608,128]{2,1,0:T(8,128)(2,1)S(1)} custom-call(bf16[8,608,128]{2,1,0:T(8,128)(2,1)} %copy-done.1, bf16[1536,1536]{1,0:T(8,128)(2,1)} %get-tuple-element.24.refs_1_, f32[1,1536]{1,0:T(1,128)S(1)} %get-tuple-element.25.refs_2_, f32[128,1536]{1,0:T(8,128)S(1)} %copy-done.9, f32[384,128]{1,0:T(8,128)S(1)} %get-tuple-element.36._.refs_4_, ...), custom_call_target="tpu_custom_call" | custom-call | flops 603979776 | bytes 1179648 | tf_op jit(solution)/shard_map/pallas_call | solution.py:423
  120.0 1.3 shard_map.114
  121.3 36.3 %all_to_all.20.packed_ref = bf16[8,608,128]{2,1,0:T(8,128)(2,1)S(1)} all-to-all(bf16[8,608,128]{2,1,0:T(8,128)(2,1)S(1)} %shard_map.114), channel_id=1, replica_groups=mesh['dp'=16,'seq'=8,'tensor'=2] {'seq'}, dimensions={0} | all-to-all | bytes 2490368 | tf_op jit(solution)/shard_map/all_to_all | solution.py:494
  157.6 1.9 %shard_map.115 = (bf16[192,1024]{1,0:T(8,128)(2,1)}, bf16[192,1024]{1,0:T(8,128)(2,1)}, bf16[192,1024]{1,0:T(8,128)(2,1)}, f32[24,1024]{1,0:T(8,128)}) custom-call(bf16[8,608,128]{2,1,0:T(8,128)(2,1)S(1)} %all_to_all.20.packed_ref), custom_call_target="tpu_custom_call" | custom-call | bytes 2490368 | tf_op jit(solution)/shard_map/pallas_call | solution.py:128
  (51 shorter events, 0.1 us)
Async XLA Ops:
  1.3 1.1 copy-start.21
  2.3 0.7 copy-start.24
  3.2 9.3 %copy-start.5 = (bf16[192,1536]{1,0:T(8,128)(2,1)}, bf16[192,1536]{1,0:T(8,128)(2,1)S(1)}, u32[]{:S(2)}) copy-start(bf16[192,1536]{1,0:T(8,128)(2,1)S(1)} %shard_map.104.refs_2_.refs_0_) | copy-start | bytes 1769476
  3.2 21.3 %collective-permute-start.1 = (bf16[192,1536]{1,0:T(8,128)(2,1)S(1)}, bf16[192,1536]{1,0:T(8,128)(2,1)S(1)}, u32[]{:S(2)}, u32[]{:S(2)}) collective-permute-start(bf16[192,1536]{1,0:T(8,128)(2,1)S(1)} %shard_map.104.refs_2_.refs_0_), channel_id=1, source_target_pairs={{0,14},{2,0},{4,2},{6,4},{8,6},{10,8},{12,10},{14,12},{1,15},{3,1}... | collective-permute-start | bytes 1769480 | tf_op jit(solution)/shard_map/ppermute | solution.py:456
  9.1 19.9 %collective-permute-start = (bf16[192,1536]{1,0:T(8,128)(2,1)S(1)}, bf16[192,1536]{1,0:T(8,128)(2,1)S(1)}, u32[]{:S(2)}, u32[]{:S(2)}) collective-permute-start(bf16[192,1536]{1,0:T(8,128)(2,1)S(1)} %shard_map.104.refs_2_.refs_0_), channel_id=1, source_target_pairs={{0,2},{2,4},{4,6},{6,8},{8,10},{10,12},{12,14},{14,0},{1,3},{3,5},... | collective-permute-start | bytes 1769480 | tf_op jit(solution)/shard_map/ppermute | solution.py:455
  12.6 40.9 %all-to-all-start = ((bf16[8,608,128]{2,1,0:T(8,128)(2,1)}), bf16[8,608,128]{2,1,0:T(8,128)(2,1)S(1)}, u32[]{:S(2)}, u32[]{:S(2)}) async-start(bf16[8,608,128]{2,1,0:T(8,128)(2,1)} %shard_map.102), calls=%async_computation | async-start | bytes 2490368 | tf_op jit(solution)/shard_map/all_to_all | solution.py:460
  24.5 4.6 %copy-start.13 = (bf16[192,1536]{1,0:T(8,128)(2,1)}, bf16[192,1536]{1,0:T(8,128)(2,1)S(1)}, u32[]{:S(2)}) copy-start(bf16[192,1536]{1,0:T(8,128)(2,1)S(1)} %collective-permute-done.1.__1_) | copy-start | bytes 1769476
  29.1 0.8 copy-start.16
  29.9 34.6 %collective-permute-start.2 = (bf16[192,1536]{1,0:T(8,128)(2,1)}, bf16[192,1536]{1,0:T(8,128)(2,1)S(1)}, u32[]{:S(2)}, u32[]{:S(2)}) collective-permute-start(bf16[192,1536]{1,0:T(8,128)(2,1)} %get-tuple-element.27.refs_2_.refs_0_), channel_id=1, source_target_pairs={{0,2},{2,4},{4,6},{6,8},{8,10},{10,12},{12,14},{14,0},{1,3},{3,5},... | collective-permute-start | bytes 1769480 | tf_op jit(solution)/shard_map/ppermute | solution.py:455
  29.9 34.6 %collective-permute-start.4 = (bf16[192,1536]{1,0:T(8,128)(2,1)}, bf16[192,1536]{1,0:T(8,128)(2,1)}, u32[]{:S(2)}, u32[]{:S(2)}) collective-permute-start(bf16[192,1536]{1,0:T(8,128)(2,1)} %get-tuple-element.28.refs_3_.refs_1_), channel_id=1, source_target_pairs={{0,14},{2,0},{4,2},{6,4},{8,6},{10,8},{12,10},{14,12},{1,15},{3,1}... | collective-permute-start | bytes 1769480 | tf_op jit(solution)/shard_map/ppermute | solution.py:456
  53.5 57.2 %copy-start.1 = (bf16[8,608,128]{2,1,0:T(8,128)(2,1)}, bf16[8,608,128]{2,1,0:T(8,128)(2,1)S(1)}, u32[]{:S(2)}) copy-start(bf16[8,608,128]{2,1,0:T(8,128)(2,1)S(1)} %all-to-all-done.packed_ref.refs_0_) | copy-start | bytes 3735556
  54.7 21.5 %all-to-all-start.1 = ((bf16[16,192,128]{2,1,0:T(8,128)(2,1)}), bf16[16,192,128]{2,1,0:T(8,128)(2,1)}, u32[]{:S(2)}, u32[]{:S(2)}) async-start(bf16[16,192,128]{2,1,0:T(8,128)(2,1)} %broadcast_in_dim.8._), calls=%async_computation.1 | async-start | bytes 1572864 | tf_op jit(solution)/shard_map/all_to_all | solution.py:465
  64.5 10.8 %copy-start.10 = (bf16[192,1536]{1,0:T(8,128)(2,1)}, bf16[192,1536]{1,0:T(8,128)(2,1)S(1)}, u32[]{:S(2)}) copy-start(bf16[192,1536]{1,0:T(8,128)(2,1)S(1)} %collective-permute-done.2.refs_4_.refs_2_) | copy-start | bytes 1769476
  64.5 15.1 %collective-permute-start.3 = (bf16[192,1536]{1,0:T(8,128)(2,1)S(1)}, bf16[192,1536]{1,0:T(8,128)(2,1)S(1)}, u32[]{:S(2)}, u32[]{:S(2)}) collective-permute-start(bf16[192,1536]{1,0:T(8,128)(2,1)S(1)} %collective-permute-done.2.refs_4_.refs_2_), channel_id=1, source_target_pairs={{0,2},{2,4},{4,6},{6,8},{8,10},{10,12},{12,14},{14,0},{1,3},{3,5},... | collective-permute-start | bytes 1769480 | tf_op jit(solution)/shard_map/ppermute | solution.py:471
  64.5 15.1 %collective-permute-start.5 = (bf16[192,1536]{1,0:T(8,128)(2,1)}, bf16[192,1536]{1,0:T(8,128)(2,1)S(1)}, u32[]{:S(2)}, u32[]{:S(2)}) collective-permute-start(bf16[192,1536]{1,0:T(8,128)(2,1)} %collective-permute-done.4.refs_5_.refs_3_), channel_id=1, source_target_pairs={{0,14},{2,0},{4,2},{6,4},{8,6},{10,8},{12,10},{14,12},{1,15},{3,1}... | collective-permute-start | bytes 1769480 | tf_op jit(solution)/shard_map/ppermute | solution.py:472
  75.3 0.9 copy-start.8
  76.2 6.7 %copy-start.19 = (bf16[128,1536]{1,0:T(8,128)(2,1)}, bf16[128,1536]{1,0:T(8,128)(2,1)S(1)}, u32[]{:S(2)}) copy-start(bf16[128,1536]{1,0:T(8,128)(2,1)S(1)} %get-tuple-element.34.refs_0_) | copy-start | bytes 1179652
  76.2 6.7 %collective-permute-start.9 = (bf16[128,1536]{1,0:T(8,128)(2,1)S(1)}, bf16[128,1536]{1,0:T(8,128)(2,1)}, u32[]{:S(2)}, u32[]{:S(2)}) collective-permute-start(bf16[128,1536]{1,0:T(8,128)(2,1)S(1)} %get-tuple-element.34.refs_0_), channel_id=1, source_target_pairs={{0,1},{1,0},{2,3},{3,2},{4,5},{5,4},{6,7},{7,6},{8,9},{9,8},{10,11... | collective-permute-start | bytes 1179656 | tf_op jit(solution)/shard_map/ppermute | solution.py:469
  76.2 6.7 %copy-start.11 = (bf16[192,1536]{1,0:T(8,128)(2,1)S(1)}, bf16[192,1536]{1,0:T(8,128)(2,1)}, u32[]{:S(2)}) copy-start(bf16[192,1536]{1,0:T(8,128)(2,1)} %copy-done.10) | copy-start | bytes 1769476
  76.2 6.7 %copy-start.14 = (bf16[192,1536]{1,0:T(8,128)(2,1)S(1)}, bf16[192,1536]{1,0:T(8,128)(2,1)}, u32[]{:S(2)}) copy-start(bf16[192,1536]{1,0:T(8,128)(2,1)} %get-tuple-element.28.refs_3_.refs_1_) | copy-start | bytes 1769476
  76.2 16.6 %collective-permute-start.8 = (bf16[3072,128]{1,0:T(8,128)(2,1)}, bf16[3072,128]{1,0:T(8,128)(2,1)S(1)}, u32[]{:S(2)}, u32[]{:S(2)}) collective-permute-start(bf16[3072,128]{1,0:T(8,128)(2,1)} %bitcast.1.refs_3_.refs_6_), channel_id=1, source_target_pairs={{0,1},{1,0},{2,3},{3,2},{4,5},{5,4},{6,7},{7,6},{8,9},{9,8},{10,11... | collective-permute-start | bytes 2359304 | tf_op jit(solution)/shard_map/ppermute | solution.py:466
  79.6 3.3 %copy-start.2 = (bf16[192,1536]{1,0:T(8,128)(2,1)}, bf16[192,1536]{1,0:T(8,128)(2,1)S(1)}, u32[]{:S(2)}) copy-start(bf16[192,1536]{1,0:T(8,128)(2,1)S(1)} %collective-permute-done.5.right_ref.refs_7_.refs_5_) | copy-start | bytes 1769476
  79.6 8.9 %copy-start.22 = (bf16[96,1536]{1,0:T(8,128)(2,1)}, bf16[96,1536]{1,0:T(8,128)(2,1)S(1)}, u32[]{:S(2)}) copy-start(bf16[96,1536]{1,0:T(8,128)(2,1)S(1)} %get-tuple-element.32.refs_8_) | copy-start | bytes 884740
  79.6 8.9 %collective-permute-start.7 = (bf16[96,1536]{1,0:T(8,128)(2,1)S(1)}, bf16[96,1536]{1,0:T(8,128)(2,1)S(1)}, u32[]{:S(2)}, u32[]{:S(2)}) collective-permute-start(bf16[96,1536]{1,0:T(8,128)(2,1)S(1)} %get-tuple-element.33), channel_id=1, source_target_pairs={{0,14},{2,0},{4,2},{6,4},{8,6},{10,8},{12,10},{14,12},{1,15},{3,1}... | collective-permute-start | bytes 884744 | tf_op jit(solution)/shard_map/ppermute | solution.py:475
  82.9 7.9 %collective-permute-start.6 = (bf16[96,1536]{1,0:T(8,128)(2,1)S(1)}, bf16[96,1536]{1,0:T(8,128)(2,1)S(1)}, u32[]{:S(2)}, u32[]{:S(2)}) collective-permute-start(bf16[96,1536]{1,0:T(8,128)(2,1)S(1)} %get-tuple-element.32.refs_8_), channel_id=1, source_target_pairs={{0,2},{2,4},{4,6},{6,8},{8,10},{10,12},{12,14},{14,0},{1,3},{3,5},... | collective-permute-start | bytes 884744 | tf_op jit(solution)/shard_map/ppermute | solution.py:475
  82.9 1.1 copy-start.3
  84.0 1.1 copy-start.17
  85.0 1.0 copy-start.20
  86.0 4.8 %copy-start.6 = (bf16[192,1536]{1,0:T(8,128)(2,1)S(1)}, bf16[192,1536]{1,0:T(8,128)(2,1)}, u32[]{:S(2)}) copy-start(bf16[192,1536]{1,0:T(8,128)(2,1)} %copy-done.5) | copy-start | bytes 1769476
  88.5 4.0 %copy-start = (f32[256,1536]{1,0:T(8,128)}, f32[256,1536]{1,0:T(8,128)S(1)}, u32[]{:S(2)}) copy-start(f32[256,1536]{1,0:T(8,128)S(1)} %shard_map.107.refs_5_.refs_6_) | copy-start | bytes 4718596
  92.5 2.3 %collective-permute-start.11 = (bf16[1536,128]{1,0:T(8,128)(2,1)S(1)}, bf16[1536,128]{1,0:T(8,128)(2,1)S(1)}, u32[]{:S(2)}, u32[]{:S(2)}) collective-permute-start(bf16[1536,128]{1,0:T(8,128)(2,1)S(1)} %get-tuple-element.38), channel_id=1, source_target_pairs={{0,1},{1,0},{2,3},{3,2},{4,5},{5,4},{6,7},{7,6},{8,9},{9,8},{10,11... | collective-permute-start | bytes 1179656 | tf_op jit(solution)/shard_map/ppermute | solution.py:486
  92.8 1.9 %copy-start.7 = (bf16[3072,128]{1,0:T(8,128)(2,1)}, bf16[3072,128]{1,0:T(8,128)(2,1)S(1)}, u32[]{:S(2)}) copy-start(bf16[3072,128]{1,0:T(8,128)(2,1)S(1)} %collective-permute-done.8.refs_4_.refs_7_) | copy-start | bytes 2359300
  94.7 8.5 %copy-start.4 = (bf16[192,1536]{1,0:T(8,128)(2,1)S(1)}, bf16[192,1536]{1,0:T(8,128)(2,1)}, u32[]{:S(2)}) copy-start(bf16[192,1536]{1,0:T(8,128)(2,1)} %copy-done.2) | copy-start | bytes 1769476
  94.7 8.5 %copy-start.12 = (bf16[192,1536]{1,0:T(8,128)(2,1)S(1)}, bf16[192,1536]{1,0:T(8,128)(2,1)}, u32[]{:S(2)}) copy-start(bf16[192,1536]{1,0:T(8,128)(2,1)} %copy-done.10) | copy-start | bytes 1769476
  95.7 24.3 %all-to-all-start.2 = ((bf16[16,192,128]{2,1,0:T(8,128)(2,1)}), bf16[16,192,128]{2,1,0:T(8,128)(2,1)}, u32[]{:S(2)}, u32[]{:S(2)}) async-start(bf16[16,192,128]{2,1,0:T(8,128)(2,1)} %shard_map.110.refs_6_), calls=%async_computation.2 | async-start | bytes 1572864 | tf_op jit(solution)/shard_map/all_to_all | solution.py:490
  103.2 1.1 copy-start.15
  104.3 1.1 copy-start.18
  105.3 1.0 copy-start.23
  106.3 4.4 %copy-start.9 = (f32[128,1536]{1,0:T(8,128)S(1)}, f32[128,1536]{1,0:T(8,128)}, u32[]{:S(2)}) copy-start(f32[128,1536]{1,0:T(8,128)} %copy-done.8) | copy-start | bytes 2359300
  109.0 1.7 %collective-permute-start.12 = (bf16[1152,128]{1,0:T(8,128)(2,1)S(1)}, bf16[1152,128]{1,0:T(8,128)(2,1)S(1)}, u32[]{:S(2)}, u32[]{:S(2)}) collective-permute-start(bf16[1152,128]{1,0:T(8,128)(2,1)S(1)} %get-tuple-element.40), channel_id=1, source_target_pairs={{0,1},{1,0},{2,3},{3,2},{4,5},{5,4},{6,7},{7,6},{8,9},{9,8},{10,11... | collective-permute-start | bytes 884744 | tf_op jit(solution)/shard_map/ppermute | solution.py:481
  109.1 7.6 %collective-permute-start.10 = (bf16[384,128]{1,0:T(8,128)(2,1)S(1)}, bf16[384,128]{1,0:T(8,128)(2,1)S(1)}, u32[]{:S(2)}, u32[]{:S(2)}) collective-permute-start(bf16[384,128]{1,0:T(8,128)(2,1)S(1)} %get-tuple-element.37), channel_id=1, source_target_pairs={{0,1},{1,0},{2,3},{3,2},{4,5},{5,4},{6,7},{7,6},{8,9},{9,8},{10,11... | collective-permute-start | bytes 294920 | tf_op jit(solution)/shard_map/ppermute | solution.py:488

commit v4 on v3

--- a/solution.py
+++ b/solution.py
@@ -9,6 +9,7 @@
 from jax.sharding import PartitionSpec as P
 
 HD = 128
+HOLD1, HOLD2, HOLD3, PACK = 100, 100, 100, 24
 PAIR = 2
 FBLOCK = 256
 MIB = 1024 * 1024
@@ -23,6 +24,10 @@
     return pl.CostEstimate(flops=int(flops), bytes_accessed=int(read), transcendentals=int(exps))
 
 
+def long_cost(micros):
+    return cost(micros * 1e9, micros * 3e6)
+
+
 def params(limit=48):
     return pltpu.CompilerParams(vmem_limit_bytes=limit * MIB)
 
@@ -65,24 +70,17 @@
     return pl.BlockSpec((1,) * (array.ndim - 2) + (16, HD), lambda *_: zeros)
 
 
-def pack_kernel(query_ref, key_ref, value_ref, weight_ref, out_ref, sems):
+def pack_kernel(query_ref, key_ref, value_ref, weight_ref, out_ref):
     rows = query_ref.shape[0]
     slots, height, _ = out_ref.shape
-    copies = []
-    for slot in range(slots):
-        for i, ref in enumerate((query_ref, key_ref, value_ref)):
-            source = ref.at[:, slot * HD : (slot + 1) * HD]
-            target = out_ref.at[slot, i * rows : (i + 1) * rows, :]
-            copies.append(pltpu.make_async_copy(source, target, sems.at[len(copies)]))
-    for copy in copies:
-        copy.start()
     weight = weight_ref[...].astype(F32)
     spare = height - 3 * rows - weight.shape[0]
     weight = jnp.concatenate([weight, jnp.zeros((spare, weight.shape[1]), F32)], axis=0).astype(BF16)
     for slot in range(slots):
-        out_ref[slot, 3 * rows : height, :] = weight[:, slot * HD : (slot + 1) * HD]
-    for copy in copies:
-        copy.wait()
+        columns = slice(slot * HD, (slot + 1) * HD)
+        for i, ref in enumerate((query_ref, key_ref, value_ref)):
+            out_ref[slot, i * rows : (i + 1) * rows, :] = ref[:, columns]
+        out_ref[slot, 3 * rows : height, :] = weight[:, columns]
 
 
 def pack(queries, keys, values, weight, slots):
@@ -92,10 +90,9 @@
     return pl.pallas_call(
         pack_kernel,
         out_shape=shape,
-        in_specs=[anywhere(), anywhere(), anywhere(), whole(weight)],
+        in_specs=[whole(queries), whole(keys), whole(values), whole(weight)],
         out_specs=whole(shape),
-        scratch_shapes=[pltpu.SemaphoreType.DMA((3 * slots,))],
-        compiler_params=params(60),
+        compiler_params=params(PACK),
         cost_estimate=cost(0, 4 * shape.size),
     )(queries, keys, values, weight)
 
@@ -261,7 +258,7 @@
 
 def weight_grad_kernel(group, final, *refs):
     start, stop = group
-    own_t_ref, other_t_ref, *refs = refs
+    own_t_ref, other_t_ref, _, *refs = refs
     if final:
         *grads, sum_ref, own_ref, other_ref = refs
     else:
@@ -280,43 +277,47 @@
             sum_ref[:, columns] = product
 
 
-def weight_grad(own_t, other_t, grads, group, before):
+def weight_grad(own_t, other_t, grads, group, before, after):
     features = grads[0].shape[1]
     final = before is not None
     if final:
         shapes = [jax.ShapeDtypeStruct((features, HD), BF16)] * 2
     else:
         shapes = [jax.ShapeDtypeStruct((2 * HD, features), F32)]
-    inputs = [own_t, other_t, *grads] + ([before] if final else [])
+    inputs = [*grads] + ([before] if final else [])
     return pl.pallas_call(
         functools.partial(weight_grad_kernel, group, final),
+        grid=(1,),
         out_shape=shapes,
-        in_specs=[whole(array) for array in inputs],
+        in_specs=[whole(own_t), whole(other_t), corner(after)] + [whole(array) for array in inputs],
         out_specs=[whole(shape) for shape in shapes],
         compiler_params=params(),
         cost_estimate=cost(4 * (group[1] - group[0]) * features * HD, 2 * (group[1] - group[0]) * features),
-    )(*inputs)
-
-
-def hold_kernel(*_):
-    pass
+    )(own_t, other_t, after, *inputs)
+
+
+def hold_kernel(*refs):
+    count = len(refs) // 2
+    for source, target in zip(refs[:count], refs[count:]):
+        target[...] = source[...]
 
 
 def hold(arrays, micros):
     return pl.pallas_call(
         hold_kernel,
         out_shape=[jax.ShapeDtypeStruct(array.shape, array.dtype) for array in arrays],
-        in_specs=[anywhere()] * len(arrays),
-        out_specs=[anywhere()] * len(arrays),
-        input_output_aliases={i: i for i in range(len(arrays))},
-        cost_estimate=pl.CostEstimate(flops=int(micros * 1e9), bytes_accessed=int(micros * 3e6), transcendentals=0),
+        in_specs=[whole(array) for array in arrays],
+        out_specs=[whole(array) for array in arrays],
+        compiler_params=params(24),
+        cost_estimate=long_cost(micros),
     )(*arrays)
 
 
-def halves_kernel(left_ref, right_ref, first_ref, second_ref):
-    half = first_ref.shape[0]
-    first_ref[...] = left_ref[:half]
-    second_ref[...] = right_ref[half:]
+def halves_kernel(left_ref, right_ref, *part_refs):
+    half = left_ref.shape[0] // 2
+    for ref, parts in ((left_ref, part_refs[:2]), (right_ref, part_refs[2:])):
+        parts[0][...] = ref[:half]
+        parts[1][...] = ref[half:]
 
 
 def halves(left, right):
@@ -324,29 +325,33 @@
     shape = jax.ShapeDtypeStruct((half, features), BF16)
     return pl.pallas_call(
         halves_kernel,
-        out_shape=[shape, shape],
+        out_shape=[shape] * 4,
         in_specs=[whole(left), whole(right)],
-        out_specs=[whole(shape), whole(shape)],
-        compiler_params=params(),
-        cost_estimate=cost(0, 4 * left.size),
+        out_specs=[whole(shape)] * 4,
+        compiler_params=params(),
+        cost_estimate=long_cost(HOLD1),
     )(left, right)
 
 
-def join_kernel(own_ref, got_ref, _, out_ref):
+def join_kernel(own_ref, got_ref, _, out_ref, sems):
     core = lax.axis_index("tensor")
-    count = out_ref.shape[0] // 2
-    out_ref[pl.ds(core * count, count)] = own_ref[...].reshape(count, *out_ref.shape[1:])
-    out_ref[pl.ds((1 - core) * count, count)] = got_ref[...].reshape(count, *out_ref.shape[1:])
-
-
-def join(own, got, slots, after):
-    shape = jax.ShapeDtypeStruct((slots, 2 * own.shape[0] // slots, HD), BF16)
+    rows = own_ref.shape[0]
+    first = pltpu.make_async_copy(own_ref, out_ref.at[pl.ds(core * rows, rows)], sems.at[0])
+    second = pltpu.make_async_copy(got_ref, out_ref.at[pl.ds((1 - core) * rows, rows)], sems.at[1])
+    first.start()
+    second.start()
+    first.wait()
+    second.wait()
+
+
+def join(own, got, after):
     return pl.pallas_call(
         join_kernel,
         grid=(1,),
-        out_shape=shape,
+        out_shape=jax.ShapeDtypeStruct((2 * own.shape[0], HD), BF16),
         in_specs=[whole(own), whole(got), corner(after)],
-        out_specs=whole(shape),
+        out_specs=anywhere(),
+        scratch_shapes=[pltpu.SemaphoreType.DMA((2,))],
         compiler_params=params(),
         cost_estimate=cost(0, 8 * own.size),
     )(own, got, after)
@@ -449,13 +454,19 @@
     right = [(i, (i + 1) % seq) for i in range(seq)]
     left = [(i, (i - 1) % seq) for i in range(seq)]
 
+    def move(array, step):
+        return lax.ppermute(array, "seq", right if step > 0 else left)
+
     own_rows = scale(out_grad, gate, lengths)
-    from_left, from_right = [own_rows], [own_rows]
+    from_left, from_right = move(own_rows, 1), move(own_rows, -1)
+    near = [from_left, from_right]
+    left_top, left_low, right_top, right_low = halves(from_left, from_right)
     for i in range(2):
-        from_left.append(lax.ppermute(from_left[-1], "seq", right))
-        from_right.append(lax.ppermute(from_right[-1], "seq", left))
-        if i == 0:
-            from_left[1], from_right[1] = hold((from_left[1], from_right[1]), 40)
+        left_top, right_low = move(left_top, 1), move(right_low, -1)
+        left_low, right_top = move(left_low, 1), move(right_top, -1)
+        if (HOLD2, HOLD3)[i]:
+            left_top, right_low = hold((left_top, right_low), (HOLD2, HOLD3)[i])
+        near += [left_top, left_low, right_top, right_low]
 
     packed = lax.all_to_all(
         pack(queries, keys, values, proj_weight, seq), "seq", split_axis=0, concat_axis=0, tiled=True
@@ -468,27 +479,23 @@
     *state, low = attend_forward(packed, lengths, rows, copies)
     low_other = lax.ppermute(low, "tensor", swap)
 
-    from_left.append(lax.ppermute(from_left[-1], "seq", right))
-    from_right.append(lax.ppermute(from_right[-1], "seq", left))
-    far_left, far_right, low = lax.optimization_barrier((from_left[3], from_right[3], low))
-    far_left, far_right = halves(far_left, far_right)
-    far = [lax.ppermute(far_left, "seq", right), lax.ppermute(far_right, "seq", left)]
-    near = [array for i in range(1, 4) for array in (from_left[i], from_right[i])]
+    left_top, right_low, low = lax.optimization_barrier((left_top, right_low, low))
+    far = [move(left_top, 1), move(right_low, -1)]
     last = [own_rows, *far]
     cut, total = 6 * rows, seq * rows
 
-    own, other = project(near, own_weight, other_weight, far_left)
-    got = lax.ppermute(other, "tensor", swap)
-    proj_sum = weight_grad(low, low_other, near, (0, cut), None)[0]
-    query_rows, *sums = attend_backward(packed, state, own, got, rows, 0, [], proj_sum)
-
-    proj_own, proj_send = weight_grad(low, low_other, last, (cut, total), proj_sum)
+    proj_sum = weight_grad(low, low_other, near, (0, cut), None, left_top)[0]
+    near_own, other = project(near, own_weight, other_weight, proj_sum)
+    near_got = lax.ppermute(other, "tensor", swap)
+
+    proj_own, proj_send = weight_grad(low, low_other, last, (cut, total), proj_sum, near_own)
     proj_got = lax.ppermute(proj_send, "tensor", swap)
     own, other = project(last, own_weight, other_weight, proj_own)
     got = lax.ppermute(other, "tensor", swap)
-    joined = join(proj_own, proj_got, dp, own)
+    joined = join(proj_own, proj_got, own).reshape(dp, seq * wrows, HD)
     parts = lax.all_to_all(joined, "dp", split_axis=0, concat_axis=0, tiled=True)
 
+    query_rows, *sums = attend_backward(packed, state, near_own, near_got, rows, 0, [], joined)
     grads = attend_backward(packed, state, own, got, rows, 6, [*sums, query_rows], joined)[0]
     result = finish(grads, parts, packed.shape[1] - 3 * rows)
     result = lax.all_to_all(result, "seq", split_axis=0, concat_axis=0, tiled=True)

time: 161 us -> 154 us (0.957)
  waiting for transfers between devices: 40.8 us -> 31.5 us
  starting transfers between devices: 36.6 us -> 44.8 us
  local copies, waits for them, and re-layouts: 11 us -> 8.05 us
  Pallas kernels: 33.2 us -> 31.4 us
    ppermute x8 -> x13, waiting for transfers between devices: 19.4 us -> 8.34 us  [the longest x12 7.06 us: move(): return lax.ppermute(array, 'seq', right if step > 0 else left)]
    ppermute x8 -> x13, starting transfers between devices: 15.7 us -> 23.2 us  [the longest x12 23.2 us: move(): return lax.ppermute(array, 'seq', right if step > 0 else left)]
    unnamed x50 -> x52, local copies, waits for them, and re-layouts: 9.74 us -> 6.85 us
    all_to_all x1, waiting for transfers between devices: 0.01 us -> 2.33 us  [per_device(): lax.all_to_all(joined, 'dp', split_axis=0, concat_axis=0, tiled=True)]
    pallas_call x1 -> x2, Pallas kernels: 0.01 us -> 1.75 us  [hold(): pl.pallas_call(hold_kernel, out_shape=[jax.ShapeDtypeStruct(array.shape,...]
  transfers between devices with their start and end apart: 16 -> 20, of which waited for: 7 -> 5; matrix products, arithmetic and copies ran while one was open for 1% -> 1% of each run, Pallas kernels for 18% -> 17%
where the time goes in v4:
time: 154 us; the launch traced here: 153 us
  starting transfers between devices  44.8 us (29%)
  blocking collectives  35.5 us (23%)
  waiting for transfers between devices  31.5 us (20%)
  Pallas kernels  31.4 us (20%)
  local copies, waits for them, and re-layouts  8.05 us (5%)
  between operations  1.74 us (1%)
    all_to_all x1, blocking collectives, per_device(): lax.all_to_all(result, 'seq', split_axis=0, concat_axis=0, tiled=True)  35.5 us
    ppermute x12, starting transfers between devices, move(): return lax.ppermute(array, 'seq', right if step > 0 else left)  23.2 us
    all_to_all x1, waiting for transfers between devices, per_device(): lax.all_to_all(pack(queries, keys, values, proj_weight, seq), 'seq', spli...  19.7 us
    pallas_call x2, Pallas kernels, attend_backward(): pl.pallas_call(functools.partial(backward_kernel, rows, start, first, las...  9.17 us
    pallas_call x1, Pallas kernels, attend_forward(): pl.pallas_call(functools.partial(forward_kernel, rows), grid=(slots // PA...  7.54 us
    all_to_all x1, starting transfers between devices, per_device(): lax.all_to_all(copies, 'dp', split_axis=0, concat_axis=0, tiled=True)  7.48 us
    all_to_all x1, starting transfers between devices, per_device(): lax.all_to_all(joined, 'dp', split_axis=0, concat_axis=0, tiled=True)  7.24 us
    ppermute x12, waiting for transfers between devices, move(): return lax.ppermute(array, 'seq', right if step > 0 else left)  7.06 us
  transfers between devices with their start and end apart: 20, of which 5 were waited for; matrix products, arithmetic and copies ran while one was open for 1% of the time, Pallas kernels for 17%

profile of v4, /device:TPU:2, one launch (start us, length us, event | category | flops | bytes accessed | tf_op | source)
XLA Modules:
  0.0 153.0 jit_solution(16491479320516729823)
XLA Ops:
  1.3 1.1 copy-done.17
  2.3 0.7 copy-done.22
  3.1 0.1 shard_map.104.refs_3_.refs_0_
  3.2 2.0 %collective-permute-start = (bf16[192,1536]{1,0:T(8,128)(2,1)S(1)}, bf16[192,1536]{1,0:T(8,128)(2,1)S(1)}, u32[]{:S(2)}, u32[]{:S(2)}) collective-permute-start(bf16[192,1536]{1,0:T(8,128)(2,1)S(1)} %shard_map.104.refs_3_.refs_0_), channel_id=1, source_target_pairs={{0,2},{2,4},{4,6},{6,8},{8,10},{10,12},{12,14},{14,0},{1,3},{3,5},... | collective-permute-start | bytes 1769480 | tf_op jit(solution)/shard_map/ppermute | solution.py:458
  5.2 4.0 %collective-permute-start.1 = (bf16[192,1536]{1,0:T(8,128)(2,1)S(1)}, bf16[192,1536]{1,0:T(8,128)(2,1)S(1)}, u32[]{:S(2)}, u32[]{:S(2)}) collective-permute-start(bf16[192,1536]{1,0:T(8,128)(2,1)S(1)} %shard_map.104.refs_3_.refs_0_), channel_id=1, source_target_pairs={{0,14},{2,0},{4,2},{6,4},{8,6},{10,8},{12,10},{14,12},{1,15},{3,1}... | collective-permute-start | bytes 1769480 | tf_op jit(solution)/shard_map/ppermute | solution.py:458
  9.3 0.8 copy-done.21
  10.1 1.3 shard_map.102
  11.3 5.8 %all-to-all-start = ((bf16[8,608,128]{2,1,0:T(8,128)(2,1)}), bf16[8,608,128]{2,1,0:T(8,128)(2,1)S(1)}, u32[]{:S(2)}, u32[]{:S(2)}) async-start(bf16[8,608,128]{2,1,0:T(8,128)(2,1)} %shard_map.102), calls=%async_computation | async-start | bytes 2490368 | tf_op jit(solution)/shard_map/all_to_all | solution.py:471
  17.1 7.0 %collective-permute-done.left_ref.refs_3_.refs_0_ = bf16[192,1536]{1,0:T(8,128)(2,1)S(1)} collective-permute-done((bf16[192,1536]{1,0:T(8,128)(2,1)S(1)}, bf16[192,1536]{1,0:T(8,128)(2,1)S(1)}, u32[]{:S(2)}, u32[]{:S(2)}) %collective-permute-start) | collective-permute-done | bytes 589856 | tf_op jit(solution)/shard_map/ppermute | solution.py:458
  24.1 1.0 shard_map.105
  25.3 0.2 copy-done.7
  25.5 3.8 %collective-permute-start.2 = (bf16[96,1536]{1,0:T(8,128)(2,1)}, bf16[96,1536]{1,0:T(8,128)(2,1)S(1)}, u32[]{:S(2)}, u32[]{:S(2)}) collective-permute-start(bf16[96,1536]{1,0:T(8,128)(2,1)} %get-tuple-element.31), channel_id=1, source_target_pairs={{0,2},{2,4},{4,6},{6,8},{8,10},{10,12},{12,14},{14,0},{1,3},{3,5},... | collective-permute-start | bytes 884744 | tf_op jit(solution)/shard_map/ppermute | solution.py:458
  29.3 0.2 collective-permute-start.3
  29.5 2.7 %collective-permute-start.10 = (bf16[96,1536]{1,0:T(8,128)(2,1)S(1)}, bf16[96,1536]{1,0:T(8,128)(2,1)S(1)}, u32[]{:S(2)}, u32[]{:S(2)}) collective-permute-start(bf16[96,1536]{1,0:T(8,128)(2,1)S(1)} %get-tuple-element.41), channel_id=1, source_target_pairs={{0,2},{2,4},{4,6},{6,8},{8,10},{10,12},{12,14},{14,0},{1,3},{3,5},... | collective-permute-start | bytes 884744 | tf_op jit(solution)/shard_map/ppermute | solution.py:458
  32.2 0.5 collective-permute-start.11
  32.7 19.7 %all-to-all-done.packed_ref.refs_0_ = bf16[8,608,128]{2,1,0:T(8,128)(2,1)S(1)} async-done(((bf16[8,608,128]{2,1,0:T(8,128)(2,1)}), bf16[8,608,128]{2,1,0:T(8,128)(2,1)S(1)}, u32[]{:S(2)}, u32[]{:S(2)}) %all-to-all-start) | async-done | bytes 1245216 | tf_op jit(solution)/shard_map/all_to_all | solution.py:471
  52.4 1.2 broadcast_in_dim.8._
  53.6 7.5 %all-to-all-start.1 = ((bf16[16,192,128]{2,1,0:T(8,128)(2,1)}), bf16[16,192,128]{2,1,0:T(8,128)(2,1)S(1)}, u32[]{:S(2)}, u32[]{:S(2)}) async-start(bf16[16,192,128]{2,1,0:T(8,128)(2,1)} %broadcast_in_dim.8._), calls=%async_computation.1 | async-start | bytes 1572864 | tf_op jit(solution)/shard_map/all_to_all | solution.py:476
  61.1 0.8 shard_map.106
  61.8 2.8 %collective-permute-start.4 = (bf16[96,1536]{1,0:T(8,128)(2,1)S(1)}, bf16[96,1536]{1,0:T(8,128)(2,1)S(1)}, u32[]{:S(2)}, u32[]{:S(2)}) collective-permute-start(bf16[96,1536]{1,0:T(8,128)(2,1)S(1)} %get-tuple-element.33.refs_5_.refs_2_), channel_id=1, source_target_pairs={{0,2},{2,4},{4,6},{6,8},{8,10},{10,12},{12,14},{14,0},{1,3},{3,5},... | collective-permute-start | bytes 884744 | tf_op jit(solution)/shard_map/ppermute | solution.py:458
  64.7 0.4 collective-permute-start.5
  65.1 1.6 %collective-permute-start.12 = (bf16[96,1536]{1,0:T(8,128)(2,1)S(1)}, bf16[96,1536]{1,0:T(8,128)(2,1)}, u32[]{:S(2)}, u32[]{:S(2)}) collective-permute-start(bf16[96,1536]{1,0:T(8,128)(2,1)S(1)} %collective-permute-done.10.refs_6_.refs_3_), channel_id=1, source_target_pairs={{0,2},{2,4},{4,6},{6,8},{8,10},{10,12},{12,14},{14,0},{1,3},{3,5},... | collective-permute-start | bytes 884744 | tf_op jit(solution)/shard_map/ppermute | solution.py:458
  66.7 1.6 %collective-permute-start.13 = (bf16[96,1536]{1,0:T(8,128)(2,1)}, bf16[96,1536]{1,0:T(8,128)(2,1)}, u32[]{:S(2)}, u32[]{:S(2)}) collective-permute-start(bf16[96,1536]{1,0:T(8,128)(2,1)} %collective-permute-done.11.refs_7_.refs_4_), channel_id=1, source_target_pairs={{0,14},{2,0},{4,2},{6,4},{8,6},{10,8},{12,10},{14,12},{1,15},{3,1}... | collective-permute-start | bytes 884744 | tf_op jit(solution)/shard_map/ppermute | solution.py:458
  68.3 7.5 %shard_map.103 = (bf16[1536,1536]{1,0:T(8,128)(2,1)}, f32[1,1536]{1,0:T(1,128)S(1)}, f32[128,1536]{1,0:T(8,128)S(1)}, bf16[128,1536]{1,0:T(8,128)(2,1)S(1)}) custom-call(s32[1]{0:T(128)S(6)} %copy.13.length_ref, bf16[8,608,128]{2,1,0:T(8,128)(2,1)S(1)} %all-to-all-done.packed_ref.refs_0_, bf16[16,192,128]{2,1,0:T(8,128)(2,1)} %broadcast_in_dim.8._), custom_call_target="tpu_custom_call" | custom-call | flops 1207959552 | bytes 4718592 | tf_op jit(solution)/shard_map/pallas_call | solution.py:207
  75.9 0.7 copy-done.24
  76.7 0.5 collective-permute-start.8
  77.2 1.0 copy-done.25
  78.2 1.0 shard_map.107
  79.2 0.7 collective-permute-start.6
  79.8 2.8 %collective-permute-start.7 = (bf16[96,1536]{1,0:T(8,128)(2,1)S(1)}, bf16[96,1536]{1,0:T(8,128)(2,1)S(1)}, u32[]{:S(2)}, u32[]{:S(2)}) collective-permute-start(bf16[96,1536]{1,0:T(8,128)(2,1)S(1)} %get-tuple-element.39.refs_12_.refs_9_), channel_id=1, source_target_pairs={{0,14},{2,0},{4,2},{6,4},{8,6},{10,8},{12,10},{14,12},{1,15},{3,1}... | collective-permute-start | bytes 884744 | tf_op jit(solution)/shard_map/ppermute | solution.py:458
  82.7 2.5 %shard_map.108.refs_12_.refs_6_ = f32[256,1536]{1,0:T(8,128)S(1)} custom-call(bf16[128,1536]{1,0:T(8,128)(2,1)S(1)} %get-tuple-element.40.refs_0_, bf16[128,1536]{1,0:T(8,128)(2,1)} %collective-permute-done.9.refs_1_, bf16[96,1536]{1,0:T(8,128)(2,1)S(1)} %get-tuple-element.38.refs_2_.refs_9_.refs_6_, bf16[192,1536]{1,0:T(8,128)(2,1)S(1)} %copy-done.6, ...), custom_call_target="tpu_custom_call" | custom-call | flops 905969664 | bytes 3538944 | tf_op jit(solution)/shard_map/pallas_call | solution.py:288
  85.3 1.2 copy-done
  86.4 1.0 copy-done.12
  87.5 2.8 %shard_map.109 = (f32[1152,128]{1,0:T(8,128)S(1)}, bf16[1152,128]{1,0:T(8,128)(2,1)S(1)}) custom-call(bf16[192,1536]{1,0:T(8,128)(2,1)S(1)} %copy-done.6, bf16[192,1536]{1,0:T(8,128)(2,1)S(1)} %copy-done.8, bf16[96,1536]{1,0:T(8,128)(2,1)S(1)} %copy-done.14, bf16[96,1536]{1,0:T(8,128)(2,1)S(1)} %copy-done.12, ...), custom_call_target="tpu_custom_call" | custom-call | flops 905969664 | bytes 3538944 | tf_op jit(solution)/shard_map/pallas_call | solution.py:248
  90.3 1.7 %shard_map.110 = (bf16[1536,128]{1,0:T(8,128)(2,1)S(1)}, bf16[1536,128]{1,0:T(8,128)(2,1)S(1)}) custom-call(bf16[128,1536]{1,0:T(8,128)(2,1)S(1)} %copy-done.10, bf16[128,1536]{1,0:T(8,128)(2,1)} %collective-permute-done.9.refs_1_, f32[1152,128]{1,0:T(8,128)S(1)} %get-tuple-element.43.refs_2_.refs_4_, bf16[192,1536]{1,0:T(8,128)(2,1)S(1)} %copy-done.4, ...), custom_call_target="tpu_custom_call" | custom-call | flops 301989888 | bytes 1179648 | tf_op jit(solution)/shard_map/pallas_call | solution.py:288
  92.1 0.1 collective-permute-start.15
  92.2 0.5 shard_map.111
  92.7 1.2 collective-permute-done.15.got_ref
  93.9 0.9 shard_map.112
  94.8 7.2 %all-to-all-start.2 = ((bf16[16,192,128]{2,1,0:T(8,128)(2,1)}), bf16[16,192,128]{2,1,0:T(8,128)(2,1)S(1)}, u32[]{:S(2)}, u32[]{:S(2)}) async-start(bf16[16,192,128]{2,1,0:T(8,128)(2,1)} %bitcast.2.refs_6_), calls=%async_computation.2 | async-start | bytes 1572864 | tf_op jit(solution)/shard_map/all_to_all | solution.py:496
  102.1 0.5 collective-permute-start.14
  102.6 1.3 collective-permute-done.16.refs_5_
  103.9 6.0 %shard_map.113 = (bf16[1152,128]{1,0:T(8,128)(2,1)S(1)}, f32[1536,128]{1,0:T(8,128)S(1)}, f32[1536,128]{1,0:T(8,128)S(1)}) custom-call(bf16[8,608,128]{2,1,0:T(8,128)(2,1)S(1)} %all-to-all-done.packed_ref.refs_0_, bf16[1536,1536]{1,0:T(8,128)(2,1)} %get-tuple-element.28.refs_1_, f32[1,1536]{1,0:T(1,128)S(1)} %get-tuple-element.29.refs_2_, ...), custom_call_target="tpu_custom_call" | custom-call | flops 1811939328 | bytes 3538944 | tf_op jit(solution)/shard_map/pallas_call | solution.py:428
  109.9 3.2 %shard_map.114.grads_ref = bf16[8,608,128]{2,1,0:T(8,128)(2,1)S(1)} custom-call(bf16[8,608,128]{2,1,0:T(8,128)(2,1)} %copy-done.2, bf16[1536,1536]{1,0:T(8,128)(2,1)} %get-tuple-element.28.refs_1_, f32[1,1536]{1,0:T(1,128)S(1)} %get-tuple-element.29.refs_2_, f32[128,1536]{1,0:T(8,128)S(1)} %get-tuple-element.30.refs_3_, f32[384,128]{1,0:T(8,128)S(1)} %copy-done.16, ...), custom_call_target="tpu_custom_call" | custom-call | flops 603979776 | bytes 1179648 | tf_op jit(solution)/shard_map/pallas_call | solution.py:428
  113.1 2.3 %all-to-all-done.2.parts_ref = bf16[16,192,128]{2,1,0:T(8,128)(2,1)S(1)} async-done(((bf16[16,192,128]{2,1,0:T(8,128)(2,1)}), bf16[16,192,128]{2,1,0:T(8,128)(2,1)S(1)}, u32[]{:S(2)}, u32[]{:S(2)}) %all-to-all-start.2) | async-done | bytes 786464 | tf_op jit(solution)/shard_map/all_to_all | solution.py:496
  115.4 0.1 shard_map.115
  115.5 35.5 %all_to_all.20.packed_ref = bf16[8,608,128]{2,1,0:T(8,128)(2,1)S(1)} all-to-all(bf16[8,608,128]{2,1,0:T(8,128)(2,1)S(1)} %shard_map.115), channel_id=1, replica_groups=mesh['dp'=16,'seq'=8,'tensor'=2] {'seq'}, dimensions={0} | all-to-all | bytes 2490368 | tf_op jit(solution)/shard_map/all_to_all | solution.py:501
  151.0 1.9 %shard_map.116 = (bf16[192,1024]{1,0:T(8,128)(2,1)}, bf16[192,1024]{1,0:T(8,128)(2,1)}, bf16[192,1024]{1,0:T(8,128)(2,1)}, f32[24,1024]{1,0:T(8,128)}) custom-call(bf16[8,608,128]{2,1,0:T(8,128)(2,1)S(1)} %all_to_all.20.packed_ref), custom_call_target="tpu_custom_call" | custom-call | bytes 2490368 | tf_op jit(solution)/shard_map/pallas_call | solution.py:125
  (62 shorter events, 0.2 us)
Async XLA Ops:
  1.3 1.1 copy-start.17
  2.3 0.7 copy-start.22
  3.1 6.2 %copy-start.18 = (bf16[192,1024]{1,0:T(8,128)(2,1)S(1)}, bf16[192,1024]{1,0:T(8,128)(2,1)}, u32[]{:S(2)}) copy-start(bf16[192,1024]{1,0:T(8,128)(2,1)} %query_ref.1) | copy-start | bytes 1179652
  3.1 6.2 %copy-start.19 = (bf16[192,1024]{1,0:T(8,128)(2,1)S(1)}, bf16[192,1024]{1,0:T(8,128)(2,1)}, u32[]{:S(2)}) copy-start(bf16[192,1024]{1,0:T(8,128)(2,1)} %key_ref.1) | copy-start | bytes 1179652
  3.1 6.2 %copy-start.20 = (bf16[192,1024]{1,0:T(8,128)(2,1)S(1)}, bf16[192,1024]{1,0:T(8,128)(2,1)}, u32[]{:S(2)}) copy-start(bf16[192,1024]{1,0:T(8,128)(2,1)} %value_ref.1) | copy-start | bytes 1179652
  3.2 8.1 %copy-start.3 = (bf16[192,1536]{1,0:T(8,128)(2,1)}, bf16[192,1536]{1,0:T(8,128)(2,1)S(1)}, u32[]{:S(2)}) copy-start(bf16[192,1536]{1,0:T(8,128)(2,1)S(1)} %shard_map.104.refs_3_.refs_0_) | copy-start | bytes 1769476
  3.2 20.9 %collective-permute-start = (bf16[192,1536]{1,0:T(8,128)(2,1)S(1)}, bf16[192,1536]{1,0:T(8,128)(2,1)S(1)}, u32[]{:S(2)}, u32[]{:S(2)}) collective-permute-start(bf16[192,1536]{1,0:T(8,128)(2,1)S(1)} %shard_map.104.refs_3_.refs_0_), channel_id=1, source_target_pairs={{0,2},{2,4},{4,6},{6,8},{8,10},{10,12},{12,14},{14,0},{1,3},{3,5},... | collective-permute-start | bytes 1769480 | tf_op jit(solution)/shard_map/ppermute | solution.py:458
  5.2 18.9 %collective-permute-start.1 = (bf16[192,1536]{1,0:T(8,128)(2,1)S(1)}, bf16[192,1536]{1,0:T(8,128)(2,1)S(1)}, u32[]{:S(2)}, u32[]{:S(2)}) collective-permute-start(bf16[192,1536]{1,0:T(8,128)(2,1)S(1)} %shard_map.104.refs_3_.refs_0_), channel_id=1, source_target_pairs={{0,14},{2,0},{4,2},{6,4},{8,6},{10,8},{12,10},{14,12},{1,15},{3,1}... | collective-permute-start | bytes 1769480 | tf_op jit(solution)/shard_map/ppermute | solution.py:458
  9.3 0.8 copy-start.21
  11.3 41.0 %all-to-all-start = ((bf16[8,608,128]{2,1,0:T(8,128)(2,1)}), bf16[8,608,128]{2,1,0:T(8,128)(2,1)S(1)}, u32[]{:S(2)}, u32[]{:S(2)}) async-start(bf16[8,608,128]{2,1,0:T(8,128)(2,1)} %shard_map.102), calls=%async_computation | async-start | bytes 2490368 | tf_op jit(solution)/shard_map/all_to_all | solution.py:471
  24.1 1.1 copy-start.5
  24.1 1.4 copy-start.7
  25.5 35.6 %collective-permute-start.2 = (bf16[96,1536]{1,0:T(8,128)(2,1)}, bf16[96,1536]{1,0:T(8,128)(2,1)S(1)}, u32[]{:S(2)}, u32[]{:S(2)}) collective-permute-start(bf16[96,1536]{1,0:T(8,128)(2,1)} %get-tuple-element.31), channel_id=1, source_target_pairs={{0,2},{2,4},{4,6},{6,8},{8,10},{10,12},{12,14},{14,0},{1,3},{3,5},... | collective-permute-start | bytes 884744 | tf_op jit(solution)/shard_map/ppermute | solution.py:458
  29.3 31.8 %collective-permute-start.3 = (bf16[96,1536]{1,0:T(8,128)(2,1)}, bf16[96,1536]{1,0:T(8,128)(2,1)S(1)}, u32[]{:S(2)}, u32[]{:S(2)}) collective-permute-start(bf16[96,1536]{1,0:T(8,128)(2,1)} %get-tuple-element.32), channel_id=1, source_target_pairs={{0,14},{2,0},{4,2},{6,4},{8,6},{10,8},{12,10},{14,12},{1,15},{3,1}... | collective-permute-start | bytes 884744 | tf_op jit(solution)/shard_map/ppermute | solution.py:458
  29.5 35.6 %collective-permute-start.10 = (bf16[96,1536]{1,0:T(8,128)(2,1)S(1)}, bf16[96,1536]{1,0:T(8,128)(2,1)S(1)}, u32[]{:S(2)}, u32[]{:S(2)}) collective-permute-start(bf16[96,1536]{1,0:T(8,128)(2,1)S(1)} %get-tuple-element.41), channel_id=1, source_target_pairs={{0,2},{2,4},{4,6},{6,8},{8,10},{10,12},{12,14},{14,0},{1,3},{3,5},... | collective-permute-start | bytes 884744 | tf_op jit(solution)/shard_map/ppermute | solution.py:458
  32.2 34.5 %collective-permute-start.11 = (bf16[96,1536]{1,0:T(8,128)(2,1)}, bf16[96,1536]{1,0:T(8,128)(2,1)}, u32[]{:S(2)}, u32[]{:S(2)}) collective-permute-start(bf16[96,1536]{1,0:T(8,128)(2,1)} %get-tuple-element.42), channel_id=1, source_target_pairs={{0,14},{2,0},{4,2},{6,4},{8,6},{10,8},{12,10},{14,12},{1,15},{3,1}... | collective-permute-start | bytes 884744 | tf_op jit(solution)/shard_map/ppermute | solution.py:458
  52.4 51.5 %copy-start.2 = (bf16[8,608,128]{2,1,0:T(8,128)(2,1)}, bf16[8,608,128]{2,1,0:T(8,128)(2,1)S(1)}, u32[]{:S(2)}) copy-start(bf16[8,608,128]{2,1,0:T(8,128)(2,1)S(1)} %all-to-all-done.packed_ref.refs_0_) | copy-start | bytes 3735556
  53.6 23.1 %all-to-all-start.1 = ((bf16[16,192,128]{2,1,0:T(8,128)(2,1)}), bf16[16,192,128]{2,1,0:T(8,128)(2,1)S(1)}, u32[]{:S(2)}, u32[]{:S(2)}) async-start(bf16[16,192,128]{2,1,0:T(8,128)(2,1)} %broadcast_in_dim.8._), calls=%async_computation.1 | async-start | bytes 1572864 | tf_op jit(solution)/shard_map/all_to_all | solution.py:476
  61.8 14.0 %copy-start.13 = (bf16[96,1536]{1,0:T(8,128)(2,1)}, bf16[96,1536]{1,0:T(8,128)(2,1)S(1)}, u32[]{:S(2)}) copy-start(bf16[96,1536]{1,0:T(8,128)(2,1)S(1)} %get-tuple-element.33.refs_5_.refs_2_) | copy-start | bytes 884740
  61.8 14.0 %collective-permute-start.4 = (bf16[96,1536]{1,0:T(8,128)(2,1)S(1)}, bf16[96,1536]{1,0:T(8,128)(2,1)S(1)}, u32[]{:S(2)}, u32[]{:S(2)}) collective-permute-start(bf16[96,1536]{1,0:T(8,128)(2,1)S(1)} %get-tuple-element.33.refs_5_.refs_2_), channel_id=1, source_target_pairs={{0,2},{2,4},{4,6},{6,8},{8,10},{10,12},{12,14},{14,0},{1,3},{3,5},... | collective-permute-start | bytes 884744 | tf_op jit(solution)/shard_map/ppermute | solution.py:458
  64.7 12.5 %collective-permute-start.5 = (bf16[96,1536]{1,0:T(8,128)(2,1)}, bf16[96,1536]{1,0:T(8,128)(2,1)}, u32[]{:S(2)}, u32[]{:S(2)}) collective-permute-start(bf16[96,1536]{1,0:T(8,128)(2,1)} %get-tuple-element.34.refs_8_.refs_5_), channel_id=1, source_target_pairs={{0,14},{2,0},{4,2},{6,4},{8,6},{10,8},{12,10},{14,12},{1,15},{3,1}... | collective-permute-start | bytes 884744 | tf_op jit(solution)/shard_map/ppermute | solution.py:458
  65.1 17.6 %copy-start.11 = (bf16[96,1536]{1,0:T(8,128)(2,1)}, bf16[96,1536]{1,0:T(8,128)(2,1)S(1)}, u32[]{:S(2)}) copy-start(bf16[96,1536]{1,0:T(8,128)(2,1)S(1)} %collective-permute-done.10.refs_6_.refs_3_) | copy-start | bytes 884740
  65.1 14.7 %collective-permute-start.12 = (bf16[96,1536]{1,0:T(8,128)(2,1)S(1)}, bf16[96,1536]{1,0:T(8,128)(2,1)}, u32[]{:S(2)}, u32[]{:S(2)}) collective-permute-start(bf16[96,1536]{1,0:T(8,128)(2,1)S(1)} %collective-permute-done.10.refs_6_.refs_3_), channel_id=1, source_target_pairs={{0,2},{2,4},{4,6},{6,8},{8,10},{10,12},{12,14},{14,0},{1,3},{3,5},... | collective-permute-start | bytes 884744 | tf_op jit(solution)/shard_map/ppermute | solution.py:458
  66.7 16.0 %collective-permute-start.13 = (bf16[96,1536]{1,0:T(8,128)(2,1)}, bf16[96,1536]{1,0:T(8,128)(2,1)}, u32[]{:S(2)}, u32[]{:S(2)}) collective-permute-start(bf16[96,1536]{1,0:T(8,128)(2,1)} %collective-permute-done.11.refs_7_.refs_4_), channel_id=1, source_target_pairs={{0,14},{2,0},{4,2},{6,4},{8,6},{10,8},{12,10},{14,12},{1,15},{3,1}... | collective-permute-start | bytes 884744 | tf_op jit(solution)/shard_map/ppermute | solution.py:458
  75.9 6.8 %copy-start.9 = (bf16[128,1536]{1,0:T(8,128)(2,1)}, bf16[128,1536]{1,0:T(8,128)(2,1)S(1)}, u32[]{:S(2)}) copy-start(bf16[128,1536]{1,0:T(8,128)(2,1)S(1)} %get-tuple-element.40.refs_0_) | copy-start | bytes 1179652
  75.9 6.8 %collective-permute-start.9 = (bf16[128,1536]{1,0:T(8,128)(2,1)S(1)}, bf16[128,1536]{1,0:T(8,128)(2,1)}, u32[]{:S(2)}, u32[]{:S(2)}) collective-permute-start(bf16[128,1536]{1,0:T(8,128)(2,1)S(1)} %get-tuple-element.40.refs_0_), channel_id=1, source_target_pairs={{0,1},{1,0},{2,3},{3,2},{4,5},{5,4},{6,7},{7,6},{8,9},{9,8},{10,11... | collective-permute-start | bytes 1179656 | tf_op jit(solution)/shard_map/ppermute | solution.py:480
  75.9 0.8 copy-start.24
  76.7 6.0 %copy-start.6 = (bf16[192,1536]{1,0:T(8,128)(2,1)S(1)}, bf16[192,1536]{1,0:T(8,128)(2,1)}, u32[]{:S(2)}) copy-start(bf16[192,1536]{1,0:T(8,128)(2,1)} %copy-done.5) | copy-start | bytes 1769476
  76.7 6.1 %copy-start.8 = (bf16[192,1536]{1,0:T(8,128)(2,1)S(1)}, bf16[192,1536]{1,0:T(8,128)(2,1)}, u32[]{:S(2)}) copy-start(bf16[192,1536]{1,0:T(8,128)(2,1)} %copy-done.7) | copy-start | bytes 1769476
  76.7 6.1 %copy-start.14 = (bf16[96,1536]{1,0:T(8,128)(2,1)S(1)}, bf16[96,1536]{1,0:T(8,128)(2,1)}, u32[]{:S(2)}) copy-start(bf16[96,1536]{1,0:T(8,128)(2,1)} %copy-done.13) | copy-start | bytes 884740
  76.7 9.8 %collective-permute-start.8 = (bf16[3072,128]{1,0:T(8,128)(2,1)S(1)}, bf16[3072,128]{1,0:T(8,128)(2,1)S(1)}, u32[]{:S(2)}, u32[]{:S(2)}) collective-permute-start(bf16[3072,128]{1,0:T(8,128)(2,1)S(1)} %bitcast.3), channel_id=1, source_target_pairs={{0,1},{1,0},{2,3},{3,2},{4,5},{5,4},{6,7},{7,6},{8,9},{9,8},{10,11... | collective-permute-start | bytes 2359304 | tf_op jit(solution)/shard_map/ppermute | solution.py:477
  77.2 1.0 copy-start.25
  79.2 11.1 %collective-permute-start.6 = (bf16[96,1536]{1,0:T(8,128)(2,1)S(1)}, bf16[96,1536]{1,0:T(8,128)(2,1)S(1)}, u32[]{:S(2)}, u32[]{:S(2)}) collective-permute-start(bf16[96,1536]{1,0:T(8,128)(2,1)S(1)} %get-tuple-element.38.refs_2_.refs_9_.refs_6_), channel_id=1, source_target_pairs={{0,2},{2,4},{4,6},{6,8},{8,10},{10,12},{12,14},{14,0},{1,3},{3,5},... | collective-permute-start | bytes 884744 | tf_op jit(solution)/shard_map/ppermute | solution.py:458
  79.8 10.5 %collective-permute-start.7 = (bf16[96,1536]{1,0:T(8,128)(2,1)S(1)}, bf16[96,1536]{1,0:T(8,128)(2,1)S(1)}, u32[]{:S(2)}, u32[]{:S(2)}) collective-permute-start(bf16[96,1536]{1,0:T(8,128)(2,1)S(1)} %get-tuple-element.39.refs_12_.refs_9_), channel_id=1, source_target_pairs={{0,14},{2,0},{4,2},{6,4},{8,6},{10,8},{12,10},{14,12},{1,15},{3,1}... | collective-permute-start | bytes 884744 | tf_op jit(solution)/shard_map/ppermute | solution.py:458
  85.3 1.2 copy-start
  86.4 3.9 %copy-start.4 = (bf16[192,1536]{1,0:T(8,128)(2,1)S(1)}, bf16[192,1536]{1,0:T(8,128)(2,1)}, u32[]{:S(2)}) copy-start(bf16[192,1536]{1,0:T(8,128)(2,1)} %copy-done.3) | copy-start | bytes 1769476
  86.4 3.9 %copy-start.10 = (bf16[128,1536]{1,0:T(8,128)(2,1)S(1)}, bf16[128,1536]{1,0:T(8,128)(2,1)}, u32[]{:S(2)}) copy-start(bf16[128,1536]{1,0:T(8,128)(2,1)} %copy-done.9) | copy-start | bytes 1179652
  86.4 1.0 copy-start.12
  87.5 2.9 %copy-start.1 = (f32[256,1536]{1,0:T(8,128)S(1)}, f32[256,1536]{1,0:T(8,128)}, u32[]{:S(2)}) copy-start(f32[256,1536]{1,0:T(8,128)} %copy-done) | copy-start | bytes 4718596
  90.3 1.8 %copy-start.23 = (bf16[1152,128]{1,0:T(8,128)(2,1)}, bf16[1152,128]{1,0:T(8,128)(2,1)S(1)}, u32[]{:S(2)}) copy-start(bf16[1152,128]{1,0:T(8,128)(2,1)S(1)} %get-tuple-element.48) | copy-start | bytes 884740
  92.1 1.8 %collective-permute-start.15 = (bf16[1536,128]{1,0:T(8,128)(2,1)S(1)}, bf16[1536,128]{1,0:T(8,128)(2,1)S(1)}, u32[]{:S(2)}, u32[]{:S(2)}) collective-permute-start(bf16[1536,128]{1,0:T(8,128)(2,1)S(1)} %get-tuple-element.47), channel_id=1, source_target_pairs={{0,1},{1,0},{2,3},{3,2},{4,5},{5,4},{6,7},{7,6},{8,9},{9,8},{10,11... | collective-permute-start | bytes 1179656 | tf_op jit(solution)/shard_map/ppermute | solution.py:492
  92.7 2.1 %copy-start.15 = (f32[384,128]{1,0:T(8,128)}, f32[384,128]{1,0:T(8,128)S(1)}, u32[]{:S(2)}) copy-start(f32[384,128]{1,0:T(8,128)S(1)} %get-tuple-element.45._.refs_4_) | copy-start | bytes 589828
  94.8 20.6 %all-to-all-start.2 = ((bf16[16,192,128]{2,1,0:T(8,128)(2,1)}), bf16[16,192,128]{2,1,0:T(8,128)(2,1)S(1)}, u32[]{:S(2)}, u32[]{:S(2)}) async-start(bf16[16,192,128]{2,1,0:T(8,128)(2,1)} %bitcast.2.refs_6_), calls=%async_computation.2 | async-start | bytes 1572864 | tf_op jit(solution)/shard_map/all_to_all | solution.py:496
  102.1 1.8 %collective-permute-start.16 = (bf16[1152,128]{1,0:T(8,128)(2,1)}, bf16[1152,128]{1,0:T(8,128)(2,1)S(1)}, u32[]{:S(2)}, u32[]{:S(2)}) collective-permute-start(bf16[1152,128]{1,0:T(8,128)(2,1)} %copy-done.23), channel_id=1, source_target_pairs={{0,1},{1,0},{2,3},{3,2},{4,5},{5,4},{6,7},{7,6},{8,9},{9,8},{10,11... | collective-permute-start | bytes 884744 | tf_op jit(solution)/shard_map/ppermute | solution.py:489
  102.1 7.8 %collective-permute-start.14 = (bf16[384,128]{1,0:T(8,128)(2,1)S(1)}, bf16[384,128]{1,0:T(8,128)(2,1)S(1)}, u32[]{:S(2)}, u32[]{:S(2)}) collective-permute-start(bf16[384,128]{1,0:T(8,128)(2,1)S(1)} %get-tuple-element.46), channel_id=1, source_target_pairs={{0,1},{1,0},{2,3},{3,2},{4,5},{5,4},{6,7},{7,6},{8,9},{9,8},{10,11... | collective-permute-start | bytes 294920 | tf_op jit(solution)/shard_map/ppermute | solution.py:494
  103.9 6.0 %copy-start.16 = (f32[384,128]{1,0:T(8,128)S(1)}, f32[384,128]{1,0:T(8,128)}, u32[]{:S(2)}) copy-start(f32[384,128]{1,0:T(8,128)} %copy-done.15) | copy-start | bytes 589828

commit v5 on v4

--- a/solution.py
+++ b/solution.py
@@ -173,7 +173,7 @@
     return lax.rem(lax.axis_index("seq") + offset, slots)
 
 
-def forward_kernel(rows, length_ref, packed_ref, _, weights_ref, inverse_ref, out_ref, low_ref, value_t):
+def forward_kernel(rows, length_ref, packed_ref, _, weights_ref, inverse_ref, out_ref, low_ref, value_t, scores_ref):
     slots = packed_ref.shape[0]
     total = slots * rows
     step = pl.program_id(0)
@@ -186,15 +186,24 @@
     block = jnp.concatenate(
         [packed_ref[slot_of(PAIR * step + i, slots), 0:rows, :] for i in range(PAIR)], axis=0
     )
-    scores = lax.dot_general(keys, block, NT, preferred_element_type=F32)
-    live = lax.broadcasted_iota(jnp.int32, (total, 1), 0) < length_ref[0]
-    scores = jnp.where(live, scores, -jnp.inf)
-    top = jnp.max(scores, axis=0, keepdims=True)
-    weights = jnp.exp2((scores - top) * FACTOR_LOG2)
-    inverse = 1.0 / jnp.sum(weights, axis=0, keepdims=True)
+    scores_ref[...] = lax.dot_general(keys, block, NT, preferred_element_type=F32)
+    width = block.shape[0]
+    grain = HD
+    top = jnp.full((8, width), -jnp.inf, F32)
+    for begin in range(0, total, grain):
+        bias = jnp.where(begin < length_ref[0], 0.0, -jnp.inf).astype(F32)
+        part = scores_ref[begin : begin + grain, :] + bias
+        top = jnp.maximum(top, jnp.max(part.reshape(grain // 8, 8, width), axis=0))
+    top = jnp.max(top, axis=0, keepdims=True)
+    norm = jnp.zeros((8, width), F32)
+    for begin in range(0, total, grain):
+        bias = jnp.where(begin < length_ref[0], 0.0, -jnp.inf).astype(F32)
+        part = jnp.exp2((scores_ref[begin : begin + grain, :] + (bias - top)) * FACTOR_LOG2)
+        norm = norm + jnp.sum(part.reshape(grain // 8, 8, width), axis=0)
+        weights_ref[begin : begin + grain, :] = part.astype(BF16)
+    inverse = 1.0 / jnp.sum(norm, axis=0, keepdims=True)
     inverse_ref[...] = inverse
-    weights = weights.astype(BF16)
-    weights_ref[...] = weights
+    weights = weights_ref[...]
     output = jnp.dot(value_t[...], weights, preferred_element_type=F32) * inverse
     out_ref[...] = output
     low_ref[...] = output.astype(BF16)
@@ -220,7 +229,7 @@
             pl.BlockSpec((HD, width), lambda i: (0, i)),
             pl.BlockSpec((HD, width), lambda i: (0, i)),
         ],
-        scratch_shapes=[pltpu.VMEM((HD, total), BF16)],
+        scratch_shapes=[pltpu.VMEM((HD, total), BF16), pltpu.VMEM((total, width), F32)],
         compiler_params=params(),
         cost_estimate=cost(4 * total * total * HD, 2 * total * total, total * total),
     )(lengths, packed, after)
@@ -256,44 +265,29 @@
     )(*grads, own_weight, other_weight, after)
 
 
-def weight_grad_kernel(group, final, *refs):
-    start, stop = group
-    own_t_ref, other_t_ref, _, *refs = refs
-    if final:
-        *grads, sum_ref, own_ref, other_ref = refs
-    else:
-        *grads, sum_ref = refs
-    outputs = jnp.concatenate([own_t_ref[:, start:stop], other_t_ref[:, start:stop]], axis=0)
-    features = grads[0].shape[1]
-    for begin in range(0, features, FBLOCK):
+def weight_grad_kernel(own_t_ref, other_t_ref, _, *refs):
+    *grads, own_ref, other_ref = refs
+    outputs = jnp.concatenate([own_t_ref[...], other_t_ref[...]], axis=0)
+    for begin in range(0, grads[0].shape[1], FBLOCK):
         columns = slice(begin, begin + FBLOCK)
         grad = jnp.concatenate([grad[:, columns] for grad in grads], axis=0)
-        product = jnp.dot(outputs, grad, preferred_element_type=F32)
-        if final:
-            product = (product + sum_ref[:, columns]).T.astype(BF16)
-            own_ref[columns, :] = product[:, :HD]
-            other_ref[columns, :] = product[:, HD:]
-        else:
-            sum_ref[:, columns] = product
-
-
-def weight_grad(own_t, other_t, grads, group, before, after):
-    features = grads[0].shape[1]
-    final = before is not None
-    if final:
-        shapes = [jax.ShapeDtypeStruct((features, HD), BF16)] * 2
-    else:
-        shapes = [jax.ShapeDtypeStruct((2 * HD, features), F32)]
-    inputs = [*grads] + ([before] if final else [])
-    return pl.pallas_call(
-        functools.partial(weight_grad_kernel, group, final),
+        product = jnp.dot(outputs, grad, preferred_element_type=F32).T.astype(BF16)
+        own_ref[columns, :] = product[:, :HD]
+        other_ref[columns, :] = product[:, HD:]
+
+
+def weight_grad(own_t, other_t, grads, after):
+    rows, features = own_t.shape[1], grads[0].shape[1]
+    shapes = [jax.ShapeDtypeStruct((features, HD), BF16)] * 2
+    return pl.pallas_call(
+        weight_grad_kernel,
         grid=(1,),
         out_shape=shapes,
-        in_specs=[whole(own_t), whole(other_t), corner(after)] + [whole(array) for array in inputs],
+        in_specs=[whole(own_t), whole(other_t), corner(after)] + [whole(array) for array in grads],
         out_specs=[whole(shape) for shape in shapes],
         compiler_params=params(),
-        cost_estimate=cost(4 * (group[1] - group[0]) * features * HD, 2 * (group[1] - group[0]) * features),
-    )(own_t, other_t, after, *inputs)
+        cost_estimate=cost(4 * rows * features * HD, 2 * rows * features),
+    )(own_t, other_t, after, *grads)
 
 
 def hold_kernel(*refs):
@@ -465,7 +459,10 @@
         left_top, right_low = move(left_top, 1), move(right_low, -1)
         left_low, right_top = move(left_low, 1), move(right_top, -1)
         if (HOLD2, HOLD3)[i]:
-            left_top, right_low = hold((left_top, right_low), (HOLD2, HOLD3)[i])
+            if i == 0:
+                (left_top,) = hold((left_top,), HOLD2)
+            else:
+                (left_low,) = hold((left_low,), HOLD3)
         near += [left_top, left_low, right_top, right_low]
 
     packed = lax.all_to_all(
@@ -482,13 +479,10 @@
     left_top, right_low, low = lax.optimization_barrier((left_top, right_low, low))
     far = [move(left_top, 1), move(right_low, -1)]
     last = [own_rows, *far]
-    cut, total = 6 * rows, seq * rows
-
-    proj_sum = weight_grad(low, low_other, near, (0, cut), None, left_top)[0]
-    near_own, other = project(near, own_weight, other_weight, proj_sum)
+
+    near_own, other = project(near, own_weight, other_weight, left_top)
     near_got = lax.ppermute(other, "tensor", swap)
-
-    proj_own, proj_send = weight_grad(low, low_other, last, (cut, total), proj_sum, near_own)
+    proj_own, proj_send = weight_grad(low, low_other, [*near, *last], near_own)
     proj_got = lax.ppermute(proj_send, "tensor", swap)
     own, other = project(last, own_weight, other_weight, proj_own)
     got = lax.ppermute(other, "tensor", swap)

time: 154 us -> 152 us (0.987)
  waiting for transfers between devices: 31.5 us -> 37.9 us
  starting transfers between devices: 44.8 us -> 41.4 us
  Pallas kernels: 31.4 us -> 29.6 us
  local copies, waits for them, and re-layouts: 8.05 us -> 6.39 us
    ppermute x12, waiting for transfers between devices: 7.06 us -> 16 us  [move(): return lax.ppermute(array, 'seq', right if step > 0 else left)]
    all_to_all x1, waiting for transfers between devices: 19.7 us -> 16.7 us  [per_device(): lax.all_to_all(pack(queries, keys, values, proj_weight, seq), 'seq', spli...]
    ppermute x12, starting transfers between devices: 23.2 us -> 21 us  [move(): return lax.ppermute(array, 'seq', right if step > 0 else left)]
    pallas_call x2, Pallas kernels: 1.75 us -> 0.04 us  [hold(): pl.pallas_call(hold_kernel, out_shape=[jax.ShapeDtypeStruct(array.shape,...]
    unnamed x52 -> x48, local copies, waits for them, and re-layouts: 6.85 us -> 5.17 us
    pallas_call x2 -> x1, Pallas kernels: 4.25 us -> 3.45 us  [weight_grad(): pl.pallas_call(weight_grad_kernel, grid=(1,), out_shape=shapes, in_specs=...]
  transfers between devices with their start and end apart: 20 -> 20, of which waited for: 5 -> 10; matrix products, arithmetic and copies ran while one was open for 1% -> 1% of each run, Pallas kernels for 17% -> 15%
where the time goes in v5:
time: 152 us
  starting transfers between devices  41.4 us (27%)
  waiting for transfers between devices  37.9 us (25%)
  blocking collectives  34.7 us (23%)
  Pallas kernels  29.6 us (19%)
  local copies, waits for them, and re-layouts  6.39 us (4%)
  between operations  1.75 us (1%)
    all_to_all x1, blocking collectives, per_device(): lax.all_to_all(result, 'seq', split_axis=0, concat_axis=0, tiled=True)  34.7 us
    ppermute x12, starting transfers between devices, move(): return lax.ppermute(array, 'seq', right if step > 0 else left)  21 us
    all_to_all x1, waiting for transfers between devices, per_device(): lax.all_to_all(pack(queries, keys, values, proj_weight, seq), 'seq', spli...  16.7 us
    ppermute x12, waiting for transfers between devices, move(): return lax.ppermute(array, 'seq', right if step > 0 else left)  16 us
    pallas_call x2, Pallas kernels, attend_backward(): pl.pallas_call(functools.partial(backward_kernel, rows, start, first, las...  9.19 us
    all_to_all x1, starting transfers between devices, per_device(): lax.all_to_all(joined, 'dp', split_axis=0, concat_axis=0, tiled=True)  7.49 us
    all_to_all x1, starting transfers between devices, per_device(): lax.all_to_all(copies, 'dp', split_axis=0, concat_axis=0, tiled=True)  7.48 us
    pallas_call x1, Pallas kernels, attend_forward(): pl.pallas_call(functools.partial(forward_kernel, rows), grid=(slots // PA...  7.22 us
  transfers between devices with their start and end apart: 20, of which 10 were waited for; matrix products, arithmetic and copies ran while one was open for 1% of the time, Pallas kernels for 15%

profile of v5, /device:TPU:2, one launch (start us, length us, event | category | flops | bytes accessed | tf_op | source)
XLA Modules:
  0.0 151.7 jit_solution(320882139647919249)
XLA Ops:
  1.3 1.1 copy-done.15
  2.3 0.7 copy-done.20
  3.1 0.1 shard_map.104.refs_10_.refs_0_
  3.2 5.9 %collective-permute-start.1 = (bf16[192,1536]{1,0:T(8,128)(2,1)S(1)}, bf16[192,1536]{1,0:T(8,128)(2,1)S(1)}, u32[]{:S(2)}, u32[]{:S(2)}) collective-permute-start(bf16[192,1536]{1,0:T(8,128)(2,1)S(1)} %shard_map.104.refs_10_.refs_0_), channel_id=1, source_target_pairs={{0,14},{2,0},{4,2},{6,4},{8,6},{10,8},{12,10},{14,12},{1,15},{3,1}... | collective-permute-start | bytes 1769480 | tf_op jit(solution)/shard_map/ppermute | solution.py:452
  9.2 0.8 copy-done.19
  10.0 1.3 shard_map.102
  11.3 4.6 %all-to-all-start = ((bf16[8,608,128]{2,1,0:T(8,128)(2,1)}), bf16[8,608,128]{2,1,0:T(8,128)(2,1)S(1)}, u32[]{:S(2)}, u32[]{:S(2)}) async-start(bf16[8,608,128]{2,1,0:T(8,128)(2,1)} %shard_map.102), calls=%async_computation | async-start | bytes 2490368 | tf_op jit(solution)/shard_map/all_to_all | solution.py:468
  15.9 10.1 %collective-permute-done.1.right_ref.refs_1_ = bf16[192,1536]{1,0:T(8,128)(2,1)S(1)} collective-permute-done((bf16[192,1536]{1,0:T(8,128)(2,1)S(1)}, bf16[192,1536]{1,0:T(8,128)(2,1)S(1)}, u32[]{:S(2)}, u32[]{:S(2)}) %collective-permute-start.1) | collective-permute-done | bytes 589856 | tf_op jit(solution)/shard_map/ppermute | solution.py:452
  26.0 3.0 %collective-permute-done.left_ref.refs_0_ = bf16[192,1536]{1,0:T(8,128)(2,1)S(1)} collective-permute-done((bf16[192,1536]{1,0:T(8,128)(2,1)S(1)}, bf16[192,1536]{1,0:T(8,128)(2,1)S(1)}, u32[]{:S(2)}, u32[]{:S(2)}) %collective-permute-start) | collective-permute-done | bytes 589856 | tf_op jit(solution)/shard_map/ppermute | solution.py:452
  29.1 1.2 shard_map.105
  30.3 0.1 copy-done.7
  30.3 3.2 %collective-permute-start.4 = (bf16[96,1536]{1,0:T(8,128)(2,1)}, bf16[96,1536]{1,0:T(8,128)(2,1)S(1)}, u32[]{:S(2)}, u32[]{:S(2)}) collective-permute-start(bf16[96,1536]{1,0:T(8,128)(2,1)} %get-tuple-element.28), channel_id=1, source_target_pairs={{0,14},{2,0},{4,2},{6,4},{8,6},{10,8},{12,10},{14,12},{1,15},{3,1}... | collective-permute-start | bytes 884744 | tf_op jit(solution)/shard_map/ppermute | solution.py:452
  33.6 3.2 %collective-permute-start.11 = (bf16[96,1536]{1,0:T(8,128)(2,1)}, bf16[96,1536]{1,0:T(8,128)(2,1)}, u32[]{:S(2)}, u32[]{:S(2)}) collective-permute-start(bf16[96,1536]{1,0:T(8,128)(2,1)} %get-tuple-element.34), channel_id=1, source_target_pairs={{0,14},{2,0},{4,2},{6,4},{8,6},{10,8},{12,10},{14,12},{1,15},{3,1}... | collective-permute-start | bytes 884744 | tf_op jit(solution)/shard_map/ppermute | solution.py:452
  36.8 16.7 %all-to-all-done.packed_ref.refs_0_ = bf16[8,608,128]{2,1,0:T(8,128)(2,1)S(1)} async-done(((bf16[8,608,128]{2,1,0:T(8,128)(2,1)}), bf16[8,608,128]{2,1,0:T(8,128)(2,1)S(1)}, u32[]{:S(2)}, u32[]{:S(2)}) %all-to-all-start) | async-done | bytes 1245216 | tf_op jit(solution)/shard_map/all_to_all | solution.py:468
  53.5 1.2 broadcast_in_dim.8._
  54.7 7.5 %all-to-all-start.1 = ((bf16[16,192,128]{2,1,0:T(8,128)(2,1)}), bf16[16,192,128]{2,1,0:T(8,128)(2,1)S(1)}, u32[]{:S(2)}, u32[]{:S(2)}) async-start(bf16[16,192,128]{2,1,0:T(8,128)(2,1)} %broadcast_in_dim.8._), calls=%async_computation.1 | async-start | bytes 1572864 | tf_op jit(solution)/shard_map/all_to_all | solution.py:473
  62.2 0.1 collective-permute-start.3
  62.3 3.2 %collective-permute-start.5 = (bf16[96,1536]{1,0:T(8,128)(2,1)S(1)}, bf16[96,1536]{1,0:T(8,128)(2,1)}, u32[]{:S(2)}, u32[]{:S(2)}) collective-permute-start(bf16[96,1536]{1,0:T(8,128)(2,1)S(1)} %collective-permute-done.4.refs_5_), channel_id=1, source_target_pairs={{0,14},{2,0},{4,2},{6,4},{8,6},{10,8},{12,10},{14,12},{1,15},{3,1}... | collective-permute-start | bytes 884744 | tf_op jit(solution)/shard_map/ppermute | solution.py:452
  65.5 0.5 collective-permute-done.10.refs_3_
  66.1 3.2 %collective-permute-start.13 = (bf16[96,1536]{1,0:T(8,128)(2,1)}, bf16[96,1536]{1,0:T(8,128)(2,1)}, u32[]{:S(2)}, u32[]{:S(2)}) collective-permute-start(bf16[96,1536]{1,0:T(8,128)(2,1)} %collective-permute-done.11.refs_4_), channel_id=1, source_target_pairs={{0,14},{2,0},{4,2},{6,4},{8,6},{10,8},{12,10},{14,12},{1,15},{3,1}... | collective-permute-start | bytes 884744 | tf_op jit(solution)/shard_map/ppermute | solution.py:452
  69.3 7.2 %shard_map.103 = (bf16[1536,1536]{1,0:T(8,128)(2,1)}, f32[1,1536]{1,0:T(1,128)S(1)}, f32[128,1536]{1,0:T(8,128)S(1)}, bf16[128,1536]{1,0:T(8,128)(2,1)}) custom-call(s32[1]{0:T(128)S(6)} %copy.13.length_ref, bf16[8,608,128]{2,1,0:T(8,128)(2,1)S(1)} %all-to-all-done.packed_ref.refs_0_, bf16[16,192,128]{2,1,0:T(8,128)(2,1)} %broadcast_in_dim.8._), custom_call_target="tpu_custom_call" | custom-call | flops 1207959552 | bytes 4718592 | tf_op jit(solution)/shard_map/pallas_call | solution.py:216
  76.5 0.1 collective-permute-start.9
  76.6 0.1 collective-permute-start.7
  76.7 2.0 %collective-permute-start.6 = (bf16[96,1536]{1,0:T(8,128)(2,1)S(1)}, bf16[96,1536]{1,0:T(8,128)(2,1)}, u32[]{:S(2)}, u32[]{:S(2)}) collective-permute-start(bf16[96,1536]{1,0:T(8,128)(2,1)S(1)} %collective-permute-done.3.refs_6_.refs_12_), channel_id=1, source_target_pairs={{0,2},{2,4},{4,6},{6,8},{8,10},{10,12},{12,14},{14,0},{1,3},{3,5},... | collective-permute-start | bytes 884744 | tf_op jit(solution)/shard_map/ppermute | solution.py:452
  78.8 0.7 copy-done.22
  79.5 0.1 collective-permute-start.8
  79.6 0.0 copy-start.23
  79.6 1.1 copy-done.23
  80.7 1.2 collective-permute-done.8.refs_11_.refs_4_
  81.9 2.7 %shard_map.108 = (f32[1152,128]{1,0:T(8,128)S(1)}, bf16[1152,128]{1,0:T(8,128)(2,1)S(1)}) custom-call(bf16[192,1536]{1,0:T(8,128)(2,1)S(1)} %copy-done.8, bf16[192,1536]{1,0:T(8,128)(2,1)S(1)} %copy-done.6, bf16[96,1536]{1,0:T(8,128)(2,1)S(1)} %copy-done.12, bf16[96,1536]{1,0:T(8,128)(2,1)} %collective-permute-done.10.refs_3_, ...), custom_call_target="tpu_custom_call" | custom-call | flops 905969664 | bytes 3538944 | tf_op jit(solution)/shard_map/pallas_call | solution.py:257
  84.6 0.0 copy-start.21
  84.6 0.7 copy-done.21
  85.3 1.0 collective-permute-done.7.refs_12_.refs_2_
  86.3 1.4 collective-permute-done.6.refs_11_.refs_1_
  87.7 3.5 %shard_map.109 = (bf16[1536,128]{1,0:T(8,128)(2,1)S(1)}, bf16[1536,128]{1,0:T(8,128)(2,1)S(1)}) custom-call(bf16[128,1536]{1,0:T(8,128)(2,1)} %get-tuple-element.32.own_t_ref, bf16[128,1536]{1,0:T(8,128)(2,1)} %collective-permute-done.9.other_t_ref, f32[1152,128]{1,0:T(8,128)S(1)} %get-tuple-element.35._.refs_4_, bf16[192,1536]{1,0:T(8,128)(2,1)S(1)} %copy-done.8, ...), custom_call_target="tpu_custom_call" | custom-call | flops 1207959552 | bytes 4718592 | tf_op jit(solution)/shard_map/pallas_call | solution.py:282
  91.1 0.1 collective-permute-start.15
  91.2 1.5 shard_map.110
  92.7 0.2 collective-permute-done.15.got_ref
  92.9 0.9 shard_map.111
  93.8 7.5 %all-to-all-start.2 = ((bf16[16,192,128]{2,1,0:T(8,128)(2,1)}), bf16[16,192,128]{2,1,0:T(8,128)(2,1)S(1)}, u32[]{:S(2)}, u32[]{:S(2)}) async-start(bf16[16,192,128]{2,1,0:T(8,128)(2,1)} %bitcast.2.refs_6_), calls=%async_computation.2 | async-start | bytes 1572864 | tf_op jit(solution)/shard_map/all_to_all | solution.py:490
  101.3 0.5 collective-permute-start.14
  101.8 1.3 collective-permute-done.16.refs_5_
  103.1 6.0 %shard_map.112 = (bf16[1152,128]{1,0:T(8,128)(2,1)S(1)}, f32[1536,128]{1,0:T(8,128)S(1)}, f32[1536,128]{1,0:T(8,128)S(1)}) custom-call(bf16[8,608,128]{2,1,0:T(8,128)(2,1)S(1)} %all-to-all-done.packed_ref.refs_0_, bf16[1536,1536]{1,0:T(8,128)(2,1)} %get-tuple-element.24.refs_1_, f32[1,1536]{1,0:T(1,128)S(1)} %get-tuple-element.25.refs_2_, ...), custom_call_target="tpu_custom_call" | custom-call | flops 1811939328 | bytes 3538944 | tf_op jit(solution)/shard_map/pallas_call | solution.py:422
  109.2 3.2 %shard_map.113.grads_ref = bf16[8,608,128]{2,1,0:T(8,128)(2,1)S(1)} custom-call(bf16[8,608,128]{2,1,0:T(8,128)(2,1)} %copy-done, bf16[1536,1536]{1,0:T(8,128)(2,1)} %get-tuple-element.24.refs_1_, f32[1,1536]{1,0:T(1,128)S(1)} %get-tuple-element.25.refs_2_, f32[128,1536]{1,0:T(8,128)S(1)} %get-tuple-element.26.refs_3_, f32[384,128]{1,0:T(8,128)S(1)} %copy-done.14, ...), custom_call_target="tpu_custom_call" | custom-call | flops 603979776 | bytes 1179648 | tf_op jit(solution)/shard_map/pallas_call | solution.py:422
  112.4 2.5 %all-to-all-done.2.parts_ref = bf16[16,192,128]{2,1,0:T(8,128)(2,1)S(1)} async-done(((bf16[16,192,128]{2,1,0:T(8,128)(2,1)}), bf16[16,192,128]{2,1,0:T(8,128)(2,1)S(1)}, u32[]{:S(2)}, u32[]{:S(2)}) %all-to-all-start.2) | async-done | bytes 786464 | tf_op jit(solution)/shard_map/all_to_all | solution.py:490
  114.9 0.1 shard_map.114
  115.0 34.7 %all_to_all.20.packed_ref = bf16[8,608,128]{2,1,0:T(8,128)(2,1)S(1)} all-to-all(bf16[8,608,128]{2,1,0:T(8,128)(2,1)S(1)} %shard_map.114), channel_id=1, replica_groups=mesh['dp'=16,'seq'=8,'tensor'=2] {'seq'}, dimensions={0} | all-to-all | bytes 2490368 | tf_op jit(solution)/shard_map/all_to_all | solution.py:495
  149.7 1.9 %shard_map.115 = (bf16[192,1024]{1,0:T(8,128)(2,1)}, bf16[192,1024]{1,0:T(8,128)(2,1)}, bf16[192,1024]{1,0:T(8,128)(2,1)}, f32[24,1024]{1,0:T(8,128)}) custom-call(bf16[8,608,128]{2,1,0:T(8,128)(2,1)S(1)} %all_to_all.20.packed_ref), custom_call_target="tpu_custom_call" | custom-call | bytes 2490368 | tf_op jit(solution)/shard_map/pallas_call | solution.py:125
  (57 shorter events, 0.2 us)
Async XLA Ops:
  1.3 1.1 copy-start.15
  2.3 0.7 copy-start.20
  3.1 6.1 %copy-start.16 = (bf16[192,1024]{1,0:T(8,128)(2,1)S(1)}, bf16[192,1024]{1,0:T(8,128)(2,1)}, u32[]{:S(2)}) copy-start(bf16[192,1024]{1,0:T(8,128)(2,1)} %query_ref.1) | copy-start | bytes 1179652
  3.1 6.1 %copy-start.17 = (bf16[192,1024]{1,0:T(8,128)(2,1)S(1)}, bf16[192,1024]{1,0:T(8,128)(2,1)}, u32[]{:S(2)}) copy-start(bf16[192,1024]{1,0:T(8,128)(2,1)} %key_ref.1) | copy-start | bytes 1179652
  3.1 6.1 %copy-start.18 = (bf16[192,1024]{1,0:T(8,128)(2,1)S(1)}, bf16[192,1024]{1,0:T(8,128)(2,1)}, u32[]{:S(2)}) copy-start(bf16[192,1024]{1,0:T(8,128)(2,1)} %value_ref.1) | copy-start | bytes 1179652
  3.2 8.1 %copy-start.1 = (bf16[192,1536]{1,0:T(8,128)(2,1)}, bf16[192,1536]{1,0:T(8,128)(2,1)S(1)}, u32[]{:S(2)}) copy-start(bf16[192,1536]{1,0:T(8,128)(2,1)S(1)} %shard_map.104.refs_10_.refs_0_) | copy-start | bytes 1769476
  3.2 22.8 %collective-permute-start.1 = (bf16[192,1536]{1,0:T(8,128)(2,1)S(1)}, bf16[192,1536]{1,0:T(8,128)(2,1)S(1)}, u32[]{:S(2)}, u32[]{:S(2)}) collective-permute-start(bf16[192,1536]{1,0:T(8,128)(2,1)S(1)} %shard_map.104.refs_10_.refs_0_), channel_id=1, source_target_pairs={{0,14},{2,0},{4,2},{6,4},{8,6},{10,8},{12,10},{14,12},{1,15},{3,1}... | collective-permute-start | bytes 1769480 | tf_op jit(solution)/shard_map/ppermute | solution.py:452
  9.2 19.9 %collective-permute-start = (bf16[192,1536]{1,0:T(8,128)(2,1)S(1)}, bf16[192,1536]{1,0:T(8,128)(2,1)S(1)}, u32[]{:S(2)}, u32[]{:S(2)}) collective-permute-start(bf16[192,1536]{1,0:T(8,128)(2,1)S(1)} %shard_map.104.refs_10_.refs_0_), channel_id=1, source_target_pairs={{0,2},{2,4},{4,6},{6,8},{8,10},{10,12},{12,14},{14,0},{1,3},{3,5},... | collective-permute-start | bytes 1769480 | tf_op jit(solution)/shard_map/ppermute | solution.py:452
  9.2 0.8 copy-start.19
  11.3 42.2 %all-to-all-start = ((bf16[8,608,128]{2,1,0:T(8,128)(2,1)}), bf16[8,608,128]{2,1,0:T(8,128)(2,1)S(1)}, u32[]{:S(2)}, u32[]{:S(2)}) async-start(bf16[8,608,128]{2,1,0:T(8,128)(2,1)} %shard_map.102), calls=%async_computation | async-start | bytes 2490368 | tf_op jit(solution)/shard_map/all_to_all | solution.py:468
  26.0 4.2 %copy-start.5 = (bf16[192,1536]{1,0:T(8,128)(2,1)}, bf16[192,1536]{1,0:T(8,128)(2,1)S(1)}, u32[]{:S(2)}) copy-start(bf16[192,1536]{1,0:T(8,128)(2,1)S(1)} %collective-permute-done.1.right_ref.refs_1_) | copy-start | bytes 1769476
  29.1 1.3 copy-start.7
  30.3 31.8 %collective-permute-start.2 = (bf16[96,1536]{1,0:T(8,128)(2,1)}, bf16[96,1536]{1,0:T(8,128)(2,1)S(1)}, u32[]{:S(2)}, u32[]{:S(2)}) collective-permute-start(bf16[96,1536]{1,0:T(8,128)(2,1)} %get-tuple-element.27), channel_id=1, source_target_pairs={{0,2},{2,4},{4,6},{6,8},{8,10},{10,12},{12,14},{14,0},{1,3},{3,5},... | collective-permute-start | bytes 884744 | tf_op jit(solution)/shard_map/ppermute | solution.py:452
  30.3 32.0 %collective-permute-start.4 = (bf16[96,1536]{1,0:T(8,128)(2,1)}, bf16[96,1536]{1,0:T(8,128)(2,1)S(1)}, u32[]{:S(2)}, u32[]{:S(2)}) collective-permute-start(bf16[96,1536]{1,0:T(8,128)(2,1)} %get-tuple-element.28), channel_id=1, source_target_pairs={{0,14},{2,0},{4,2},{6,4},{8,6},{10,8},{12,10},{14,12},{1,15},{3,1}... | collective-permute-start | bytes 884744 | tf_op jit(solution)/shard_map/ppermute | solution.py:452
  33.6 32.5 %collective-permute-start.10 = (bf16[96,1536]{1,0:T(8,128)(2,1)}, bf16[96,1536]{1,0:T(8,128)(2,1)}, u32[]{:S(2)}, u32[]{:S(2)}) collective-permute-start(bf16[96,1536]{1,0:T(8,128)(2,1)} %get-tuple-element.33), channel_id=1, source_target_pairs={{0,2},{2,4},{4,6},{6,8},{8,10},{10,12},{12,14},{14,0},{1,3},{3,5},... | collective-permute-start | bytes 884744 | tf_op jit(solution)/shard_map/ppermute | solution.py:452
  33.6 32.5 %collective-permute-start.11 = (bf16[96,1536]{1,0:T(8,128)(2,1)}, bf16[96,1536]{1,0:T(8,128)(2,1)}, u32[]{:S(2)}, u32[]{:S(2)}) collective-permute-start(bf16[96,1536]{1,0:T(8,128)(2,1)} %get-tuple-element.34), channel_id=1, source_target_pairs={{0,14},{2,0},{4,2},{6,4},{8,6},{10,8},{12,10},{14,12},{1,15},{3,1}... | collective-permute-start | bytes 884744 | tf_op jit(solution)/shard_map/ppermute | solution.py:452
  53.5 49.7 %copy-start = (bf16[8,608,128]{2,1,0:T(8,128)(2,1)}, bf16[8,608,128]{2,1,0:T(8,128)(2,1)S(1)}, u32[]{:S(2)}) copy-start(bf16[8,608,128]{2,1,0:T(8,128)(2,1)S(1)} %all-to-all-done.packed_ref.refs_0_) | copy-start | bytes 3735556
  54.7 24.8 %all-to-all-start.1 = ((bf16[16,192,128]{2,1,0:T(8,128)(2,1)}), bf16[16,192,128]{2,1,0:T(8,128)(2,1)S(1)}, u32[]{:S(2)}, u32[]{:S(2)}) async-start(bf16[16,192,128]{2,1,0:T(8,128)(2,1)} %broadcast_in_dim.8._), calls=%async_computation.1 | async-start | bytes 1572864 | tf_op jit(solution)/shard_map/all_to_all | solution.py:473
  62.2 14.3 %copy-start.11 = (bf16[96,1536]{1,0:T(8,128)(2,1)}, bf16[96,1536]{1,0:T(8,128)(2,1)S(1)}, u32[]{:S(2)}) copy-start(bf16[96,1536]{1,0:T(8,128)(2,1)S(1)} %shard_map.106.refs_2_) | copy-start | bytes 884740
  62.2 14.4 %collective-permute-start.3 = (bf16[96,1536]{1,0:T(8,128)(2,1)S(1)}, bf16[96,1536]{1,0:T(8,128)(2,1)S(1)}, u32[]{:S(2)}, u32[]{:S(2)}) collective-permute-start(bf16[96,1536]{1,0:T(8,128)(2,1)S(1)} %shard_map.106.refs_2_), channel_id=1, source_target_pairs={{0,2},{2,4},{4,6},{6,8},{8,10},{10,12},{12,14},{14,0},{1,3},{3,5},... | collective-permute-start | bytes 884744 | tf_op jit(solution)/shard_map/ppermute | solution.py:452
  62.3 14.2 %copy-start.9 = (bf16[96,1536]{1,0:T(8,128)(2,1)}, bf16[96,1536]{1,0:T(8,128)(2,1)S(1)}, u32[]{:S(2)}) copy-start(bf16[96,1536]{1,0:T(8,128)(2,1)S(1)} %collective-permute-done.4.refs_5_) | copy-start | bytes 884740
  62.3 14.3 %collective-permute-start.5 = (bf16[96,1536]{1,0:T(8,128)(2,1)S(1)}, bf16[96,1536]{1,0:T(8,128)(2,1)}, u32[]{:S(2)}, u32[]{:S(2)}) collective-permute-start(bf16[96,1536]{1,0:T(8,128)(2,1)S(1)} %collective-permute-done.4.refs_5_), channel_id=1, source_target_pairs={{0,14},{2,0},{4,2},{6,4},{8,6},{10,8},{12,10},{14,12},{1,15},{3,1}... | collective-permute-start | bytes 884744 | tf_op jit(solution)/shard_map/ppermute | solution.py:452
  66.0 12.7 %collective-permute-start.12 = (bf16[96,1536]{1,0:T(8,128)(2,1)}, bf16[96,1536]{1,0:T(8,128)(2,1)S(1)}, u32[]{:S(2)}, u32[]{:S(2)}) collective-permute-start(bf16[96,1536]{1,0:T(8,128)(2,1)} %collective-permute-done.10.refs_3_), channel_id=1, source_target_pairs={{0,2},{2,4},{4,6},{6,8},{8,10},{10,12},{12,14},{14,0},{1,3},{3,5},... | collective-permute-start | bytes 884744 | tf_op jit(solution)/shard_map/ppermute | solution.py:452
  66.1 14.6 %collective-permute-start.13 = (bf16[96,1536]{1,0:T(8,128)(2,1)}, bf16[96,1536]{1,0:T(8,128)(2,1)}, u32[]{:S(2)}, u32[]{:S(2)}) collective-permute-start(bf16[96,1536]{1,0:T(8,128)(2,1)} %collective-permute-done.11.refs_4_), channel_id=1, source_target_pairs={{0,14},{2,0},{4,2},{6,4},{8,6},{10,8},{12,10},{14,12},{1,15},{3,1}... | collective-permute-start | bytes 884744 | tf_op jit(solution)/shard_map/ppermute | solution.py:452
  76.5 11.1 %collective-permute-start.9 = (bf16[128,1536]{1,0:T(8,128)(2,1)}, bf16[128,1536]{1,0:T(8,128)(2,1)}, u32[]{:S(2)}, u32[]{:S(2)}) collective-permute-start(bf16[128,1536]{1,0:T(8,128)(2,1)} %get-tuple-element.32.own_t_ref), channel_id=1, source_target_pairs={{0,1},{1,0},{2,3},{3,2},{4,5},{5,4},{6,7},{7,6},{8,9},{9,8},{10,11... | collective-permute-start | bytes 1179656 | tf_op jit(solution)/shard_map/ppermute | solution.py:477
  76.6 9.6 %collective-permute-start.7 = (bf16[96,1536]{1,0:T(8,128)(2,1)}, bf16[96,1536]{1,0:T(8,128)(2,1)S(1)}, u32[]{:S(2)}, u32[]{:S(2)}) collective-permute-start(bf16[96,1536]{1,0:T(8,128)(2,1)} %collective-permute-done.5.refs_9_), channel_id=1, source_target_pairs={{0,14},{2,0},{4,2},{6,4},{8,6},{10,8},{12,10},{14,12},{1,15},{3,1}... | collective-permute-start | bytes 884744 | tf_op jit(solution)/shard_map/ppermute | solution.py:452
  76.7 10.9 %collective-permute-start.6 = (bf16[96,1536]{1,0:T(8,128)(2,1)S(1)}, bf16[96,1536]{1,0:T(8,128)(2,1)}, u32[]{:S(2)}, u32[]{:S(2)}) collective-permute-start(bf16[96,1536]{1,0:T(8,128)(2,1)S(1)} %collective-permute-done.3.refs_6_.refs_12_), channel_id=1, source_target_pairs={{0,2},{2,4},{4,6},{6,8},{8,10},{10,12},{12,14},{14,0},{1,3},{3,5},... | collective-permute-start | bytes 884744 | tf_op jit(solution)/shard_map/ppermute | solution.py:452
  78.8 0.7 copy-start.22
  79.5 2.4 %copy-start.6 = (bf16[192,1536]{1,0:T(8,128)(2,1)S(1)}, bf16[192,1536]{1,0:T(8,128)(2,1)}, u32[]{:S(2)}) copy-start(bf16[192,1536]{1,0:T(8,128)(2,1)} %copy-done.5) | copy-start | bytes 1769476
  79.5 2.4 %copy-start.8 = (bf16[192,1536]{1,0:T(8,128)(2,1)S(1)}, bf16[192,1536]{1,0:T(8,128)(2,1)}, u32[]{:S(2)}) copy-start(bf16[192,1536]{1,0:T(8,128)(2,1)} %copy-done.7) | copy-start | bytes 1769476
  79.5 2.4 %copy-start.10 = (bf16[96,1536]{1,0:T(8,128)(2,1)S(1)}, bf16[96,1536]{1,0:T(8,128)(2,1)}, u32[]{:S(2)}) copy-start(bf16[96,1536]{1,0:T(8,128)(2,1)} %copy-done.9) | copy-start | bytes 884740
  79.5 2.4 %copy-start.12 = (bf16[96,1536]{1,0:T(8,128)(2,1)S(1)}, bf16[96,1536]{1,0:T(8,128)(2,1)}, u32[]{:S(2)}) copy-start(bf16[96,1536]{1,0:T(8,128)(2,1)} %copy-done.11) | copy-start | bytes 884740
  79.5 2.4 %collective-permute-start.8 = (bf16[3072,128]{1,0:T(8,128)(2,1)S(1)}, bf16[3072,128]{1,0:T(8,128)(2,1)S(1)}, u32[]{:S(2)}, u32[]{:S(2)}) collective-permute-start(bf16[3072,128]{1,0:T(8,128)(2,1)S(1)} %bitcast.3), channel_id=1, source_target_pairs={{0,1},{1,0},{2,3},{3,2},{4,5},{5,4},{6,7},{7,6},{8,9},{9,8},{10,11... | collective-permute-start | bytes 2359304 | tf_op jit(solution)/shard_map/ppermute | solution.py:474
  79.6 1.1 copy-start.23
  84.6 0.7 copy-start.21
  85.3 5.8 %copy-start.3 = (f32[1152,128]{1,0:T(8,128)}, f32[1152,128]{1,0:T(8,128)S(1)}, u32[]{:S(2)}) copy-start(f32[1152,128]{1,0:T(8,128)S(1)} %get-tuple-element.35._.refs_4_) | copy-start | bytes 1769476
  87.7 3.6 %copy-start.2 = (bf16[192,1536]{1,0:T(8,128)(2,1)S(1)}, bf16[192,1536]{1,0:T(8,128)(2,1)}, u32[]{:S(2)}) copy-start(bf16[192,1536]{1,0:T(8,128)(2,1)} %copy-done.1) | copy-start | bytes 1769476
  91.1 1.8 %collective-permute-start.15 = (bf16[1536,128]{1,0:T(8,128)(2,1)S(1)}, bf16[1536,128]{1,0:T(8,128)(2,1)S(1)}, u32[]{:S(2)}, u32[]{:S(2)}) collective-permute-start(bf16[1536,128]{1,0:T(8,128)(2,1)S(1)} %get-tuple-element.39), channel_id=1, source_target_pairs={{0,1},{1,0},{2,3},{3,2},{4,5},{5,4},{6,7},{7,6},{8,9},{9,8},{10,11... | collective-permute-start | bytes 1179656 | tf_op jit(solution)/shard_map/ppermute | solution.py:486
  92.7 1.1 copy-start.13
  92.9 10.2 %copy-start.4 = (f32[1152,128]{1,0:T(8,128)S(1)}, f32[1152,128]{1,0:T(8,128)}, u32[]{:S(2)}) copy-start(f32[1152,128]{1,0:T(8,128)} %copy-done.3) | copy-start | bytes 1769476
  93.8 21.0 %all-to-all-start.2 = ((bf16[16,192,128]{2,1,0:T(8,128)(2,1)}), bf16[16,192,128]{2,1,0:T(8,128)(2,1)S(1)}, u32[]{:S(2)}, u32[]{:S(2)}) async-start(bf16[16,192,128]{2,1,0:T(8,128)(2,1)} %bitcast.2.refs_6_), calls=%async_computation.2 | async-start | bytes 1572864 | tf_op jit(solution)/shard_map/all_to_all | solution.py:490
  101.3 1.8 %collective-permute-start.16 = (bf16[1152,128]{1,0:T(8,128)(2,1)}, bf16[1152,128]{1,0:T(8,128)(2,1)S(1)}, u32[]{:S(2)}, u32[]{:S(2)}) collective-permute-start(bf16[1152,128]{1,0:T(8,128)(2,1)} %copy-done.21), channel_id=1, source_target_pairs={{0,1},{1,0},{2,3},{3,2},{4,5},{5,4},{6,7},{7,6},{8,9},{9,8},{10,11... | collective-permute-start | bytes 884744 | tf_op jit(solution)/shard_map/ppermute | solution.py:484
  101.3 7.8 %collective-permute-start.14 = (bf16[384,128]{1,0:T(8,128)(2,1)S(1)}, bf16[384,128]{1,0:T(8,128)(2,1)S(1)}, u32[]{:S(2)}, u32[]{:S(2)}) collective-permute-start(bf16[384,128]{1,0:T(8,128)(2,1)S(1)} %get-tuple-element.38), channel_id=1, source_target_pairs={{0,1},{1,0},{2,3},{3,2},{4,5},{5,4},{6,7},{7,6},{8,9},{9,8},{10,11... | collective-permute-start | bytes 294920 | tf_op jit(solution)/shard_map/ppermute | solution.py:488
  103.1 6.0 %copy-start.14 = (f32[384,128]{1,0:T(8,128)S(1)}, f32[384,128]{1,0:T(8,128)}, u32[]{:S(2)}) copy-start(f32[384,128]{1,0:T(8,128)} %copy-done.13) | copy-start | bytes 589828

commit v6 on v5

--- a/solution.py
+++ b/solution.py
@@ -97,42 +97,34 @@
     )(queries, keys, values, weight)
 
 
-def unpack_kernel(packed_ref, query_ref, key_ref, value_ref, weight_ref, padded, sems):
+def unpack_kernel(packed_ref, query_ref, key_ref, value_ref, weight_ref, rows_scr, sems):
     rows = query_ref.shape[0]
     slots, height, _ = packed_ref.shape
-    wrows = weight_ref.shape[0]
-    first = pltpu.make_async_copy(packed_ref.at[:, 3 * rows : height, :], padded, sems.at[0])
-    first.start()
     copies = []
+    for i, ref in enumerate((query_ref, key_ref, value_ref)):
+        for slot in range(slots):
+            rows_scr[i, :, slot * HD : (slot + 1) * HD] = packed_ref[slot, i * rows : (i + 1) * rows, :]
+        copies.append(pltpu.make_async_copy(rows_scr.at[i], ref, sems.at[i]))
+        copies[i].start()
     for slot in range(slots):
-        for i, ref in enumerate((query_ref, key_ref, value_ref)):
-            source = packed_ref.at[slot, i * rows : (i + 1) * rows, :]
-            target = ref.at[:, slot * HD : (slot + 1) * HD]
-            copies.append(pltpu.make_async_copy(source, target, sems.at[len(copies) + 1]))
-    for copy in copies:
-        copy.start()
-    first.wait()
-    for slot in range(slots):
-        weight_ref[:, slot * HD : (slot + 1) * HD] = padded[slot].astype(F32)[:wrows]
+        last = packed_ref[slot, 3 * rows : height, :].astype(F32)
+        weight_ref[:, slot * HD : (slot + 1) * HD] = last[: weight_ref.shape[0]]
     for copy in copies:
         copy.wait()
 
 
 def unpack(packed, rows, wrows):
-    slots, height, _ = packed.shape
+    slots = packed.shape[0]
     token = jax.ShapeDtypeStruct((rows, slots * HD), BF16)
     weight = jax.ShapeDtypeStruct((wrows, slots * HD), F32)
     return pl.pallas_call(
         unpack_kernel,
         out_shape=[token, token, token, weight],
-        in_specs=[anywhere()],
+        in_specs=[whole(packed)],
         out_specs=[anywhere(), anywhere(), anywhere(), whole(weight)],
-        scratch_shapes=[
-            pltpu.VMEM((slots, height - 3 * rows, HD), BF16),
-            pltpu.SemaphoreType.DMA((3 * slots + 1,)),
-        ],
-        compiler_params=params(),
-        cost_estimate=cost(0, 2 * 2 * slots * height * HD),
+        scratch_shapes=[pltpu.VMEM((3, rows, slots * HD), BF16), pltpu.SemaphoreType.DMA((3,))],
+        compiler_params=params(),
+        cost_estimate=cost(0, 4 * packed.size),
     )(packed)
 
 
@@ -165,6 +157,29 @@
     )(grads, parts)
 
 
+def spread_kernel(rows, wrows, packed_ref, _, out_ref, weight_scr):
+    slots, height, _ = packed_ref.shape
+    for slot in range(slots):
+        last = packed_ref[slot, 3 * rows : height, :].astype(F32)
+        weight_scr[slot * wrows : (slot + 1) * wrows, :] = last[:wrows]
+    out_ref[...] = jnp.broadcast_to(weight_scr[...].astype(BF16)[None], out_ref.shape)
+
+
+def spread(packed, rows, wrows, copies, after):
+    total = packed.shape[0] * wrows
+    shape = jax.ShapeDtypeStruct((copies, total, HD), BF16)
+    return pl.pallas_call(
+        functools.partial(spread_kernel, rows, wrows),
+        grid=(1,),
+        out_shape=shape,
+        in_specs=[whole(packed), corner(after)],
+        out_specs=whole(shape),
+        scratch_shapes=[pltpu.VMEM((total, HD), F32)],
+        compiler_params=params(),
+        cost_estimate=cost(0, 2 * shape.size),
+    )(packed, after)
+
+
 def slot_of(number, slots):
     even = number % 2 == 0
     distance = number // 2 + 1
@@ -192,8 +207,8 @@
     top = jnp.full((8, width), -jnp.inf, F32)
     for begin in range(0, total, grain):
         bias = jnp.where(begin < length_ref[0], 0.0, -jnp.inf).astype(F32)
-        part = scores_ref[begin : begin + grain, :] + bias
-        top = jnp.maximum(top, jnp.max(part.reshape(grain // 8, 8, width), axis=0))
+        part = scores_ref[begin : begin + grain, :]
+        top = jnp.maximum(top, jnp.max(part.reshape(grain // 8, 8, width), axis=0) + bias)
     top = jnp.max(top, axis=0, keepdims=True)
     norm = jnp.zeros((8, width), F32)
     for begin in range(0, total, grain):
@@ -343,7 +358,7 @@
         join_kernel,
         grid=(1,),
         out_shape=jax.ShapeDtypeStruct((2 * own.shape[0], HD), BF16),
-        in_specs=[whole(own), whole(got), corner(after)],
+        in_specs=[anywhere(), anywhere(), corner(after)],
         out_specs=anywhere(),
         scratch_shapes=[pltpu.SemaphoreType.DMA((2,))],
         compiler_params=params(),
@@ -468,8 +483,7 @@
     packed = lax.all_to_all(
         pack(queries, keys, values, proj_weight, seq), "seq", split_axis=0, concat_axis=0, tiled=True
     )
-    weight_rows = packed[:, 3 * rows : 3 * rows + wrows].reshape(1, seq * wrows, HD)
-    copies = jnp.broadcast_to(weight_rows, (dp, seq * wrows, HD))
+    copies = spread(packed, rows, wrows, dp, packed)
     own_weight = lax.all_to_all(copies, "dp", split_axis=0, concat_axis=0, tiled=True).reshape(-1, HD)
     other_weight = lax.ppermute(own_weight, "tensor", swap)
 

time: 152 us -> 152 us (level)
  transfers between devices with their start and end apart: 20 -> 20, of which waited for: 10 -> 10; matrix products, arithmetic and copies ran while one was open for 1% -> 0% of each run, Pallas kernels for 15% -> 16%
where the time goes in v6:
time: 152 us
  starting transfers between devices  41.4 us (27%)
  waiting for transfers between devices  38 us (25%)
  blocking collectives  34.7 us (23%)
  Pallas kernels  30.6 us (20%)
  local copies, waits for them, and re-layouts  5.17 us (3%)
  between operations  1.75 us (1%)
    all_to_all x1, blocking collectives, per_device(): lax.all_to_all(result, 'seq', split_axis=0, concat_axis=0, tiled=True)  34.7 us
    ppermute x12, starting transfers between devices, move(): return lax.ppermute(array, 'seq', right if step > 0 else left)  21 us
    all_to_all x1, waiting for transfers between devices, per_device(): lax.all_to_all(pack(queries, keys, values, proj_weight, seq), 'seq', spli...  16.7 us
    ppermute x12, waiting for transfers between devices, move(): return lax.ppermute(array, 'seq', right if step > 0 else left)  16.2 us
    pallas_call x2, Pallas kernels, attend_backward(): pl.pallas_call(functools.partial(backward_kernel, rows, start, first, las...  9.19 us
    all_to_all x1, starting transfers between devices, per_device(): lax.all_to_all(joined, 'dp', split_axis=0, concat_axis=0, tiled=True)  7.49 us
    all_to_all x1, starting transfers between devices, per_device(): lax.all_to_all(copies, 'dp', split_axis=0, concat_axis=0, tiled=True)  7.48 us
    pallas_call x1, Pallas kernels, attend_forward(): pl.pallas_call(functools.partial(forward_kernel, rows), grid=(slots // PA...  7.2 us
  transfers between devices with their start and end apart: 20, of which 10 were waited for; matrix products, arithmetic and copies ran while one was open for 0% of the time, Pallas kernels for 16%

profile of v6, /device:TPU:2, one launch (start us, length us, event | category | flops | bytes accessed | tf_op | source)
XLA Modules:
  0.0 151.6 jit_solution(5595058771550639975)
XLA Ops:
  1.3 1.1 copy-done.15
  2.3 0.7 copy-done.20
  3.1 0.1 shard_map.105.refs_10_.refs_0_
  3.2 5.9 %collective-permute-start.1 = (bf16[192,1536]{1,0:T(8,128)(2,1)S(1)}, bf16[192,1536]{1,0:T(8,128)(2,1)S(1)}, u32[]{:S(2)}, u32[]{:S(2)}) collective-permute-start(bf16[192,1536]{1,0:T(8,128)(2,1)S(1)} %shard_map.105.refs_10_.refs_0_), channel_id=1, source_target_pairs={{0,14},{2,0},{4,2},{6,4},{8,6},{10,8},{12,10},{14,12},{1,15},{3,1}... | collective-permute-start | bytes 1769480 | tf_op jit(solution)/shard_map/ppermute | solution.py:467
  9.2 0.0 copy-start.19
  9.2 0.8 copy-done.19
  10.0 1.3 shard_map.102
  11.3 4.6 %all-to-all-start = ((bf16[8,608,128]{2,1,0:T(8,128)(2,1)}), bf16[8,608,128]{2,1,0:T(8,128)(2,1)S(1)}, u32[]{:S(2)}, u32[]{:S(2)}) async-start(bf16[8,608,128]{2,1,0:T(8,128)(2,1)} %shard_map.102), calls=%async_computation | async-start | bytes 2490368 | tf_op jit(solution)/shard_map/all_to_all | solution.py:483
  15.9 10.1 %collective-permute-done.1.right_ref.refs_1_ = bf16[192,1536]{1,0:T(8,128)(2,1)S(1)} collective-permute-done((bf16[192,1536]{1,0:T(8,128)(2,1)S(1)}, bf16[192,1536]{1,0:T(8,128)(2,1)S(1)}, u32[]{:S(2)}, u32[]{:S(2)}) %collective-permute-start.1) | collective-permute-done | bytes 589856 | tf_op jit(solution)/shard_map/ppermute | solution.py:467
  26.0 3.0 %collective-permute-done.left_ref.refs_0_ = bf16[192,1536]{1,0:T(8,128)(2,1)S(1)} collective-permute-done((bf16[192,1536]{1,0:T(8,128)(2,1)S(1)}, bf16[192,1536]{1,0:T(8,128)(2,1)S(1)}, u32[]{:S(2)}, u32[]{:S(2)}) %collective-permute-start) | collective-permute-done | bytes 589856 | tf_op jit(solution)/shard_map/ppermute | solution.py:467
  29.1 1.2 shard_map.106
  30.3 0.1 copy-done.7
  30.3 3.2 %collective-permute-start.4 = (bf16[96,1536]{1,0:T(8,128)(2,1)}, bf16[96,1536]{1,0:T(8,128)(2,1)S(1)}, u32[]{:S(2)}, u32[]{:S(2)}) collective-permute-start(bf16[96,1536]{1,0:T(8,128)(2,1)} %get-tuple-element.28), channel_id=1, source_target_pairs={{0,14},{2,0},{4,2},{6,4},{8,6},{10,8},{12,10},{14,12},{1,15},{3,1}... | collective-permute-start | bytes 884744 | tf_op jit(solution)/shard_map/ppermute | solution.py:467
  33.6 3.2 %collective-permute-start.11 = (bf16[96,1536]{1,0:T(8,128)(2,1)}, bf16[96,1536]{1,0:T(8,128)(2,1)}, u32[]{:S(2)}, u32[]{:S(2)}) collective-permute-start(bf16[96,1536]{1,0:T(8,128)(2,1)} %get-tuple-element.34), channel_id=1, source_target_pairs={{0,14},{2,0},{4,2},{6,4},{8,6},{10,8},{12,10},{14,12},{1,15},{3,1}... | collective-permute-start | bytes 884744 | tf_op jit(solution)/shard_map/ppermute | solution.py:467
  36.8 16.7 %all-to-all-done.packed_ref._.refs_0_ = bf16[8,608,128]{2,1,0:T(8,128)(2,1)S(1)} async-done(((bf16[8,608,128]{2,1,0:T(8,128)(2,1)}), bf16[8,608,128]{2,1,0:T(8,128)(2,1)S(1)}, u32[]{:S(2)}, u32[]{:S(2)}) %all-to-all-start) | async-done | bytes 1245216 | tf_op jit(solution)/shard_map/all_to_all | solution.py:483
  53.5 1.1 shard_map.103._
  54.5 7.5 %all-to-all-start.1 = ((bf16[16,192,128]{2,1,0:T(8,128)(2,1)}), bf16[16,192,128]{2,1,0:T(8,128)(2,1)S(1)}, u32[]{:S(2)}, u32[]{:S(2)}) async-start(bf16[16,192,128]{2,1,0:T(8,128)(2,1)} %shard_map.103._), calls=%async_computation.1 | async-start | bytes 1572864 | tf_op jit(solution)/shard_map/all_to_all | solution.py:487
  62.1 0.1 collective-permute-start.3
  62.2 3.2 %collective-permute-start.5 = (bf16[96,1536]{1,0:T(8,128)(2,1)S(1)}, bf16[96,1536]{1,0:T(8,128)(2,1)}, u32[]{:S(2)}, u32[]{:S(2)}) collective-permute-start(bf16[96,1536]{1,0:T(8,128)(2,1)S(1)} %collective-permute-done.4.refs_5_), channel_id=1, source_target_pairs={{0,14},{2,0},{4,2},{6,4},{8,6},{10,8},{12,10},{14,12},{1,15},{3,1}... | collective-permute-start | bytes 884744 | tf_op jit(solution)/shard_map/ppermute | solution.py:467
  65.4 0.7 collective-permute-done.10.refs_3_
  66.1 3.2 %collective-permute-start.13 = (bf16[96,1536]{1,0:T(8,128)(2,1)}, bf16[96,1536]{1,0:T(8,128)(2,1)}, u32[]{:S(2)}, u32[]{:S(2)}) collective-permute-start(bf16[96,1536]{1,0:T(8,128)(2,1)} %collective-permute-done.11.refs_4_), channel_id=1, source_target_pairs={{0,14},{2,0},{4,2},{6,4},{8,6},{10,8},{12,10},{14,12},{1,15},{3,1}... | collective-permute-start | bytes 884744 | tf_op jit(solution)/shard_map/ppermute | solution.py:467
  69.3 7.2 %shard_map.104 = (bf16[1536,1536]{1,0:T(8,128)(2,1)}, f32[1,1536]{1,0:T(1,128)S(1)}, f32[128,1536]{1,0:T(8,128)S(1)}, bf16[128,1536]{1,0:T(8,128)(2,1)}) custom-call(s32[1]{0:T(128)S(6)} %copy.13.length_ref, bf16[8,608,128]{2,1,0:T(8,128)(2,1)S(1)} %all-to-all-done.packed_ref._.refs_0_, bf16[16,192,128]{2,1,0:T(8,128)(2,1)} %shard_map.103._), custom_call_target="tpu_custom_call" | custom-call | flops 1207959552 | bytes 4718592 | tf_op jit(solution)/shard_map/pallas_call | solution.py:231
  76.5 0.1 collective-permute-start.9
  76.6 0.1 collective-permute-start.7
  76.7 2.0 %collective-permute-start.6 = (bf16[96,1536]{1,0:T(8,128)(2,1)S(1)}, bf16[96,1536]{1,0:T(8,128)(2,1)}, u32[]{:S(2)}, u32[]{:S(2)}) collective-permute-start(bf16[96,1536]{1,0:T(8,128)(2,1)S(1)} %collective-permute-done.3.refs_6_.refs_12_), channel_id=1, source_target_pairs={{0,2},{2,4},{4,6},{6,8},{8,10},{10,12},{12,14},{14,0},{1,3},{3,5},... | collective-permute-start | bytes 884744 | tf_op jit(solution)/shard_map/ppermute | solution.py:467
  78.7 0.7 copy-done.22
  79.5 0.1 collective-permute-start.8
  79.6 1.1 copy-done.23
  80.7 1.2 collective-permute-done.8.refs_11_.refs_4_
  81.9 2.7 %shard_map.109 = (f32[1152,128]{1,0:T(8,128)S(1)}, bf16[1152,128]{1,0:T(8,128)(2,1)S(1)}) custom-call(bf16[192,1536]{1,0:T(8,128)(2,1)S(1)} %copy-done.8, bf16[192,1536]{1,0:T(8,128)(2,1)S(1)} %copy-done.6, bf16[96,1536]{1,0:T(8,128)(2,1)S(1)} %copy-done.12, bf16[96,1536]{1,0:T(8,128)(2,1)} %collective-permute-done.10.refs_3_, ...), custom_call_target="tpu_custom_call" | custom-call | flops 905969664 | bytes 3538944 | tf_op jit(solution)/shard_map/pallas_call | solution.py:272
  84.6 0.7 copy-done.21
  85.3 1.0 collective-permute-done.7.refs_12_.refs_2_
  86.3 1.4 collective-permute-done.6.refs_11_.refs_1_
  87.6 3.5 %shard_map.110 = (bf16[1536,128]{1,0:T(8,128)(2,1)S(1)}, bf16[1536,128]{1,0:T(8,128)(2,1)S(1)}) custom-call(bf16[128,1536]{1,0:T(8,128)(2,1)} %get-tuple-element.32.own_t_ref, bf16[128,1536]{1,0:T(8,128)(2,1)} %collective-permute-done.9.other_t_ref, f32[1152,128]{1,0:T(8,128)S(1)} %get-tuple-element.35._.refs_4_, bf16[192,1536]{1,0:T(8,128)(2,1)S(1)} %copy-done.8, ...), custom_call_target="tpu_custom_call" | custom-call | flops 1207959552 | bytes 4718592 | tf_op jit(solution)/shard_map/pallas_call | solution.py:297
  91.1 0.1 collective-permute-start.15
  91.2 1.5 shard_map.111
  92.7 0.0 copy-start.13
  92.7 0.2 collective-permute-done.15.got_ref
  92.9 0.9 shard_map.112
  93.8 7.5 %all-to-all-start.2 = ((bf16[16,192,128]{2,1,0:T(8,128)(2,1)}), bf16[16,192,128]{2,1,0:T(8,128)(2,1)S(1)}, u32[]{:S(2)}, u32[]{:S(2)}) async-start(bf16[16,192,128]{2,1,0:T(8,128)(2,1)} %bitcast.1.refs_6_), calls=%async_computation.2 | async-start | bytes 1572864 | tf_op jit(solution)/shard_map/all_to_all | solution.py:504
  101.3 0.5 collective-permute-start.14
  101.8 1.3 collective-permute-done.16.refs_5_
  103.1 6.0 %shard_map.113 = (bf16[1152,128]{1,0:T(8,128)(2,1)S(1)}, f32[1536,128]{1,0:T(8,128)S(1)}, f32[1536,128]{1,0:T(8,128)S(1)}) custom-call(bf16[8,608,128]{2,1,0:T(8,128)(2,1)S(1)} %all-to-all-done.packed_ref._.refs_0_, bf16[1536,1536]{1,0:T(8,128)(2,1)} %get-tuple-element.24.refs_1_, f32[1,1536]{1,0:T(1,128)S(1)} %get-tuple-element.25.refs_2_, ...), custom_call_target="tpu_custom_call" | custom-call | flops 1811939328 | bytes 3538944 | tf_op jit(solution)/shard_map/pallas_call | solution.py:437
  109.2 3.2 %shard_map.114.grads_ref = bf16[8,608,128]{2,1,0:T(8,128)(2,1)S(1)} custom-call(bf16[8,608,128]{2,1,0:T(8,128)(2,1)} %copy-done, bf16[1536,1536]{1,0:T(8,128)(2,1)} %get-tuple-element.24.refs_1_, f32[1,1536]{1,0:T(1,128)S(1)} %get-tuple-element.25.refs_2_, f32[128,1536]{1,0:T(8,128)S(1)} %get-tuple-element.26.refs_3_, f32[384,128]{1,0:T(8,128)S(1)} %copy-done.14, ...), custom_call_target="tpu_custom_call" | custom-call | flops 603979776 | bytes 1179648 | tf_op jit(solution)/shard_map/pallas_call | solution.py:437
  112.3 2.5 %all-to-all-done.2.parts_ref = bf16[16,192,128]{2,1,0:T(8,128)(2,1)S(1)} async-done(((bf16[16,192,128]{2,1,0:T(8,128)(2,1)}), bf16[16,192,128]{2,1,0:T(8,128)(2,1)S(1)}, u32[]{:S(2)}, u32[]{:S(2)}) %all-to-all-start.2) | async-done | bytes 786464 | tf_op jit(solution)/shard_map/all_to_all | solution.py:504
  114.8 0.1 shard_map.115
  115.0 34.7 %all_to_all.20.packed_ref = bf16[8,608,128]{2,1,0:T(8,128)(2,1)S(1)} all-to-all(bf16[8,608,128]{2,1,0:T(8,128)(2,1)S(1)} %shard_map.115), channel_id=1, replica_groups=mesh['dp'=16,'seq'=8,'tensor'=2] {'seq'}, dimensions={0} | all-to-all | bytes 2490368 | tf_op jit(solution)/shard_map/all_to_all | solution.py:509
  149.7 1.8 %shard_map.116 = (bf16[192,1024]{1,0:T(8,128)(2,1)}, bf16[192,1024]{1,0:T(8,128)(2,1)}, bf16[192,1024]{1,0:T(8,128)(2,1)}, f32[24,1024]{1,0:T(8,128)}) custom-call(bf16[8,608,128]{2,1,0:T(8,128)(2,1)S(1)} %all_to_all.20.packed_ref), custom_call_target="tpu_custom_call" | custom-call | bytes 2490368 | tf_op jit(solution)/shard_map/pallas_call | solution.py:120
  (56 shorter events, 0.2 us)
Async XLA Ops:
  1.3 1.1 copy-start.15
  2.3 0.7 copy-start.20
  3.1 6.1 %copy-start.16 = (bf16[192,1024]{1,0:T(8,128)(2,1)S(1)}, bf16[192,1024]{1,0:T(8,128)(2,1)}, u32[]{:S(2)}) copy-start(bf16[192,1024]{1,0:T(8,128)(2,1)} %query_ref.1) | copy-start | bytes 1179652
  3.1 6.1 %copy-start.17 = (bf16[192,1024]{1,0:T(8,128)(2,1)S(1)}, bf16[192,1024]{1,0:T(8,128)(2,1)}, u32[]{:S(2)}) copy-start(bf16[192,1024]{1,0:T(8,128)(2,1)} %key_ref.1) | copy-start | bytes 1179652
  3.1 6.1 %copy-start.18 = (bf16[192,1024]{1,0:T(8,128)(2,1)S(1)}, bf16[192,1024]{1,0:T(8,128)(2,1)}, u32[]{:S(2)}) copy-start(bf16[192,1024]{1,0:T(8,128)(2,1)} %value_ref.1) | copy-start | bytes 1179652
  3.2 8.1 %copy-start.1 = (bf16[192,1536]{1,0:T(8,128)(2,1)}, bf16[192,1536]{1,0:T(8,128)(2,1)S(1)}, u32[]{:S(2)}) copy-start(bf16[192,1536]{1,0:T(8,128)(2,1)S(1)} %shard_map.105.refs_10_.refs_0_) | copy-start | bytes 1769476
  3.2 22.8 %collective-permute-start.1 = (bf16[192,1536]{1,0:T(8,128)(2,1)S(1)}, bf16[192,1536]{1,0:T(8,128)(2,1)S(1)}, u32[]{:S(2)}, u32[]{:S(2)}) collective-permute-start(bf16[192,1536]{1,0:T(8,128)(2,1)S(1)} %shard_map.105.refs_10_.refs_0_), channel_id=1, source_target_pairs={{0,14},{2,0},{4,2},{6,4},{8,6},{10,8},{12,10},{14,12},{1,15},{3,1}... | collective-permute-start | bytes 1769480 | tf_op jit(solution)/shard_map/ppermute | solution.py:467
  9.2 19.9 %collective-permute-start = (bf16[192,1536]{1,0:T(8,128)(2,1)S(1)}, bf16[192,1536]{1,0:T(8,128)(2,1)S(1)}, u32[]{:S(2)}, u32[]{:S(2)}) collective-permute-start(bf16[192,1536]{1,0:T(8,128)(2,1)S(1)} %shard_map.105.refs_10_.refs_0_), channel_id=1, source_target_pairs={{0,2},{2,4},{4,6},{6,8},{8,10},{10,12},{12,14},{14,0},{1,3},{3,5},... | collective-permute-start | bytes 1769480 | tf_op jit(solution)/shard_map/ppermute | solution.py:467
  9.2 0.8 copy-start.19
  11.3 42.2 %all-to-all-start = ((bf16[8,608,128]{2,1,0:T(8,128)(2,1)}), bf16[8,608,128]{2,1,0:T(8,128)(2,1)S(1)}, u32[]{:S(2)}, u32[]{:S(2)}) async-start(bf16[8,608,128]{2,1,0:T(8,128)(2,1)} %shard_map.102), calls=%async_computation | async-start | bytes 2490368 | tf_op jit(solution)/shard_map/all_to_all | solution.py:483
  26.0 4.2 %copy-start.5 = (bf16[192,1536]{1,0:T(8,128)(2,1)}, bf16[192,1536]{1,0:T(8,128)(2,1)S(1)}, u32[]{:S(2)}) copy-start(bf16[192,1536]{1,0:T(8,128)(2,1)S(1)} %collective-permute-done.1.right_ref.refs_1_) | copy-start | bytes 1769476
  29.1 1.3 copy-start.7
  30.3 31.7 %collective-permute-start.2 = (bf16[96,1536]{1,0:T(8,128)(2,1)}, bf16[96,1536]{1,0:T(8,128)(2,1)S(1)}, u32[]{:S(2)}, u32[]{:S(2)}) collective-permute-start(bf16[96,1536]{1,0:T(8,128)(2,1)} %get-tuple-element.27), channel_id=1, source_target_pairs={{0,2},{2,4},{4,6},{6,8},{8,10},{10,12},{12,14},{14,0},{1,3},{3,5},... | collective-permute-start | bytes 884744 | tf_op jit(solution)/shard_map/ppermute | solution.py:467
  30.3 31.8 %collective-permute-start.4 = (bf16[96,1536]{1,0:T(8,128)(2,1)}, bf16[96,1536]{1,0:T(8,128)(2,1)S(1)}, u32[]{:S(2)}, u32[]{:S(2)}) collective-permute-start(bf16[96,1536]{1,0:T(8,128)(2,1)} %get-tuple-element.28), channel_id=1, source_target_pairs={{0,14},{2,0},{4,2},{6,4},{8,6},{10,8},{12,10},{14,12},{1,15},{3,1}... | collective-permute-start | bytes 884744 | tf_op jit(solution)/shard_map/ppermute | solution.py:467
  33.6 32.5 %collective-permute-start.10 = (bf16[96,1536]{1,0:T(8,128)(2,1)}, bf16[96,1536]{1,0:T(8,128)(2,1)}, u32[]{:S(2)}, u32[]{:S(2)}) collective-permute-start(bf16[96,1536]{1,0:T(8,128)(2,1)} %get-tuple-element.33), channel_id=1, source_target_pairs={{0,2},{2,4},{4,6},{6,8},{8,10},{10,12},{12,14},{14,0},{1,3},{3,5},... | collective-permute-start | bytes 884744 | tf_op jit(solution)/shard_map/ppermute | solution.py:467
  33.6 32.5 %collective-permute-start.11 = (bf16[96,1536]{1,0:T(8,128)(2,1)}, bf16[96,1536]{1,0:T(8,128)(2,1)}, u32[]{:S(2)}, u32[]{:S(2)}) collective-permute-start(bf16[96,1536]{1,0:T(8,128)(2,1)} %get-tuple-element.34), channel_id=1, source_target_pairs={{0,14},{2,0},{4,2},{6,4},{8,6},{10,8},{12,10},{14,12},{1,15},{3,1}... | collective-permute-start | bytes 884744 | tf_op jit(solution)/shard_map/ppermute | solution.py:467
  53.5 49.6 %copy-start = (bf16[8,608,128]{2,1,0:T(8,128)(2,1)}, bf16[8,608,128]{2,1,0:T(8,128)(2,1)S(1)}, u32[]{:S(2)}) copy-start(bf16[8,608,128]{2,1,0:T(8,128)(2,1)S(1)} %all-to-all-done.packed_ref._.refs_0_) | copy-start | bytes 3735556
  54.5 24.9 %all-to-all-start.1 = ((bf16[16,192,128]{2,1,0:T(8,128)(2,1)}), bf16[16,192,128]{2,1,0:T(8,128)(2,1)S(1)}, u32[]{:S(2)}, u32[]{:S(2)}) async-start(bf16[16,192,128]{2,1,0:T(8,128)(2,1)} %shard_map.103._), calls=%async_computation.1 | async-start | bytes 1572864 | tf_op jit(solution)/shard_map/all_to_all | solution.py:487
  62.1 14.4 %copy-start.11 = (bf16[96,1536]{1,0:T(8,128)(2,1)}, bf16[96,1536]{1,0:T(8,128)(2,1)S(1)}, u32[]{:S(2)}) copy-start(bf16[96,1536]{1,0:T(8,128)(2,1)S(1)} %shard_map.107.refs_2_) | copy-start | bytes 884740
  62.1 14.5 %collective-permute-start.3 = (bf16[96,1536]{1,0:T(8,128)(2,1)S(1)}, bf16[96,1536]{1,0:T(8,128)(2,1)S(1)}, u32[]{:S(2)}, u32[]{:S(2)}) collective-permute-start(bf16[96,1536]{1,0:T(8,128)(2,1)S(1)} %shard_map.107.refs_2_), channel_id=1, source_target_pairs={{0,2},{2,4},{4,6},{6,8},{8,10},{10,12},{12,14},{14,0},{1,3},{3,5},... | collective-permute-start | bytes 884744 | tf_op jit(solution)/shard_map/ppermute | solution.py:467
  62.2 14.3 %copy-start.9 = (bf16[96,1536]{1,0:T(8,128)(2,1)}, bf16[96,1536]{1,0:T(8,128)(2,1)S(1)}, u32[]{:S(2)}) copy-start(bf16[96,1536]{1,0:T(8,128)(2,1)S(1)} %collective-permute-done.4.refs_5_) | copy-start | bytes 884740
  62.2 14.4 %collective-permute-start.5 = (bf16[96,1536]{1,0:T(8,128)(2,1)S(1)}, bf16[96,1536]{1,0:T(8,128)(2,1)}, u32[]{:S(2)}, u32[]{:S(2)}) collective-permute-start(bf16[96,1536]{1,0:T(8,128)(2,1)S(1)} %collective-permute-done.4.refs_5_), channel_id=1, source_target_pairs={{0,14},{2,0},{4,2},{6,4},{8,6},{10,8},{12,10},{14,12},{1,15},{3,1}... | collective-permute-start | bytes 884744 | tf_op jit(solution)/shard_map/ppermute | solution.py:467
  66.0 12.7 %collective-permute-start.12 = (bf16[96,1536]{1,0:T(8,128)(2,1)}, bf16[96,1536]{1,0:T(8,128)(2,1)S(1)}, u32[]{:S(2)}, u32[]{:S(2)}) collective-permute-start(bf16[96,1536]{1,0:T(8,128)(2,1)} %collective-permute-done.10.refs_3_), channel_id=1, source_target_pairs={{0,2},{2,4},{4,6},{6,8},{8,10},{10,12},{12,14},{14,0},{1,3},{3,5},... | collective-permute-start | bytes 884744 | tf_op jit(solution)/shard_map/ppermute | solution.py:467
  66.1 14.6 %collective-permute-start.13 = (bf16[96,1536]{1,0:T(8,128)(2,1)}, bf16[96,1536]{1,0:T(8,128)(2,1)}, u32[]{:S(2)}, u32[]{:S(2)}) collective-permute-start(bf16[96,1536]{1,0:T(8,128)(2,1)} %collective-permute-done.11.refs_4_), channel_id=1, source_target_pairs={{0,14},{2,0},{4,2},{6,4},{8,6},{10,8},{12,10},{14,12},{1,15},{3,1}... | collective-permute-start | bytes 884744 | tf_op jit(solution)/shard_map/ppermute | solution.py:467
  76.5 11.1 %collective-permute-start.9 = (bf16[128,1536]{1,0:T(8,128)(2,1)}, bf16[128,1536]{1,0:T(8,128)(2,1)}, u32[]{:S(2)}, u32[]{:S(2)}) collective-permute-start(bf16[128,1536]{1,0:T(8,128)(2,1)} %get-tuple-element.32.own_t_ref), channel_id=1, source_target_pairs={{0,1},{1,0},{2,3},{3,2},{4,5},{5,4},{6,7},{7,6},{8,9},{9,8},{10,11... | collective-permute-start | bytes 1179656 | tf_op jit(solution)/shard_map/ppermute | solution.py:491
  76.6 9.6 %collective-permute-start.7 = (bf16[96,1536]{1,0:T(8,128)(2,1)}, bf16[96,1536]{1,0:T(8,128)(2,1)S(1)}, u32[]{:S(2)}, u32[]{:S(2)}) collective-permute-start(bf16[96,1536]{1,0:T(8,128)(2,1)} %collective-permute-done.5.refs_9_), channel_id=1, source_target_pairs={{0,14},{2,0},{4,2},{6,4},{8,6},{10,8},{12,10},{14,12},{1,15},{3,1}... | collective-permute-start | bytes 884744 | tf_op jit(solution)/shard_map/ppermute | solution.py:467
  76.7 10.9 %collective-permute-start.6 = (bf16[96,1536]{1,0:T(8,128)(2,1)S(1)}, bf16[96,1536]{1,0:T(8,128)(2,1)}, u32[]{:S(2)}, u32[]{:S(2)}) collective-permute-start(bf16[96,1536]{1,0:T(8,128)(2,1)S(1)} %collective-permute-done.3.refs_6_.refs_12_), channel_id=1, source_target_pairs={{0,2},{2,4},{4,6},{6,8},{8,10},{10,12},{12,14},{14,0},{1,3},{3,5},... | collective-permute-start | bytes 884744 | tf_op jit(solution)/shard_map/ppermute | solution.py:467
  78.7 0.7 copy-start.22
  79.4 2.4 %copy-start.6 = (bf16[192,1536]{1,0:T(8,128)(2,1)S(1)}, bf16[192,1536]{1,0:T(8,128)(2,1)}, u32[]{:S(2)}) copy-start(bf16[192,1536]{1,0:T(8,128)(2,1)} %copy-done.5) | copy-start | bytes 1769476
  79.5 2.4 %copy-start.8 = (bf16[192,1536]{1,0:T(8,128)(2,1)S(1)}, bf16[192,1536]{1,0:T(8,128)(2,1)}, u32[]{:S(2)}) copy-start(bf16[192,1536]{1,0:T(8,128)(2,1)} %copy-done.7) | copy-start | bytes 1769476
  79.5 2.4 %copy-start.10 = (bf16[96,1536]{1,0:T(8,128)(2,1)S(1)}, bf16[96,1536]{1,0:T(8,128)(2,1)}, u32[]{:S(2)}) copy-start(bf16[96,1536]{1,0:T(8,128)(2,1)} %copy-done.9) | copy-start | bytes 884740
  79.5 2.4 %copy-start.12 = (bf16[96,1536]{1,0:T(8,128)(2,1)S(1)}, bf16[96,1536]{1,0:T(8,128)(2,1)}, u32[]{:S(2)}) copy-start(bf16[96,1536]{1,0:T(8,128)(2,1)} %copy-done.11) | copy-start | bytes 884740
  79.5 2.4 %collective-permute-start.8 = (bf16[3072,128]{1,0:T(8,128)(2,1)S(1)}, bf16[3072,128]{1,0:T(8,128)(2,1)S(1)}, u32[]{:S(2)}, u32[]{:S(2)}) collective-permute-start(bf16[3072,128]{1,0:T(8,128)(2,1)S(1)} %bitcast.2), channel_id=1, source_target_pairs={{0,1},{1,0},{2,3},{3,2},{4,5},{5,4},{6,7},{7,6},{8,9},{9,8},{10,11... | collective-permute-start | bytes 2359304 | tf_op jit(solution)/shard_map/ppermute | solution.py:488
  79.6 1.1 copy-start.23
  84.6 0.7 copy-start.21
  85.3 5.8 %copy-start.3 = (f32[1152,128]{1,0:T(8,128)}, f32[1152,128]{1,0:T(8,128)S(1)}, u32[]{:S(2)}) copy-start(f32[1152,128]{1,0:T(8,128)S(1)} %get-tuple-element.35._.refs_4_) | copy-start | bytes 1769476
  87.6 3.6 %copy-start.2 = (bf16[192,1536]{1,0:T(8,128)(2,1)S(1)}, bf16[192,1536]{1,0:T(8,128)(2,1)}, u32[]{:S(2)}) copy-start(bf16[192,1536]{1,0:T(8,128)(2,1)} %copy-done.1) | copy-start | bytes 1769476
  91.1 1.8 %collective-permute-start.15 = (bf16[1536,128]{1,0:T(8,128)(2,1)S(1)}, bf16[1536,128]{1,0:T(8,128)(2,1)S(1)}, u32[]{:S(2)}, u32[]{:S(2)}) collective-permute-start(bf16[1536,128]{1,0:T(8,128)(2,1)S(1)} %get-tuple-element.39), channel_id=1, source_target_pairs={{0,1},{1,0},{2,3},{3,2},{4,5},{5,4},{6,7},{7,6},{8,9},{9,8},{10,11... | collective-permute-start | bytes 1179656 | tf_op jit(solution)/shard_map/ppermute | solution.py:500
  92.7 1.1 copy-start.13
  92.9 10.2 %copy-start.4 = (f32[1152,128]{1,0:T(8,128)S(1)}, f32[1152,128]{1,0:T(8,128)}, u32[]{:S(2)}) copy-start(f32[1152,128]{1,0:T(8,128)} %copy-done.3) | copy-start | bytes 1769476
  93.8 21.0 %all-to-all-start.2 = ((bf16[16,192,128]{2,1,0:T(8,128)(2,1)}), bf16[16,192,128]{2,1,0:T(8,128)(2,1)S(1)}, u32[]{:S(2)}, u32[]{:S(2)}) async-start(bf16[16,192,128]{2,1,0:T(8,128)(2,1)} %bitcast.1.refs_6_), calls=%async_computation.2 | async-start | bytes 1572864 | tf_op jit(solution)/shard_map/all_to_all | solution.py:504
  101.3 1.8 %collective-permute-start.16 = (bf16[1152,128]{1,0:T(8,128)(2,1)}, bf16[1152,128]{1,0:T(8,128)(2,1)S(1)}, u32[]{:S(2)}, u32[]{:S(2)}) collective-permute-start(bf16[1152,128]{1,0:T(8,128)(2,1)} %copy-done.21), channel_id=1, source_target_pairs={{0,1},{1,0},{2,3},{3,2},{4,5},{5,4},{6,7},{7,6},{8,9},{9,8},{10,11... | collective-permute-start | bytes 884744 | tf_op jit(solution)/shard_map/ppermute | solution.py:498
  101.3 7.8 %collective-permute-start.14 = (bf16[384,128]{1,0:T(8,128)(2,1)S(1)}, bf16[384,128]{1,0:T(8,128)(2,1)S(1)}, u32[]{:S(2)}, u32[]{:S(2)}) collective-permute-start(bf16[384,128]{1,0:T(8,128)(2,1)S(1)} %get-tuple-element.38), channel_id=1, source_target_pairs={{0,1},{1,0},{2,3},{3,2},{4,5},{5,4},{6,7},{7,6},{8,9},{9,8},{10,11... | collective-permute-start | bytes 294920 | tf_op jit(solution)/shard_map/ppermute | solution.py:502
  103.1 6.0 %copy-start.14 = (f32[384,128]{1,0:T(8,128)S(1)}, f32[384,128]{1,0:T(8,128)}, u32[]{:S(2)}) copy-start(f32[384,128]{1,0:T(8,128)} %copy-done.13) | copy-start | bytes 589828

commit v7 on v6

--- a/solution.py
+++ b/solution.py
@@ -11,6 +11,7 @@
 HD = 128
 HOLD1, HOLD2, HOLD3, PACK = 100, 100, 100, 24
 PAIR = 2
+WIDE = 4
 FBLOCK = 256
 MIB = 1024 * 1024
 BF16 = jnp.bfloat16
@@ -199,7 +200,7 @@
 
     keys = packed_ref[:, rows : 2 * rows, :].reshape(total, HD)
     block = jnp.concatenate(
-        [packed_ref[slot_of(PAIR * step + i, slots), 0:rows, :] for i in range(PAIR)], axis=0
+        [packed_ref[slot_of(WIDE * step + i, slots), 0:rows, :] for i in range(WIDE)], axis=0
     )
     scores_ref[...] = lax.dot_general(keys, block, NT, preferred_element_type=F32)
     width = block.shape[0]
@@ -227,10 +228,10 @@
 def attend_forward(packed, lengths, rows, after):
     slots = packed.shape[0]
     total = slots * rows
-    width = PAIR * rows
+    width = WIDE * rows
     return pl.pallas_call(
         functools.partial(forward_kernel, rows),
-        grid=(slots // PAIR,),
+        grid=(slots // WIDE,),
         out_shape=[
             jax.ShapeDtypeStruct((total, total), BF16),
             jax.ShapeDtypeStruct((1, total), F32),

time: 152 us -> 151 us (level)
  transfers between devices with their start and end apart: 20 -> 20, of which waited for: 10 -> 10; matrix products, arithmetic and copies ran while one was open for 0% -> 0% of each run, Pallas kernels for 16% -> 15%
where the time goes in v7:
time: 151 us; the launch traced here: 150 us
  starting transfers between devices  41.4 us (27%)
  waiting for transfers between devices  38 us (25%)
  blocking collectives  34.7 us (23%)
  Pallas kernels  29.4 us (19%)
  local copies, waits for them, and re-layouts  5.17 us (3%)
  between operations  1.75 us (1%)
    all_to_all x1, blocking collectives, per_device(): lax.all_to_all(result, 'seq', split_axis=0, concat_axis=0, tiled=True)  34.7 us
    ppermute x12, starting transfers between devices, move(): return lax.ppermute(array, 'seq', right if step > 0 else left)  21 us
    all_to_all x1, waiting for transfers between devices, per_device(): lax.all_to_all(pack(queries, keys, values, proj_weight, seq), 'seq', spli...  16.7 us
    ppermute x12, waiting for transfers between devices, move(): return lax.ppermute(array, 'seq', right if step > 0 else left)  16.2 us
    pallas_call x2, Pallas kernels, attend_backward(): pl.pallas_call(functools.partial(backward_kernel, rows, start, first, las...  9.19 us
    all_to_all x1, starting transfers between devices, per_device(): lax.all_to_all(joined, 'dp', split_axis=0, concat_axis=0, tiled=True)  7.49 us
    all_to_all x1, starting transfers between devices, per_device(): lax.all_to_all(copies, 'dp', split_axis=0, concat_axis=0, tiled=True)  7.48 us
    pallas_call x1, Pallas kernels, attend_forward(): pl.pallas_call(functools.partial(forward_kernel, rows), grid=(slots // WI...  6.08 us
  transfers between devices with their start and end apart: 20, of which 10 were waited for; matrix products, arithmetic and copies ran while one was open for 0% of the time, Pallas kernels for 15%

profile of v7, /device:TPU:2, one launch (start us, length us, event | category | flops | bytes accessed | tf_op | source)
XLA Modules:
  0.0 150.5 jit_solution(17988915087909397906)
XLA Ops:
  1.3 1.1 copy-done.15
  2.3 0.7 copy-done.20
  3.1 0.1 shard_map.105.refs_10_.refs_0_
  3.2 5.9 %collective-permute-start.1 = (bf16[192,1536]{1,0:T(8,128)(2,1)S(1)}, bf16[192,1536]{1,0:T(8,128)(2,1)S(1)}, u32[]{:S(2)}, u32[]{:S(2)}) collective-permute-start(bf16[192,1536]{1,0:T(8,128)(2,1)S(1)} %shard_map.105.refs_10_.refs_0_), channel_id=1, source_target_pairs={{0,14},{2,0},{4,2},{6,4},{8,6},{10,8},{12,10},{14,12},{1,15},{3,1}... | collective-permute-start | bytes 1769480 | tf_op jit(solution)/shard_map/ppermute | solution.py:468
  9.2 0.0 copy-start.19
  9.2 0.8 copy-done.19
  10.0 1.3 shard_map.102
  11.3 4.6 %all-to-all-start = ((bf16[8,608,128]{2,1,0:T(8,128)(2,1)}), bf16[8,608,128]{2,1,0:T(8,128)(2,1)S(1)}, u32[]{:S(2)}, u32[]{:S(2)}) async-start(bf16[8,608,128]{2,1,0:T(8,128)(2,1)} %shard_map.102), calls=%async_computation | async-start | bytes 2490368 | tf_op jit(solution)/shard_map/all_to_all | solution.py:484
  15.9 10.1 %collective-permute-done.1.right_ref.refs_1_ = bf16[192,1536]{1,0:T(8,128)(2,1)S(1)} collective-permute-done((bf16[192,1536]{1,0:T(8,128)(2,1)S(1)}, bf16[192,1536]{1,0:T(8,128)(2,1)S(1)}, u32[]{:S(2)}, u32[]{:S(2)}) %collective-permute-start.1) | collective-permute-done | bytes 589856 | tf_op jit(solution)/shard_map/ppermute | solution.py:468
  26.0 3.0 %collective-permute-done.left_ref.refs_0_ = bf16[192,1536]{1,0:T(8,128)(2,1)S(1)} collective-permute-done((bf16[192,1536]{1,0:T(8,128)(2,1)S(1)}, bf16[192,1536]{1,0:T(8,128)(2,1)S(1)}, u32[]{:S(2)}, u32[]{:S(2)}) %collective-permute-start) | collective-permute-done | bytes 589856 | tf_op jit(solution)/shard_map/ppermute | solution.py:468
  29.1 1.2 shard_map.106
  30.3 0.1 copy-done.7
  30.3 3.2 %collective-permute-start.4 = (bf16[96,1536]{1,0:T(8,128)(2,1)}, bf16[96,1536]{1,0:T(8,128)(2,1)S(1)}, u32[]{:S(2)}, u32[]{:S(2)}) collective-permute-start(bf16[96,1536]{1,0:T(8,128)(2,1)} %get-tuple-element.28), channel_id=1, source_target_pairs={{0,14},{2,0},{4,2},{6,4},{8,6},{10,8},{12,10},{14,12},{1,15},{3,1}... | collective-permute-start | bytes 884744 | tf_op jit(solution)/shard_map/ppermute | solution.py:468
  33.6 3.2 %collective-permute-start.11 = (bf16[96,1536]{1,0:T(8,128)(2,1)}, bf16[96,1536]{1,0:T(8,128)(2,1)}, u32[]{:S(2)}, u32[]{:S(2)}) collective-permute-start(bf16[96,1536]{1,0:T(8,128)(2,1)} %get-tuple-element.34), channel_id=1, source_target_pairs={{0,14},{2,0},{4,2},{6,4},{8,6},{10,8},{12,10},{14,12},{1,15},{3,1}... | collective-permute-start | bytes 884744 | tf_op jit(solution)/shard_map/ppermute | solution.py:468
  36.8 16.7 %all-to-all-done.packed_ref._.refs_0_ = bf16[8,608,128]{2,1,0:T(8,128)(2,1)S(1)} async-done(((bf16[8,608,128]{2,1,0:T(8,128)(2,1)}), bf16[8,608,128]{2,1,0:T(8,128)(2,1)S(1)}, u32[]{:S(2)}, u32[]{:S(2)}) %all-to-all-start) | async-done | bytes 1245216 | tf_op jit(solution)/shard_map/all_to_all | solution.py:484
  53.5 1.1 shard_map.103._
  54.5 7.5 %all-to-all-start.1 = ((bf16[16,192,128]{2,1,0:T(8,128)(2,1)}), bf16[16,192,128]{2,1,0:T(8,128)(2,1)S(1)}, u32[]{:S(2)}, u32[]{:S(2)}) async-start(bf16[16,192,128]{2,1,0:T(8,128)(2,1)} %shard_map.103._), calls=%async_computation.1 | async-start | bytes 1572864 | tf_op jit(solution)/shard_map/all_to_all | solution.py:488
  62.1 0.1 collective-permute-start.3
  62.2 3.2 %collective-permute-start.5 = (bf16[96,1536]{1,0:T(8,128)(2,1)S(1)}, bf16[96,1536]{1,0:T(8,128)(2,1)}, u32[]{:S(2)}, u32[]{:S(2)}) collective-permute-start(bf16[96,1536]{1,0:T(8,128)(2,1)S(1)} %collective-permute-done.4.refs_5_), channel_id=1, source_target_pairs={{0,14},{2,0},{4,2},{6,4},{8,6},{10,8},{12,10},{14,12},{1,15},{3,1}... | collective-permute-start | bytes 884744 | tf_op jit(solution)/shard_map/ppermute | solution.py:468
  65.4 0.7 collective-permute-done.10.refs_3_
  66.1 3.2 %collective-permute-start.13 = (bf16[96,1536]{1,0:T(8,128)(2,1)}, bf16[96,1536]{1,0:T(8,128)(2,1)}, u32[]{:S(2)}, u32[]{:S(2)}) collective-permute-start(bf16[96,1536]{1,0:T(8,128)(2,1)} %collective-permute-done.11.refs_4_), channel_id=1, source_target_pairs={{0,14},{2,0},{4,2},{6,4},{8,6},{10,8},{12,10},{14,12},{1,15},{3,1}... | collective-permute-start | bytes 884744 | tf_op jit(solution)/shard_map/ppermute | solution.py:468
  69.3 6.1 %shard_map.104 = (bf16[1536,1536]{1,0:T(8,128)(2,1)}, f32[1,1536]{1,0:T(1,128)S(1)}, f32[128,1536]{1,0:T(8,128)S(1)}, bf16[128,1536]{1,0:T(8,128)(2,1)}) custom-call(s32[1]{0:T(128)S(6)} %copy.13.length_ref, bf16[8,608,128]{2,1,0:T(8,128)(2,1)S(1)} %all-to-all-done.packed_ref._.refs_0_, bf16[16,192,128]{2,1,0:T(8,128)(2,1)} %shard_map.103._), custom_call_target="tpu_custom_call" | custom-call | flops 1207959552 | bytes 4718592 | tf_op jit(solution)/shard_map/pallas_call | solution.py:232
  75.4 0.1 collective-permute-start.9
  75.5 1.1 collective-permute-start.7
  76.6 1.1 collective-permute-start.6
  77.6 0.7 copy-done.22
  78.3 0.1 collective-permute-start.8
  78.5 1.1 copy-done.23
  79.6 1.2 collective-permute-done.8.refs_11_.refs_4_
  80.7 2.7 %shard_map.109 = (f32[1152,128]{1,0:T(8,128)S(1)}, bf16[1152,128]{1,0:T(8,128)(2,1)S(1)}) custom-call(bf16[192,1536]{1,0:T(8,128)(2,1)S(1)} %copy-done.8, bf16[192,1536]{1,0:T(8,128)(2,1)S(1)} %copy-done.6, bf16[96,1536]{1,0:T(8,128)(2,1)S(1)} %copy-done.12, bf16[96,1536]{1,0:T(8,128)(2,1)} %collective-permute-done.10.refs_3_, ...), custom_call_target="tpu_custom_call" | custom-call | flops 905969664 | bytes 3538944 | tf_op jit(solution)/shard_map/pallas_call | solution.py:273
  83.4 0.7 copy-done.21
  84.1 1.0 collective-permute-done.7.refs_12_.refs_2_
  85.1 1.3 collective-permute-done.6.refs_11_.refs_1_
  86.5 3.5 %shard_map.110 = (bf16[1536,128]{1,0:T(8,128)(2,1)S(1)}, bf16[1536,128]{1,0:T(8,128)(2,1)S(1)}) custom-call(bf16[128,1536]{1,0:T(8,128)(2,1)} %get-tuple-element.32.own_t_ref, bf16[128,1536]{1,0:T(8,128)(2,1)} %collective-permute-done.9.other_t_ref, f32[1152,128]{1,0:T(8,128)S(1)} %get-tuple-element.35._.refs_4_, bf16[192,1536]{1,0:T(8,128)(2,1)S(1)} %copy-done.8, ...), custom_call_target="tpu_custom_call" | custom-call | flops 1207959552 | bytes 4718592 | tf_op jit(solution)/shard_map/pallas_call | solution.py:298
  90.0 0.1 collective-permute-start.15
  90.1 1.5 shard_map.111
  91.5 0.0 copy-start.13
  91.6 0.2 collective-permute-done.15.got_ref
  91.8 0.9 shard_map.112
  92.7 7.5 %all-to-all-start.2 = ((bf16[16,192,128]{2,1,0:T(8,128)(2,1)}), bf16[16,192,128]{2,1,0:T(8,128)(2,1)S(1)}, u32[]{:S(2)}, u32[]{:S(2)}) async-start(bf16[16,192,128]{2,1,0:T(8,128)(2,1)} %bitcast.1.refs_6_), calls=%async_computation.2 | async-start | bytes 1572864 | tf_op jit(solution)/shard_map/all_to_all | solution.py:505
  100.2 0.5 collective-permute-start.14
  100.7 1.3 collective-permute-done.16.refs_5_
  102.0 6.0 %shard_map.113 = (bf16[1152,128]{1,0:T(8,128)(2,1)S(1)}, f32[1536,128]{1,0:T(8,128)S(1)}, f32[1536,128]{1,0:T(8,128)S(1)}) custom-call(bf16[8,608,128]{2,1,0:T(8,128)(2,1)S(1)} %all-to-all-done.packed_ref._.refs_0_, bf16[1536,1536]{1,0:T(8,128)(2,1)} %get-tuple-element.24.refs_1_, f32[1,1536]{1,0:T(1,128)S(1)} %get-tuple-element.25.refs_2_, ...), custom_call_target="tpu_custom_call" | custom-call | flops 1811939328 | bytes 3538944 | tf_op jit(solution)/shard_map/pallas_call | solution.py:438
  108.0 3.2 %shard_map.114.grads_ref = bf16[8,608,128]{2,1,0:T(8,128)(2,1)S(1)} custom-call(bf16[8,608,128]{2,1,0:T(8,128)(2,1)} %copy-done, bf16[1536,1536]{1,0:T(8,128)(2,1)} %get-tuple-element.24.refs_1_, f32[1,1536]{1,0:T(1,128)S(1)} %get-tuple-element.25.refs_2_, f32[128,1536]{1,0:T(8,128)S(1)} %get-tuple-element.26.refs_3_, f32[384,128]{1,0:T(8,128)S(1)} %copy-done.14, ...), custom_call_target="tpu_custom_call" | custom-call | flops 603979776 | bytes 1179648 | tf_op jit(solution)/shard_map/pallas_call | solution.py:438
  111.2 2.5 %all-to-all-done.2.parts_ref = bf16[16,192,128]{2,1,0:T(8,128)(2,1)S(1)} async-done(((bf16[16,192,128]{2,1,0:T(8,128)(2,1)}), bf16[16,192,128]{2,1,0:T(8,128)(2,1)S(1)}, u32[]{:S(2)}, u32[]{:S(2)}) %all-to-all-start.2) | async-done | bytes 786464 | tf_op jit(solution)/shard_map/all_to_all | solution.py:505
  113.7 0.1 shard_map.115
  113.8 34.7 %all_to_all.20.packed_ref = bf16[8,608,128]{2,1,0:T(8,128)(2,1)S(1)} all-to-all(bf16[8,608,128]{2,1,0:T(8,128)(2,1)S(1)} %shard_map.115), channel_id=1, replica_groups=mesh['dp'=16,'seq'=8,'tensor'=2] {'seq'}, dimensions={0} | all-to-all | bytes 2490368 | tf_op jit(solution)/shard_map/all_to_all | solution.py:510
  148.5 1.8 %shard_map.116 = (bf16[192,1024]{1,0:T(8,128)(2,1)}, bf16[192,1024]{1,0:T(8,128)(2,1)}, bf16[192,1024]{1,0:T(8,128)(2,1)}, f32[24,1024]{1,0:T(8,128)}) custom-call(bf16[8,608,128]{2,1,0:T(8,128)(2,1)S(1)} %all_to_all.20.packed_ref), custom_call_target="tpu_custom_call" | custom-call | bytes 2490368 | tf_op jit(solution)/shard_map/pallas_call | solution.py:121
  (56 shorter events, 0.2 us)
Async XLA Ops:
  1.3 1.1 copy-start.15
  2.3 0.7 copy-start.20
  3.1 6.1 %copy-start.16 = (bf16[192,1024]{1,0:T(8,128)(2,1)S(1)}, bf16[192,1024]{1,0:T(8,128)(2,1)}, u32[]{:S(2)}) copy-start(bf16[192,1024]{1,0:T(8,128)(2,1)} %query_ref.1) | copy-start | bytes 1179652
  3.1 6.1 %copy-start.17 = (bf16[192,1024]{1,0:T(8,128)(2,1)S(1)}, bf16[192,1024]{1,0:T(8,128)(2,1)}, u32[]{:S(2)}) copy-start(bf16[192,1024]{1,0:T(8,128)(2,1)} %key_ref.1) | copy-start | bytes 1179652
  3.1 6.1 %copy-start.18 = (bf16[192,1024]{1,0:T(8,128)(2,1)S(1)}, bf16[192,1024]{1,0:T(8,128)(2,1)}, u32[]{:S(2)}) copy-start(bf16[192,1024]{1,0:T(8,128)(2,1)} %value_ref.1) | copy-start | bytes 1179652
  3.2 8.1 %copy-start.1 = (bf16[192,1536]{1,0:T(8,128)(2,1)}, bf16[192,1536]{1,0:T(8,128)(2,1)S(1)}, u32[]{:S(2)}) copy-start(bf16[192,1536]{1,0:T(8,128)(2,1)S(1)} %shard_map.105.refs_10_.refs_0_) | copy-start | bytes 1769476
  3.2 22.8 %collective-permute-start.1 = (bf16[192,1536]{1,0:T(8,128)(2,1)S(1)}, bf16[192,1536]{1,0:T(8,128)(2,1)S(1)}, u32[]{:S(2)}, u32[]{:S(2)}) collective-permute-start(bf16[192,1536]{1,0:T(8,128)(2,1)S(1)} %shard_map.105.refs_10_.refs_0_), channel_id=1, source_target_pairs={{0,14},{2,0},{4,2},{6,4},{8,6},{10,8},{12,10},{14,12},{1,15},{3,1}... | collective-permute-start | bytes 1769480 | tf_op jit(solution)/shard_map/ppermute | solution.py:468
  9.2 19.9 %collective-permute-start = (bf16[192,1536]{1,0:T(8,128)(2,1)S(1)}, bf16[192,1536]{1,0:T(8,128)(2,1)S(1)}, u32[]{:S(2)}, u32[]{:S(2)}) collective-permute-start(bf16[192,1536]{1,0:T(8,128)(2,1)S(1)} %shard_map.105.refs_10_.refs_0_), channel_id=1, source_target_pairs={{0,2},{2,4},{4,6},{6,8},{8,10},{10,12},{12,14},{14,0},{1,3},{3,5},... | collective-permute-start | bytes 1769480 | tf_op jit(solution)/shard_map/ppermute | solution.py:468
  9.2 0.8 copy-start.19
  11.3 42.2 %all-to-all-start = ((bf16[8,608,128]{2,1,0:T(8,128)(2,1)}), bf16[8,608,128]{2,1,0:T(8,128)(2,1)S(1)}, u32[]{:S(2)}, u32[]{:S(2)}) async-start(bf16[8,608,128]{2,1,0:T(8,128)(2,1)} %shard_map.102), calls=%async_computation | async-start | bytes 2490368 | tf_op jit(solution)/shard_map/all_to_all | solution.py:484
  26.0 4.2 %copy-start.5 = (bf16[192,1536]{1,0:T(8,128)(2,1)}, bf16[192,1536]{1,0:T(8,128)(2,1)S(1)}, u32[]{:S(2)}) copy-start(bf16[192,1536]{1,0:T(8,128)(2,1)S(1)} %collective-permute-done.1.right_ref.refs_1_) | copy-start | bytes 1769476
  29.1 1.3 copy-start.7
  30.3 31.7 %collective-permute-start.2 = (bf16[96,1536]{1,0:T(8,128)(2,1)}, bf16[96,1536]{1,0:T(8,128)(2,1)S(1)}, u32[]{:S(2)}, u32[]{:S(2)}) collective-permute-start(bf16[96,1536]{1,0:T(8,128)(2,1)} %get-tuple-element.27), channel_id=1, source_target_pairs={{0,2},{2,4},{4,6},{6,8},{8,10},{10,12},{12,14},{14,0},{1,3},{3,5},... | collective-permute-start | bytes 884744 | tf_op jit(solution)/shard_map/ppermute | solution.py:468
  30.3 31.8 %collective-permute-start.4 = (bf16[96,1536]{1,0:T(8,128)(2,1)}, bf16[96,1536]{1,0:T(8,128)(2,1)S(1)}, u32[]{:S(2)}, u32[]{:S(2)}) collective-permute-start(bf16[96,1536]{1,0:T(8,128)(2,1)} %get-tuple-element.28), channel_id=1, source_target_pairs={{0,14},{2,0},{4,2},{6,4},{8,6},{10,8},{12,10},{14,12},{1,15},{3,1}... | collective-permute-start | bytes 884744 | tf_op jit(solution)/shard_map/ppermute | solution.py:468
  33.6 32.5 %collective-permute-start.10 = (bf16[96,1536]{1,0:T(8,128)(2,1)}, bf16[96,1536]{1,0:T(8,128)(2,1)}, u32[]{:S(2)}, u32[]{:S(2)}) collective-permute-start(bf16[96,1536]{1,0:T(8,128)(2,1)} %get-tuple-element.33), channel_id=1, source_target_pairs={{0,2},{2,4},{4,6},{6,8},{8,10},{10,12},{12,14},{14,0},{1,3},{3,5},... | collective-permute-start | bytes 884744 | tf_op jit(solution)/shard_map/ppermute | solution.py:468
  33.6 32.5 %collective-permute-start.11 = (bf16[96,1536]{1,0:T(8,128)(2,1)}, bf16[96,1536]{1,0:T(8,128)(2,1)}, u32[]{:S(2)}, u32[]{:S(2)}) collective-permute-start(bf16[96,1536]{1,0:T(8,128)(2,1)} %get-tuple-element.34), channel_id=1, source_target_pairs={{0,14},{2,0},{4,2},{6,4},{8,6},{10,8},{12,10},{14,12},{1,15},{3,1}... | collective-permute-start | bytes 884744 | tf_op jit(solution)/shard_map/ppermute | solution.py:468
  53.5 48.5 %copy-start = (bf16[8,608,128]{2,1,0:T(8,128)(2,1)}, bf16[8,608,128]{2,1,0:T(8,128)(2,1)S(1)}, u32[]{:S(2)}) copy-start(bf16[8,608,128]{2,1,0:T(8,128)(2,1)S(1)} %all-to-all-done.packed_ref._.refs_0_) | copy-start | bytes 3735556
  54.5 23.8 %all-to-all-start.1 = ((bf16[16,192,128]{2,1,0:T(8,128)(2,1)}), bf16[16,192,128]{2,1,0:T(8,128)(2,1)S(1)}, u32[]{:S(2)}, u32[]{:S(2)}) async-start(bf16[16,192,128]{2,1,0:T(8,128)(2,1)} %shard_map.103._), calls=%async_computation.1 | async-start | bytes 1572864 | tf_op jit(solution)/shard_map/all_to_all | solution.py:488
  62.1 13.3 %copy-start.11 = (bf16[96,1536]{1,0:T(8,128)(2,1)}, bf16[96,1536]{1,0:T(8,128)(2,1)S(1)}, u32[]{:S(2)}) copy-start(bf16[96,1536]{1,0:T(8,128)(2,1)S(1)} %shard_map.107.refs_2_) | copy-start | bytes 884740
  62.1 13.4 %collective-permute-start.3 = (bf16[96,1536]{1,0:T(8,128)(2,1)S(1)}, bf16[96,1536]{1,0:T(8,128)(2,1)S(1)}, u32[]{:S(2)}, u32[]{:S(2)}) collective-permute-start(bf16[96,1536]{1,0:T(8,128)(2,1)S(1)} %shard_map.107.refs_2_), channel_id=1, source_target_pairs={{0,2},{2,4},{4,6},{6,8},{8,10},{10,12},{12,14},{14,0},{1,3},{3,5},... | collective-permute-start | bytes 884744 | tf_op jit(solution)/shard_map/ppermute | solution.py:468
  62.2 13.2 %copy-start.9 = (bf16[96,1536]{1,0:T(8,128)(2,1)}, bf16[96,1536]{1,0:T(8,128)(2,1)S(1)}, u32[]{:S(2)}) copy-start(bf16[96,1536]{1,0:T(8,128)(2,1)S(1)} %collective-permute-done.4.refs_5_) | copy-start | bytes 884740
  62.2 13.3 %collective-permute-start.5 = (bf16[96,1536]{1,0:T(8,128)(2,1)S(1)}, bf16[96,1536]{1,0:T(8,128)(2,1)}, u32[]{:S(2)}, u32[]{:S(2)}) collective-permute-start(bf16[96,1536]{1,0:T(8,128)(2,1)S(1)} %collective-permute-done.4.refs_5_), channel_id=1, source_target_pairs={{0,14},{2,0},{4,2},{6,4},{8,6},{10,8},{12,10},{14,12},{1,15},{3,1}... | collective-permute-start | bytes 884744 | tf_op jit(solution)/shard_map/ppermute | solution.py:468
  66.0 11.6 %collective-permute-start.12 = (bf16[96,1536]{1,0:T(8,128)(2,1)}, bf16[96,1536]{1,0:T(8,128)(2,1)S(1)}, u32[]{:S(2)}, u32[]{:S(2)}) collective-permute-start(bf16[96,1536]{1,0:T(8,128)(2,1)} %collective-permute-done.10.refs_3_), channel_id=1, source_target_pairs={{0,2},{2,4},{4,6},{6,8},{8,10},{10,12},{12,14},{14,0},{1,3},{3,5},... | collective-permute-start | bytes 884744 | tf_op jit(solution)/shard_map/ppermute | solution.py:468
  66.1 13.5 %collective-permute-start.13 = (bf16[96,1536]{1,0:T(8,128)(2,1)}, bf16[96,1536]{1,0:T(8,128)(2,1)}, u32[]{:S(2)}, u32[]{:S(2)}) collective-permute-start(bf16[96,1536]{1,0:T(8,128)(2,1)} %collective-permute-done.11.refs_4_), channel_id=1, source_target_pairs={{0,14},{2,0},{4,2},{6,4},{8,6},{10,8},{12,10},{14,12},{1,15},{3,1}... | collective-permute-start | bytes 884744 | tf_op jit(solution)/shard_map/ppermute | solution.py:468
  75.4 11.1 %collective-permute-start.9 = (bf16[128,1536]{1,0:T(8,128)(2,1)}, bf16[128,1536]{1,0:T(8,128)(2,1)}, u32[]{:S(2)}, u32[]{:S(2)}) collective-permute-start(bf16[128,1536]{1,0:T(8,128)(2,1)} %get-tuple-element.32.own_t_ref), channel_id=1, source_target_pairs={{0,1},{1,0},{2,3},{3,2},{4,5},{5,4},{6,7},{7,6},{8,9},{9,8},{10,11... | collective-permute-start | bytes 1179656 | tf_op jit(solution)/shard_map/ppermute | solution.py:492
  75.5 9.6 %collective-permute-start.7 = (bf16[96,1536]{1,0:T(8,128)(2,1)}, bf16[96,1536]{1,0:T(8,128)(2,1)S(1)}, u32[]{:S(2)}, u32[]{:S(2)}) collective-permute-start(bf16[96,1536]{1,0:T(8,128)(2,1)} %collective-permute-done.5.refs_9_), channel_id=1, source_target_pairs={{0,14},{2,0},{4,2},{6,4},{8,6},{10,8},{12,10},{14,12},{1,15},{3,1}... | collective-permute-start | bytes 884744 | tf_op jit(solution)/shard_map/ppermute | solution.py:468
  76.6 9.9 %collective-permute-start.6 = (bf16[96,1536]{1,0:T(8,128)(2,1)S(1)}, bf16[96,1536]{1,0:T(8,128)(2,1)}, u32[]{:S(2)}, u32[]{:S(2)}) collective-permute-start(bf16[96,1536]{1,0:T(8,128)(2,1)S(1)} %collective-permute-done.3.refs_6_.refs_12_), channel_id=1, source_target_pairs={{0,2},{2,4},{4,6},{6,8},{8,10},{10,12},{12,14},{14,0},{1,3},{3,5},... | collective-permute-start | bytes 884744 | tf_op jit(solution)/shard_map/ppermute | solution.py:468
  77.6 0.7 copy-start.22
  78.3 2.4 %copy-start.6 = (bf16[192,1536]{1,0:T(8,128)(2,1)S(1)}, bf16[192,1536]{1,0:T(8,128)(2,1)}, u32[]{:S(2)}) copy-start(bf16[192,1536]{1,0:T(8,128)(2,1)} %copy-done.5) | copy-start | bytes 1769476
  78.3 2.4 %copy-start.8 = (bf16[192,1536]{1,0:T(8,128)(2,1)S(1)}, bf16[192,1536]{1,0:T(8,128)(2,1)}, u32[]{:S(2)}) copy-start(bf16[192,1536]{1,0:T(8,128)(2,1)} %copy-done.7) | copy-start | bytes 1769476
  78.3 2.4 %copy-start.10 = (bf16[96,1536]{1,0:T(8,128)(2,1)S(1)}, bf16[96,1536]{1,0:T(8,128)(2,1)}, u32[]{:S(2)}) copy-start(bf16[96,1536]{1,0:T(8,128)(2,1)} %copy-done.9) | copy-start | bytes 884740
  78.3 2.4 %copy-start.12 = (bf16[96,1536]{1,0:T(8,128)(2,1)S(1)}, bf16[96,1536]{1,0:T(8,128)(2,1)}, u32[]{:S(2)}) copy-start(bf16[96,1536]{1,0:T(8,128)(2,1)} %copy-done.11) | copy-start | bytes 884740
  78.3 2.4 %collective-permute-start.8 = (bf16[3072,128]{1,0:T(8,128)(2,1)S(1)}, bf16[3072,128]{1,0:T(8,128)(2,1)S(1)}, u32[]{:S(2)}, u32[]{:S(2)}) collective-permute-start(bf16[3072,128]{1,0:T(8,128)(2,1)S(1)} %bitcast.2), channel_id=1, source_target_pairs={{0,1},{1,0},{2,3},{3,2},{4,5},{5,4},{6,7},{7,6},{8,9},{9,8},{10,11... | collective-permute-start | bytes 2359304 | tf_op jit(solution)/shard_map/ppermute | solution.py:489
  78.4 1.1 copy-start.23
  83.4 0.7 copy-start.21
  84.1 5.8 %copy-start.3 = (f32[1152,128]{1,0:T(8,128)}, f32[1152,128]{1,0:T(8,128)S(1)}, u32[]{:S(2)}) copy-start(f32[1152,128]{1,0:T(8,128)S(1)} %get-tuple-element.35._.refs_4_) | copy-start | bytes 1769476
  86.5 3.6 %copy-start.2 = (bf16[192,1536]{1,0:T(8,128)(2,1)S(1)}, bf16[192,1536]{1,0:T(8,128)(2,1)}, u32[]{:S(2)}) copy-start(bf16[192,1536]{1,0:T(8,128)(2,1)} %copy-done.1) | copy-start | bytes 1769476
  90.0 1.8 %collective-permute-start.15 = (bf16[1536,128]{1,0:T(8,128)(2,1)S(1)}, bf16[1536,128]{1,0:T(8,128)(2,1)S(1)}, u32[]{:S(2)}, u32[]{:S(2)}) collective-permute-start(bf16[1536,128]{1,0:T(8,128)(2,1)S(1)} %get-tuple-element.39), channel_id=1, source_target_pairs={{0,1},{1,0},{2,3},{3,2},{4,5},{5,4},{6,7},{7,6},{8,9},{9,8},{10,11... | collective-permute-start | bytes 1179656 | tf_op jit(solution)/shard_map/ppermute | solution.py:501
  91.5 1.1 copy-start.13
  91.8 10.2 %copy-start.4 = (f32[1152,128]{1,0:T(8,128)S(1)}, f32[1152,128]{1,0:T(8,128)}, u32[]{:S(2)}) copy-start(f32[1152,128]{1,0:T(8,128)} %copy-done.3) | copy-start | bytes 1769476
  92.7 21.0 %all-to-all-start.2 = ((bf16[16,192,128]{2,1,0:T(8,128)(2,1)}), bf16[16,192,128]{2,1,0:T(8,128)(2,1)S(1)}, u32[]{:S(2)}, u32[]{:S(2)}) async-start(bf16[16,192,128]{2,1,0:T(8,128)(2,1)} %bitcast.1.refs_6_), calls=%async_computation.2 | async-start | bytes 1572864 | tf_op jit(solution)/shard_map/all_to_all | solution.py:505
  100.2 1.8 %collective-permute-start.16 = (bf16[1152,128]{1,0:T(8,128)(2,1)}, bf16[1152,128]{1,0:T(8,128)(2,1)S(1)}, u32[]{:S(2)}, u32[]{:S(2)}) collective-permute-start(bf16[1152,128]{1,0:T(8,128)(2,1)} %copy-done.21), channel_id=1, source_target_pairs={{0,1},{1,0},{2,3},{3,2},{4,5},{5,4},{6,7},{7,6},{8,9},{9,8},{10,11... | collective-permute-start | bytes 884744 | tf_op jit(solution)/shard_map/ppermute | solution.py:499
  100.2 7.8 %collective-permute-start.14 = (bf16[384,128]{1,0:T(8,128)(2,1)S(1)}, bf16[384,128]{1,0:T(8,128)(2,1)S(1)}, u32[]{:S(2)}, u32[]{:S(2)}) collective-permute-start(bf16[384,128]{1,0:T(8,128)(2,1)S(1)} %get-tuple-element.38), channel_id=1, source_target_pairs={{0,1},{1,0},{2,3},{3,2},{4,5},{5,4},{6,7},{7,6},{8,9},{9,8},{10,11... | collective-permute-start | bytes 294920 | tf_op jit(solution)/shard_map/ppermute | solution.py:503
  102.0 6.0 %copy-start.14 = (f32[384,128]{1,0:T(8,128)S(1)}, f32[384,128]{1,0:T(8,128)}, u32[]{:S(2)}) copy-start(f32[384,128]{1,0:T(8,128)} %copy-done.13) | copy-start | bytes 589828
